TPU v7x, 32 devices: a whole 2x2x4 slice. The times are simulated.
32 devices in a mesh: dp: 8 (over z, x), row: 2 (over y), col: 2 (over core).
Axes of the slice: x: 2, y: 2, z: 4, core: 2. Of those that a mesh axis runs over, the one named last changes fastest.
Arguments:
- residual: bfloat16 [2, 16384, 1024], P(None, ('dp', 'row'), 'col'), may hold values from -6 to 6
- attend_norm_gain: float32 [1024], replicated, may hold values from 0.25 to 1.75
- attend_norm_bias: float32 [1024], replicated, may hold values from -3 to 3
- expand_norm_gain: float32 [1024], replicated, may hold values from 0.25 to 1.75
- expand_norm_bias: float32 [1024], replicated, may hold values from -3 to 3
- attend_weight: bfloat16 [1024, 16, 192], P('col', 'row', 'dp'), may hold values from -0.1875 to 0.1875
- attend_bias: float32 [16, 192], replicated, may hold values from -3 to 3
- output_weight: bfloat16 [16, 64, 1024], P('row', 'dp', 'col'), may hold values from -2 to 2
- output_bias: float32 [1024], replicated, may hold values from -4 to 4
- expand_weight: bfloat16 [1024, 4096], P('col', ('dp', 'row')), may hold values from -0.1875 to 0.1875
- expand_bias: float32 [4096], replicated, may hold values from -4 to 4
- shrink_weight: bfloat16 [4096, 1024], P(('dp', 'row'), 'col'), may hold values from -0.09375 to 0.09375
- shrink_bias: float32 [1024], replicated, may hold values from -4 to 4
- cotangent: bfloat16 [2, 16384, 1024], P(None, ('dp', 'row'), 'col'), may hold values from -6 to 6
Outputs:
- layer_output: bfloat16 [2, 16384, 1024], P(None, ('dp', 'row'), 'col')
- residual_grad: float32 [2, 16384, 1024], P(None, ('dp', 'row'), 'col')
- attend_norm_gain_grad: float32 [1024], replicated
- attend_norm_bias_grad: float32 [1024], replicated
- expand_norm_gain_grad: float32 [1024], replicated
- expand_norm_bias_grad: float32 [1024], replicated
- attend_weight_grad: float32 [1024, 16, 192], P('col', 'row', 'dp')
- attend_bias_grad: float32 [16, 192], replicated
- output_weight_grad: float32 [16, 64, 1024], P('row', 'dp', 'col')
- output_bias_grad: float32 [1024], replicated
- expand_weight_grad: float32 [1024, 4096], P('col', ('dp', 'row'))
- expand_bias_grad: float32 [4096], replicated
- shrink_weight_grad: float32 [4096, 1024], P(('dp', 'row'), 'col')
- shrink_bias_grad: float32 [1024], replicated
All inputs are finite; a program needn't handle non-finite values.
Results may differ from a plain program's by a relative error of at most 0.013.
Values may be sent and summed in bfloat16 or wider, within the bound.
A program may use at most 256 MiB of HBM per device.

v0:
```python
from functools import partial

import jax
import jax.numpy as jnp
from jax import lax
from jax.sharding import PartitionSpec as P

D = 1024
HS = 64
ROT = 16


EPSILON = 1e-05
MASKED = -1e30
ROWS_CONTRACT = (((0,), (0,)), ((), ()))
COLS_CONTRACT = (((1,), (1,)), ((), ()))


def rotary_tables(length):
    places = jnp.arange(length, dtype=jnp.float32)
    powers = jnp.arange(ROT // 2, dtype=jnp.float32) * (2.0 / ROT)
    inverse = jnp.power(10000.0, -powers)
    angles = places[:, None] * inverse[None, :]
    angles = jnp.concatenate([angles, angles], axis=1)
    return (jnp.cos(angles)[:, None, :], jnp.sin(angles)[:, None, :])


def rotate(features, cosine_table, sine_table):
    halfway = ROT // 2
    turned = jnp.concatenate([-features[..., halfway:ROT], features[..., :halfway]], axis=-1)
    spun_part = features[..., :ROT] * cosine_table + turned * sine_table
    return jnp.concatenate([spun_part, features[..., ROT:]], axis=-1)


def unrotate(features, cosine_table, sine_table):
    halfway = ROT // 2
    scaled = features[..., :ROT] * sine_table
    turned = jnp.concatenate([scaled[..., halfway:], -scaled[..., :halfway]], axis=-1)
    spun_part = features[..., :ROT] * cosine_table + turned
    return jnp.concatenate([spun_part, features[..., ROT:]], axis=-1)


def causal_scores(query_block, keys_all, begin_row, block_rows):
    length = keys_all.shape[0]
    scores = jnp.einsum(
        "qhe,khe->hqk", query_block, keys_all, preferred_element_type=jnp.float32
    ) * HS ** (-0.5)
    allowed = jnp.arange(length)[None, :] <= (begin_row + jnp.arange(block_rows))[:, None]
    return jnp.where(allowed[None], scores, MASKED)


def attend_forward(queries, keys_all, values, block_rows):
    length = keys_all.shape[0]

    def one_block(begin_row):
        query_block = lax.dynamic_slice_in_dim(queries, begin_row, block_rows, 0)
        scores = causal_scores(query_block, keys_all, begin_row, block_rows)
        highest = jnp.max(scores, axis=-1, keepdims=True)
        raised = jnp.exp(scores - highest)
        totals = jnp.sum(raised, axis=-1, keepdims=True)
        weights = (raised / totals).astype(jnp.bfloat16)
        block_out = jnp.einsum("hqk,khe->qhe", weights, values, preferred_element_type=jnp.float32)
        return (block_out.astype(jnp.bfloat16), (highest + jnp.log(totals))[..., 0])

    starts = jnp.arange(length // block_rows) * block_rows
    outputs, logsum = lax.map(one_block, starts)
    return (outputs.reshape(length, queries.shape[1], HS), logsum)


def attend_backward(queries, keys_all, values, logsum, heads_grad, block_rows):
    length = keys_all.shape[0]
    factor = HS ** (-0.5)

    def one_block(running, inputs_now):
        begin_row, block_sum = inputs_now
        key_grad, value_grad = running
        query_block = lax.dynamic_slice_in_dim(queries, begin_row, block_rows, 0)
        grad_block = lax.dynamic_slice_in_dim(heads_grad, begin_row, block_rows, 0)
        scores = causal_scores(query_block, keys_all, begin_row, block_rows)
        probability = jnp.exp(scores - block_sum[..., None])
        value_grad = value_grad + jnp.einsum(
            "hqk,qhe->khe",
            probability.astype(jnp.bfloat16),
            grad_block,
            preferred_element_type=jnp.float32,
        )
        prob_grad = jnp.einsum(
            "qhe,khe->hqk", grad_block, values, preferred_element_type=jnp.float32
        )
        inner_sum = jnp.sum(probability * prob_grad, axis=-1, keepdims=True)
        score_grad = (probability * (prob_grad - inner_sum)).astype(jnp.bfloat16)
        query_grad = (
            jnp.einsum("hqk,khe->qhe", score_grad, keys_all, preferred_element_type=jnp.float32)
            * factor
        )
        key_grad = (
            key_grad
            + jnp.einsum(
                "hqk,qhe->khe", score_grad, query_block, preferred_element_type=jnp.float32
            )
            * factor
        )
        return ((key_grad, value_grad), query_grad)

    starts = jnp.arange(length // block_rows) * block_rows
    empty = jnp.zeros(keys_all.shape, jnp.float32)
    (key_grad, value_grad), query_grad = lax.scan(one_block, (empty, empty), (starts, logsum))
    return (query_grad.reshape(keys_all.shape), key_grad, value_grad)


def gather_tiles(attend_weight, output_weight, expand_weight, shrink_weight):
    return (
        lax.all_gather(attend_weight, "dp", axis=2, tiled=True),
        lax.all_gather(output_weight, "dp", axis=1, tiled=True),
        lax.all_gather(expand_weight, "dp", axis=1, tiled=True),
        lax.all_gather(shrink_weight, "dp", axis=0, tiled=True),
    )


def reduce_tiles(first_tile, second_tile, third_tile, fourth_tile):
    return (
        lax.psum_scatter(
            first_tile.astype(jnp.bfloat16), "dp", scatter_dimension=2, tiled=True
        ).astype(jnp.float32),
        lax.psum_scatter(
            second_tile.astype(jnp.bfloat16), "dp", scatter_dimension=1, tiled=True
        ).astype(jnp.float32),
        lax.psum_scatter(
            third_tile.astype(jnp.bfloat16), "dp", scatter_dimension=1, tiled=True
        ).astype(jnp.float32),
        lax.psum_scatter(
            fourth_tile.astype(jnp.bfloat16), "dp", scatter_dimension=0, tiled=True
        ).astype(jnp.float32),
    )


def body(
    residual,
    attend_norm_gain,
    attend_norm_bias,
    expand_norm_gain,
    expand_norm_bias,
    attend_weight,
    attend_bias,
    output_weight,
    output_bias,
    expand_weight,
    expand_bias,
    shrink_weight,
    shrink_bias,
    cotangent,
):
    row_count = lax.axis_size("row")
    col_count = lax.axis_size("col")
    dp_count = lax.axis_size("dp")
    row_index = lax.axis_index("row")
    col_index = lax.axis_index("col")
    local_rows = residual.shape[1]
    length = local_rows * row_count
    width_part = residual.shape[2]
    heads_here = attend_bias.shape[0] // (row_count * col_count)
    ffn_piece = expand_weight.shape[1]
    pieces_per_col = dp_count // col_count
    block_rows = min(512, length)
    cosine_table, sine_table = rotary_tables(length)
    column_begin = col_index * width_part
    head_begin = (row_index * col_count + col_index) * heads_here

    def column_slice(vector):
        return lax.dynamic_slice_in_dim(vector, column_begin, width_part, 0)

    gain_first = column_slice(attend_norm_gain)
    bias_first = column_slice(attend_norm_bias)
    gain_second = column_slice(expand_norm_gain)
    bias_second = column_slice(expand_norm_bias)
    residual_bias = column_slice(output_bias) + column_slice(shrink_bias)
    triple_bias_here = lax.dynamic_slice_in_dim(attend_bias, head_begin, heads_here, 0).reshape(-1)
    bias_grid = expand_bias.reshape(dp_count, row_count, ffn_piece)
    bias_rows = lax.dynamic_slice_in_dim(bias_grid, row_index, 1, 1)
    expand_bias_here = lax.dynamic_slice_in_dim(
        bias_rows, col_index * pieces_per_col, pieces_per_col, 0
    ).reshape(-1)

    def micro_step(running, micro_pair):
        tile_sums, vector_sums = running
        tokens_now, grad_now = micro_pair
        gathered = gather_tiles(attend_weight, output_weight, expand_weight, shrink_weight)
        triple_tile, output_tile, expand_tile, shrink_tile = gathered
        triple_flat = triple_tile.reshape(width_part, -1)
        output_flat = output_tile.reshape(-1, width_part)
        tokens_float = tokens_now.astype(jnp.float32)
        sum_first, sum_second = lax.psum(
            (jnp.sum(tokens_float, axis=1), jnp.sum(tokens_float * tokens_float, axis=1)), "col"
        )
        center = sum_first / D
        spread = sum_second / D - center * center
        inv_std = lax.rsqrt(spread + EPSILON)[:, None]
        normed = (tokens_float - center[:, None]) * inv_std
        first_in = (normed * gain_first + bias_first).astype(jnp.bfloat16)
        second_in = (normed * gain_second + bias_second).astype(jnp.bfloat16)
        first_full, second_full, grad_full = (
            lax.all_gather(first_in, "row", axis=0, tiled=True),
            lax.all_gather(second_in, "row", axis=0, tiled=True),
            lax.all_gather(grad_now, "row", axis=0, tiled=True),
        )
        triple_part = jnp.dot(first_full, triple_flat, preferred_element_type=jnp.float32)
        expand_part = jnp.dot(second_full, expand_tile, preferred_element_type=jnp.float32)
        triple_sum, expand_sum = (
            lax.psum_scatter(triple_part, "col", scatter_dimension=1, tiled=True),
            lax.psum_scatter(expand_part, "col", scatter_dimension=1, tiled=True),
        )
        triple = (triple_sum + triple_bias_here).reshape(length, heads_here, 3 * HS)
        queries = rotate(triple[..., :HS], cosine_table, sine_table).astype(jnp.bfloat16)
        keys_all = rotate(triple[..., HS : 2 * HS], cosine_table, sine_table).astype(jnp.bfloat16)
        values = triple[..., 2 * HS :].astype(jnp.bfloat16)
        expanded = expand_sum + expand_bias_here
        activated = jax.nn.gelu(expanded, approximate=False).astype(jnp.bfloat16)
        attended, logsum = attend_forward(queries, keys_all, values, block_rows)
        attended_flat = attended.reshape(length, -1)
        attended_full, activated_full = (
            lax.all_gather(attended_flat, "col", axis=1, tiled=True),
            lax.all_gather(activated, "col", axis=1, tiled=True),
        )
        mixed_sum = lax.psum_scatter(
            jnp.dot(attended_full, output_flat, preferred_element_type=jnp.float32)
            + jnp.dot(activated_full, shrink_tile, preferred_element_type=jnp.float32),
            "row",
            scatter_dimension=0,
            tiled=True,
        )
        output_now = (tokens_float + mixed_sum + residual_bias).astype(jnp.bfloat16)
        heads_part = lax.dot_general(
            grad_full, output_flat, COLS_CONTRACT, preferred_element_type=jnp.float32
        )
        hidden_part = lax.dot_general(
            grad_full, shrink_tile, COLS_CONTRACT, preferred_element_type=jnp.float32
        )
        heads_sum, hidden_sum = (
            lax.psum_scatter(heads_part, "col", scatter_dimension=1, tiled=True),
            lax.psum_scatter(hidden_part, "col", scatter_dimension=1, tiled=True),
        )
        output_weight_grad = lax.dot_general(
            attended_full, grad_full, ROWS_CONTRACT, preferred_element_type=jnp.float32
        )
        shrink_weight_grad = lax.dot_general(
            activated_full, grad_full, ROWS_CONTRACT, preferred_element_type=jnp.float32
        )
        heads_grad = heads_sum.astype(jnp.bfloat16).reshape(length, heads_here, HS)
        query_grad, key_grad, value_grad = attend_backward(
            queries, keys_all, values, logsum, heads_grad, block_rows
        )
        triple_grad = jnp.concatenate(
            [
                unrotate(query_grad, cosine_table, sine_table),
                unrotate(key_grad, cosine_table, sine_table),
                value_grad,
            ],
            axis=-1,
        )
        triple_grad = triple_grad.astype(jnp.bfloat16).reshape(length, -1)
        _, gelu_pull = jax.vjp(partial(jax.nn.gelu, approximate=False), expanded)
        expand_grad = gelu_pull(hidden_sum)[0].astype(jnp.bfloat16)
        triple_grad_full, expand_grad_full = (
            lax.all_gather(triple_grad, "col", axis=1, tiled=True),
            lax.all_gather(expand_grad, "col", axis=1, tiled=True),
        )
        triple_weight_grad = lax.dot_general(
            first_full, triple_grad_full, ROWS_CONTRACT, preferred_element_type=jnp.float32
        )
        expand_weight_grad = lax.dot_general(
            second_full, expand_grad_full, ROWS_CONTRACT, preferred_element_type=jnp.float32
        )
        first_part = lax.dot_general(
            triple_grad_full, triple_flat, COLS_CONTRACT, preferred_element_type=jnp.float32
        )
        second_part = lax.dot_general(
            expand_grad_full, expand_tile, COLS_CONTRACT, preferred_element_type=jnp.float32
        )
        first_grad, second_grad = (
            lax.psum_scatter(
                first_part.astype(jnp.bfloat16), "row", scatter_dimension=0, tiled=True
            ).astype(jnp.float32),
            lax.psum_scatter(
                second_part.astype(jnp.bfloat16), "row", scatter_dimension=0, tiled=True
            ).astype(jnp.float32),
        )
        normed_grad = first_grad * gain_first + second_grad * gain_second
        total_first, total_second = lax.psum(
            (jnp.sum(normed_grad, axis=1), jnp.sum(normed_grad * normed, axis=1)), "col"
        )
        input_grad = grad_now.astype(jnp.float32) + inv_std * (
            normed_grad - total_first[:, None] / D - normed * total_second[:, None] / D
        )
        vector_terms = (
            jnp.sum(first_grad * normed, axis=0),
            jnp.sum(first_grad, axis=0),
            jnp.sum(second_grad * normed, axis=0),
            jnp.sum(second_grad, axis=0),
            jnp.sum(grad_now.astype(jnp.float32), axis=0),
            jnp.sum(triple_grad.astype(jnp.float32), axis=0),
            jnp.sum(expand_grad.astype(jnp.float32), axis=0),
        )
        vector_sums = jax.tree.map(jnp.add, vector_sums, vector_terms)
        tile_terms = (
            triple_weight_grad.reshape(triple_tile.shape),
            output_weight_grad.reshape(output_tile.shape),
            expand_weight_grad,
            shrink_weight_grad,
        )
        reduced = reduce_tiles(tile_terms[0], tile_terms[1], tile_terms[2], tile_terms[3])
        tile_sums = jax.tree.map(jnp.add, tile_sums, reduced)
        return ((tile_sums, vector_sums), (output_now, input_grad))

    tile_start = (
        jnp.zeros(attend_weight.shape, jnp.float32),
        jnp.zeros(output_weight.shape, jnp.float32),
        jnp.zeros(expand_weight.shape, jnp.float32),
        jnp.zeros(shrink_weight.shape, jnp.float32),
    )
    column_zero = jnp.zeros((width_part,), jnp.float32)
    vector_start = (
        column_zero,
        column_zero,
        column_zero,
        column_zero,
        column_zero,
        jnp.zeros((heads_here * 3 * HS,), jnp.float32),
        jnp.zeros((pieces_per_col * ffn_piece,), jnp.float32),
    )
    (tile_sums, vector_sums), (outputs, input_grads) = lax.scan(
        micro_step, (tile_start, vector_start), (residual, cotangent)
    )

    def place_columns(vector):
        return lax.dynamic_update_slice_in_dim(
            jnp.zeros((width_part * col_count,), jnp.float32), vector, column_begin, 0
        )

    triple_bias_full = lax.dynamic_update_slice_in_dim(
        jnp.zeros(attend_bias.shape, jnp.float32),
        vector_sums[5].reshape(heads_here, 3 * HS),
        head_begin,
        0,
    )
    expand_bias_full = lax.dynamic_update_slice(
        jnp.zeros((dp_count, row_count, ffn_piece), jnp.float32),
        vector_sums[6].reshape(pieces_per_col, 1, ffn_piece),
        (col_index * pieces_per_col, row_index, jnp.zeros((), jnp.int32)),
    ).reshape(-1)
    summed = lax.psum(
        (
            place_columns(vector_sums[0]),
            place_columns(vector_sums[1]),
            place_columns(vector_sums[2]),
            place_columns(vector_sums[3]),
            place_columns(vector_sums[4]),
            triple_bias_full,
            expand_bias_full,
        ),
        ("dp", "row", "col"),
    )
    return (
        outputs,
        input_grads,
        summed[0],
        summed[1],
        summed[2],
        summed[3],
        tile_sums[0],
        summed[5],
        tile_sums[1],
        summed[4],
        tile_sums[2],
        summed[6],
        tile_sums[3],
        summed[4],
    )


def solution(mesh):
    in_specs = (
        P(None, ("dp", "row"), "col"),
        P(),
        P(),
        P(),
        P(),
        P("col", "row", "dp"),
        P(),
        P("row", "dp", "col"),
        P(),
        P("col", ("dp", "row")),
        P(),
        P(("dp", "row"), "col"),
        P(),
        P(None, ("dp", "row"), "col"),
    )
    out_specs = (
        P(None, ("dp", "row"), "col"),
        P(None, ("dp", "row"), "col"),
        P(),
        P(),
        P(),
        P(),
        P("col", "row", "dp"),
        P(),
        P("row", "dp", "col"),
        P(),
        P("col", ("dp", "row")),
        P(),
        P(("dp", "row"), "col"),
        P(),
    )
    return jax.shard_map(body, mesh=mesh, in_specs=in_specs, out_specs=out_specs, check_vma=False)
```

profile of v0, /device:TPU:0, one launch (start us, length us, event | category | flops | bytes accessed | tf_op | source)
XLA Modules:
  0.0 2400.8 jit_solution(13358376787633428177)
XLA Ops:
  13.5 2333.5 %while.69 = (s32[]{:T(128)}, f32[512,8,24]{0,2,1:T(8,128)}, f32[8,8,512]{2,1,0:T(8,128)}, f32[512,256]{1,0:T(8,128)}, f32[256,512]{1,0:T(8,128)}, /*index=5*/f32...) while((s32[]{:T(128)}, f32[512,8,24]{0,2,1:T(8,128)}, ...), condition=%wide.wide.region_34.35_spmd.clone, body=%wide.wide.region_0.34_spmd.clone.sunk | while | flops 42745069568 | bytes 1098400896 | solution.py:330
  26.2 33.1 %all_gather.65 = bf16[8,64,512]{2,1,0:T(8,128)(2,1)S(1)} all-gather(bf16[8,8,512]{2,1,0:T(8,128)(2,1)S(1)} %copy-done.23), channel_id=1, replica_groups=mesh['dp'=8,'row'=2,'col'=2] {'dp'}, dimensions={1}, use_global_device_ids=true | all-gather | bytes 589824 | tf_op jit(solution)/shard_map/while/body/eval_jaxpr/all_gather | solution.py:114
  64.6 23.2 all-gather.16.cloned.1.call-done
  87.8 46.4 %all-gather.18.cloned.1.call-done = bf16[512,8,192]{0,2,1:T(8,128)(2,1)} async-done(((bf16[512,8,24]{0,2,1:T(8,128)(2,1)}), bf16[512,8,192]{0,2,1:T(8,128)(2,1)}) %all-gather.18.cloned.1.call-update) | async-done | bytes 1572880 | tf_op jit(solution)/shard_map/while/body/eval_jaxpr/all_gather | solution.py:113
  144.9 22.7 all-gather.26.cloned.1.call-done
  167.6 53.0 %all-gather.30.cloned.1.call-done = bf16[512,2048]{1,0:T(8,128)(2,1)} async-done(((bf16[512,256]{1,0:T(8,128)(2,1)}), bf16[512,2048]{1,0:T(8,128)(2,1)}) %all-gather.30.cloned.1.call-update) | async-done | bytes 2097168 | tf_op jit(solution)/shard_map/while/body/eval_jaxpr/all_gather | solution.py:115
  220.6 12.5 fusion.258
  233.9 36.5 %all-gather.28.cloned.1.call-done = bf16[2048,512]{1,0:T(8,128)(2,1)} async-done(((bf16[256,512]{1,0:T(8,128)(2,1)}), bf16[2048,512]{1,0:T(8,128)(2,1)}) %all-gather.28.cloned.1.call-update) | async-done | bytes 2097168 | tf_op jit(solution)/shard_map/while/body/eval_jaxpr/all_gather | solution.py:116
  286.3 22.0 reduce-scatter.22.cloned.1.call-done
  330.2 74.8 %while.70 = (s32[]{:T(128)}, bf16[4,512,4,64]{1,3,2,0:T(8,128)(2,1)}, f32[4,4,512]{2,1,0:T(4,128)S(1)}, s32[4]{0:T(128)S(1)}, bf16[2048,4,64]{0,2,1:T(8,128)(2,1...) while((s32[]{:T(128)}, ...), condition=%wide.region_9.9_spmd, body=%wide.region_6.8_spmd.sunk | while | flops 1125251584 | bytes 57217692 | solution.py:66
  405.0 289.6 %while.71 = (s32[]{:T(128)}, f32[2048,4,64]{0,2,1:T(8,128)}, f32[2048,4,64]{0,2,1:T(8,128)}, f32[4,512,4,64]{1,0,3,2:T(4,128)}, s32[4]{0:T(128)S(1)}, /*index=5*...) while((s32[]{:T(128)}, f32[2048,4,64]{0,2,1:T(8,128)}, ...), condition=%wide.region_13.13_spmd.clone, body=%wide.region_11.12_spmd.clone.sunk | while | flops 2751068672 | bytes 187232528 | solution.py:107
  418.6 12.6 multiply_reduce_fusion.2
  490.0 12.6 multiply_reduce_fusion.2
  536.8 12.5 fusion.279
  562.7 12.6 multiply_reduce_fusion.2
  609.4 12.5 fusion.279
  635.3 12.6 multiply_reduce_fusion.2
  708.7 23.9 convert_reduce_fusion.16
  817.4 27.0 %reduce-scatter.28.cloned.1.call-done = bf16[8,4096]{1,0:T(8,128)(2,1)} async-done(((bf16[64,4096]{1,0:T(8,128)(2,1)}), bf16[8,4096]{1,0:T(8,128)(2,1)}) %reduce-scatter.28.cloned.1.call-update) | async-done | bytes 65552 | tf_op jit(solution)/shard_map/while
  846.7 65.2 %reduce-scatter.26.cloned.1.call-done = bf16[24,4096]{1,0:T(8,128)(2,1)} async-done(((bf16[192,4096]{1,0:T(8,128)(2,1)}), bf16[24,4096]{1,0:T(8,128)(2,1)}) %reduce-scatter.26.cloned.1.call-update) | async-done | bytes 196624 | tf_op jit(solution)/shard_map/while
  913.8 31.0 %reduce-scatter.40.cloned.1.call-done = bf16[1024,512]{1,0:T(8,128)(2,1)} async-done(((bf16[2048,512]{1,0:T(8,128)(2,1)}), bf16[1024,512]{1,0:T(8,128)(2,1)}) %reduce-scatter.40.cloned.1.call-update) | async-done | bytes 1048592 | tf_op jit(solution)/shard_map/while/body/eval_jaxpr/reduce_scatter | solution.py:280
  944.9 34.1 %reduce-scatter.38.cloned.1.call-done = bf16[1024,512]{1,0:T(8,128)(2,1)} async-done(((bf16[2048,512]{1,0:T(8,128)(2,1)}), bf16[1024,512]{1,0:T(8,128)(2,1)}) %reduce-scatter.38.cloned.1.call-update) | async-done | bytes 1048592 | tf_op jit(solution)/shard_map/while/body/eval_jaxpr/reduce_scatter | solution.py:283
  989.6 61.0 %reduce-scatter.36.cloned.1.call-done = bf16[256,512]{1,0:T(8,128)(2,1)} async-done(((bf16[2048,512]{1,0:T(8,128)(2,1)}), bf16[256,512]{1,0:T(8,128)(2,1)}) %reduce-scatter.36.cloned.1.call-update) | async-done | bytes 262160 | tf_op jit(solution)/shard_map/while/body/eval_jaxpr/reduce_scatter | solution.py:131
  1052.4 69.3 %reduce-scatter.34.cloned.1.call-done = bf16[512,256]{1,0:T(8,128)(2,1)} async-done(((bf16[512,2048]{1,0:T(8,128)(2,1)}), bf16[512,256]{1,0:T(8,128)(2,1)}) %reduce-scatter.34.cloned.1.call-update) | async-done | bytes 262160 | tf_op jit(solution)/shard_map/while/body/eval_jaxpr/reduce_scatter | solution.py:128
  1127.2 50.2 %reduce-scatter.42.cloned.1.call-done = f32[1024,512]{1,0:T(8,128)} async-done(((f32[2048,512]{1,0:T(8,128)}), f32[1024,512]{1,0:T(8,128)}) %reduce-scatter.42.cloned.1.call-update) | async-done | bytes 2097168 | tf_op jit(solution)/shard_map/while/body/eval_jaxpr/reduce_scatter | solution.py:224
  1192.9 31.4 %all_gather.65 = bf16[8,64,512]{2,1,0:T(8,128)(2,1)S(1)} all-gather(bf16[8,8,512]{2,1,0:T(8,128)(2,1)S(1)} %copy-done.23), channel_id=1, replica_groups=mesh['dp'=8,'row'=2,'col'=2] {'dp'}, dimensions={1}, use_global_device_ids=true | all-gather | bytes 589824 | tf_op jit(solution)/shard_map/while/body/eval_jaxpr/all_gather | solution.py:114
  1229.6 22.3 all-gather.16.cloned.1.call-done
  1251.9 46.3 %all-gather.18.cloned.1.call-done = bf16[512,8,192]{0,2,1:T(8,128)(2,1)} async-done(((bf16[512,8,24]{0,2,1:T(8,128)(2,1)}), bf16[512,8,192]{0,2,1:T(8,128)(2,1)}) %all-gather.18.cloned.1.call-update) | async-done | bytes 1572880 | tf_op jit(solution)/shard_map/while/body/eval_jaxpr/all_gather | solution.py:113
  1308.9 22.8 all-gather.26.cloned.1.call-done
  1331.7 53.0 %all-gather.30.cloned.1.call-done = bf16[512,2048]{1,0:T(8,128)(2,1)} async-done(((bf16[512,256]{1,0:T(8,128)(2,1)}), bf16[512,2048]{1,0:T(8,128)(2,1)}) %all-gather.30.cloned.1.call-update) | async-done | bytes 2097168 | tf_op jit(solution)/shard_map/while/body/eval_jaxpr/all_gather | solution.py:115
  1384.7 12.5 fusion.258
  1397.8 36.6 %all-gather.28.cloned.1.call-done = bf16[2048,512]{1,0:T(8,128)(2,1)} async-done(((bf16[256,512]{1,0:T(8,128)(2,1)}), bf16[2048,512]{1,0:T(8,128)(2,1)}) %all-gather.28.cloned.1.call-update) | async-done | bytes 2097168 | tf_op jit(solution)/shard_map/while/body/eval_jaxpr/all_gather | solution.py:116
  1450.4 22.0 reduce-scatter.22.cloned.1.call-done
  1494.3 74.8 %while.70 = (s32[]{:T(128)}, bf16[4,512,4,64]{1,3,2,0:T(8,128)(2,1)}, f32[4,4,512]{2,1,0:T(4,128)S(1)}, s32[4]{0:T(128)S(1)}, bf16[2048,4,64]{0,2,1:T(8,128)(2,1...) while((s32[]{:T(128)}, ...), condition=%wide.region_9.9_spmd, body=%wide.region_6.8_spmd.sunk | while | flops 1125251584 | bytes 57217692 | solution.py:66
  1569.1 289.6 %while.71 = (s32[]{:T(128)}, f32[2048,4,64]{0,2,1:T(8,128)}, f32[2048,4,64]{0,2,1:T(8,128)}, f32[4,512,4,64]{1,0,3,2:T(4,128)}, s32[4]{0:T(128)S(1)}, /*index=5*...) while((s32[]{:T(128)}, f32[2048,4,64]{0,2,1:T(8,128)}, ...), condition=%wide.region_13.13_spmd.clone, body=%wide.region_11.12_spmd.clone.sunk | while | flops 2751068672 | bytes 187232528 | solution.py:107
  1582.7 12.6 multiply_reduce_fusion.2
  1654.1 12.6 multiply_reduce_fusion.2
  1726.7 12.6 multiply_reduce_fusion.2
  1799.4 12.6 multiply_reduce_fusion.2
  1872.8 23.9 convert_reduce_fusion.16
  1981.4 27.2 %reduce-scatter.28.cloned.1.call-done = bf16[8,4096]{1,0:T(8,128)(2,1)} async-done(((bf16[64,4096]{1,0:T(8,128)(2,1)}), bf16[8,4096]{1,0:T(8,128)(2,1)}) %reduce-scatter.28.cloned.1.call-update) | async-done | bytes 65552 | tf_op jit(solution)/shard_map/while
  2010.9 65.2 %reduce-scatter.26.cloned.1.call-done = bf16[24,4096]{1,0:T(8,128)(2,1)} async-done(((bf16[192,4096]{1,0:T(8,128)(2,1)}), bf16[24,4096]{1,0:T(8,128)(2,1)}) %reduce-scatter.26.cloned.1.call-update) | async-done | bytes 196624 | tf_op jit(solution)/shard_map/while
  2079.0 30.1 %reduce-scatter.40.cloned.1.call-done = bf16[1024,512]{1,0:T(8,128)(2,1)} async-done(((bf16[2048,512]{1,0:T(8,128)(2,1)}), bf16[1024,512]{1,0:T(8,128)(2,1)}) %reduce-scatter.40.cloned.1.call-update) | async-done | bytes 1048592 | tf_op jit(solution)/shard_map/while/body/eval_jaxpr/reduce_scatter | solution.py:280
  2109.1 34.1 %reduce-scatter.38.cloned.1.call-done = bf16[1024,512]{1,0:T(8,128)(2,1)} async-done(((bf16[2048,512]{1,0:T(8,128)(2,1)}), bf16[1024,512]{1,0:T(8,128)(2,1)}) %reduce-scatter.38.cloned.1.call-update) | async-done | bytes 1048592 | tf_op jit(solution)/shard_map/while/body/eval_jaxpr/reduce_scatter | solution.py:283
  2153.8 60.9 %reduce-scatter.36.cloned.1.call-done = bf16[256,512]{1,0:T(8,128)(2,1)} async-done(((bf16[2048,512]{1,0:T(8,128)(2,1)}), bf16[256,512]{1,0:T(8,128)(2,1)}) %reduce-scatter.36.cloned.1.call-update) | async-done | bytes 262160 | tf_op jit(solution)/shard_map/while/body/eval_jaxpr/reduce_scatter | solution.py:131
  2216.7 69.2 %reduce-scatter.34.cloned.1.call-done = bf16[512,256]{1,0:T(8,128)(2,1)} async-done(((bf16[512,2048]{1,0:T(8,128)(2,1)}), bf16[512,256]{1,0:T(8,128)(2,1)}) %reduce-scatter.34.cloned.1.call-update) | async-done | bytes 262160 | tf_op jit(solution)/shard_map/while/body/eval_jaxpr/reduce_scatter | solution.py:128
  2291.7 50.0 %reduce-scatter.42.cloned.1.call-done = f32[1024,512]{1,0:T(8,128)} async-done(((f32[2048,512]{1,0:T(8,128)}), f32[1024,512]{1,0:T(8,128)}) %reduce-scatter.42.cloned.1.call-update) | async-done | bytes 2097168 | tf_op jit(solution)/shard_map/while/body/eval_jaxpr/reduce_scatter | solution.py:224
  2352.9 40.6 %all-reduce.2 = (f32[1024]{0:T(1024)}, f32[1024]{0:T(1024)}, f32[1024]{0:T(1024)}, f32[1024]{0:T(1024)}, f32[16,192]{1,0:T(8,128)}, /*index=5*/f32[1024]{0:T(1024)S(1)}, f32[4096]{0:T(1024)}) all-reduce(f32[1024]{0:T(1024)S(1)} %dynamic_update_slice.41, ...), channel_id=1, replica_groups=mesh['dp'=8,'row'=2,'col'=2] {'dp','row','col'}, use_global_device_ids=true, to_apply=%region_35.36 | all-reduce | flops 12288 | bytes 98304 | tf_op jit(solution)/shard_map/psum | solution.py:350
  (626 shorter events, 964.3 us)
Async XLA Ops:
  13.8 313.6 %copy-start.16 = (f32[2048,1,16]{0,2,1:T(8,128)}, f32[2048,1,16]{0,2,1:T(8,128)S(1)}, u32[]{:S(2)}) copy-start(f32[2048,1,16]{0,2,1:T(8,128)S(1)} %get-tuple-element.1317) | copy-start | bytes 393220 | tf_op jit(solution)/shard_map/while
  13.8 313.6 %copy-start.19 = (f32[2048,1,16]{0,2,1:T(8,128)}, f32[2048,1,16]{0,2,1:T(8,128)S(1)}, u32[]{:S(2)}) copy-start(f32[2048,1,16]{0,2,1:T(8,128)S(1)} %get-tuple-element.1318) | copy-start | bytes 393220 | tf_op jit(solution)/shard_map/while
  13.9 45.4 %all-gather.20.cloned.1.call-start = ((), (), s32[]{:S(2)}) async-start(), calls=%async_computation.14 | async-start | bytes 3145728 | tf_op jit(solution)/shard_map/while/body/eval_jaxpr/all_gather | solution.py:204
  17.1 70.7 %all-gather.16.cloned.1.call-start = ((), (), s32[]{:S(2)}) async-start(), calls=%async_computation.11 | async-start | bytes 3145728 | tf_op jit(solution)/shard_map/while/body/eval_jaxpr/all_gather | solution.py:202
  23.7 110.5 %all-gather.18.cloned.1.call-start = ((), (), s32[]{:S(2)}) async-start(), calls=%async_computation.12 | async-start | bytes 1769472 | tf_op jit(solution)/shard_map/while/body/eval_jaxpr/all_gather | solution.py:113
  24.4 143.2 %all-gather.26.cloned.1.call-start = ((), (), s32[]{:S(2)}) async-start(), calls=%async_computation.20 | async-start | bytes 3145728 | tf_op jit(solution)/shard_map/while/body/eval_jaxpr/all_gather | solution.py:203
  25.0 195.7 %all-gather.30.cloned.1.call-start = ((), (), s32[]{:S(2)}) async-start(), calls=%async_computation.23 | async-start | bytes 2359296 | tf_op jit(solution)/shard_map/while/body/eval_jaxpr/all_gather | solution.py:115
  25.6 244.8 %all-gather.28.cloned.1.call-start = ((), (), s32[]{:S(2)}) async-start(), calls=%async_computation.21 | async-start | bytes 2359296 | tf_op jit(solution)/shard_map/while/body/eval_jaxpr/all_gather | solution.py:116
  26.1 257.0 %reduce-scatter.24.cloned.1.call-start = ((), (), s32[]{:S(2)}) async-start(), calls=%async_computation.15 | async-start | bytes 6291456 | tf_op jit(solution)/shard_map/while/body/eval_jaxpr/reduce_scatter | solution.py:239
  64.5 243.8 %reduce-scatter.22.cloned.1.call-start = ((), (), s32[]{:S(2)}) async-start(), calls=%async_computation.13 | async-start | bytes 18874368 | tf_op jit(solution)/shard_map/while/body/eval_jaxpr/reduce_scatter | solution.py:209
  144.9 563.8 %reduce-scatter.32.cloned.1.call-start = ((), (), s32[]{:S(2)}) async-start(), calls=%async_computation.24 | async-start | bytes 25165824 | tf_op jit(solution)/shard_map/while/body/eval_jaxpr/reduce_scatter | solution.py:210
  233.2 475.5 %reduce-scatter.30.cloned.1.call-start = ((), (), s32[]{:S(2)}) async-start(), calls=%async_computation.22 | async-start | bytes 25165824 | tf_op jit(solution)/shard_map/while/body/eval_jaxpr/reduce_scatter | solution.py:240
  281.5 461.5 %all-gather.24.cloned.1.call-start = ((), (), s32[]{:S(2)}) async-start(), calls=%async_computation.18 | async-start | bytes 3145728 | tf_op jit(solution)/shard_map/while/body/eval_jaxpr/all_gather | solution.py:221
  701.5 47.9 %all-gather.22.cloned.1.call-start = ((), (), s32[]{:S(2)}) async-start(), calls=%async_computation.16 | async-start | bytes 9437184 | tf_op jit(solution)/shard_map/while/body/eval_jaxpr/all_gather | solution.py:264
  708.6 59.2 %all-gather.32.cloned.1.call-start = ((), (), s32[]{:S(2)}) async-start(), calls=%async_computation.25 | async-start | bytes 12582912 | tf_op jit(solution)/shard_map/while/body/eval_jaxpr/all_gather | solution.py:265
  732.7 47.1 %all-gather.34.cloned.1.call-start = ((), (), s32[]{:S(2)}) async-start(), calls=%async_computation.27 | async-start | bytes 12582912 | tf_op jit(solution)/shard_map/while/body/eval_jaxpr/all_gather | solution.py:222
  743.0 101.5 %reduce-scatter.28.cloned.1.call-start = ((), (), s32[]{:S(2)}) async-start(), calls=%async_computation.19 | async-start | bytes 589824 | tf_op jit(solution)/shard_map/while
  749.0 163.0 %reduce-scatter.26.cloned.1.call-start = ((), (), s32[]{:S(2)}) async-start(), calls=%async_computation.17 | async-start | bytes 1769472 | tf_op jit(solution)/shard_map/while
  759.5 185.4 %reduce-scatter.40.cloned.1.call-start = ((), (), s32[]{:S(2)}) async-start(), calls=%async_computation.30 | async-start | bytes 3145728 | tf_op jit(solution)/shard_map/while/body/eval_jaxpr/reduce_scatter | solution.py:280
  767.7 211.2 %reduce-scatter.38.cloned.1.call-start = ((), (), s32[]{:S(2)}) async-start(), calls=%async_computation.29 | async-start | bytes 3145728 | tf_op jit(solution)/shard_map/while/body/eval_jaxpr/reduce_scatter | solution.py:283
  779.5 271.1 %reduce-scatter.36.cloned.1.call-start = ((), (), s32[]{:S(2)}) async-start(), calls=%async_computation.28 | async-start | bytes 2359296 | tf_op jit(solution)/shard_map/while/body/eval_jaxpr/reduce_scatter | solution.py:131
  789.3 332.4 %reduce-scatter.34.cloned.1.call-start = ((), (), s32[]{:S(2)}) async-start(), calls=%async_computation.26 | async-start | bytes 2359296 | tf_op jit(solution)/shard_map/while/body/eval_jaxpr/reduce_scatter | solution.py:128
  799.4 378.0 %reduce-scatter.42.cloned.1.call-start = ((), (), s32[]{:S(2)}) async-start(), calls=%async_computation.31 | async-start | bytes 6291456 | tf_op jit(solution)/shard_map/while/body/eval_jaxpr/reduce_scatter | solution.py:224
  814.7 308.8 %copy-start.8 = (bf16[1,1024,512]{2,1,0:T(8,128)(2,1)S(1)}, bf16[1,1024,512]{2,1,0:T(8,128)(2,1)}, u32[]{:S(2)}) copy-start(bf16[1,1024,512]{2,1,0:T(8,128)(2,1)} %get-tuple-element.1104) | copy-start | bytes 3145732 | tf_op jit(solution)/shard_map/while
  1180.6 310.9 %copy-start.16 = (f32[2048,1,16]{0,2,1:T(8,128)}, f32[2048,1,16]{0,2,1:T(8,128)S(1)}, u32[]{:S(2)}) copy-start(f32[2048,1,16]{0,2,1:T(8,128)S(1)} %get-tuple-element.1317) | copy-start | bytes 393220 | tf_op jit(solution)/shard_map/while
  1180.6 310.9 %copy-start.19 = (f32[2048,1,16]{0,2,1:T(8,128)}, f32[2048,1,16]{0,2,1:T(8,128)S(1)}, u32[]{:S(2)}) copy-start(f32[2048,1,16]{0,2,1:T(8,128)S(1)} %get-tuple-element.1318) | copy-start | bytes 393220 | tf_op jit(solution)/shard_map/while
  1180.6 43.7 %all-gather.20.cloned.1.call-start = ((), (), s32[]{:S(2)}) async-start(), calls=%async_computation.14 | async-start | bytes 3145728 | tf_op jit(solution)/shard_map/while/body/eval_jaxpr/all_gather | solution.py:204
  1183.9 68.0 %all-gather.16.cloned.1.call-start = ((), (), s32[]{:S(2)}) async-start(), calls=%async_computation.11 | async-start | bytes 3145728 | tf_op jit(solution)/shard_map/while/body/eval_jaxpr/all_gather | solution.py:202
  1190.3 107.8 %all-gather.18.cloned.1.call-start = ((), (), s32[]{:S(2)}) async-start(), calls=%async_computation.12 | async-start | bytes 1769472 | tf_op jit(solution)/shard_map/while/body/eval_jaxpr/all_gather | solution.py:113
  1190.9 140.8 %all-gather.26.cloned.1.call-start = ((), (), s32[]{:S(2)}) async-start(), calls=%async_computation.20 | async-start | bytes 3145728 | tf_op jit(solution)/shard_map/while/body/eval_jaxpr/all_gather | solution.py:203
  1191.7 193.1 %all-gather.30.cloned.1.call-start = ((), (), s32[]{:S(2)}) async-start(), calls=%async_computation.23 | async-start | bytes 2359296 | tf_op jit(solution)/shard_map/while/body/eval_jaxpr/all_gather | solution.py:115
  1192.2 242.2 %all-gather.28.cloned.1.call-start = ((), (), s32[]{:S(2)}) async-start(), calls=%async_computation.21 | async-start | bytes 2359296 | tf_op jit(solution)/shard_map/while/body/eval_jaxpr/all_gather | solution.py:116
  1192.8 254.5 %reduce-scatter.24.cloned.1.call-start = ((), (), s32[]{:S(2)}) async-start(), calls=%async_computation.15 | async-start | bytes 6291456 | tf_op jit(solution)/shard_map/while/body/eval_jaxpr/reduce_scatter | solution.py:239
  1229.6 242.9 %reduce-scatter.22.cloned.1.call-start = ((), (), s32[]{:S(2)}) async-start(), calls=%async_computation.13 | async-start | bytes 18874368 | tf_op jit(solution)/shard_map/while/body/eval_jaxpr/reduce_scatter | solution.py:209
  1308.8 563.9 %reduce-scatter.32.cloned.1.call-start = ((), (), s32[]{:S(2)}) async-start(), calls=%async_computation.24 | async-start | bytes 25165824 | tf_op jit(solution)/shard_map/while/body/eval_jaxpr/reduce_scatter | solution.py:210
  1397.3 475.5 %reduce-scatter.30.cloned.1.call-start = ((), (), s32[]{:S(2)}) async-start(), calls=%async_computation.22 | async-start | bytes 25165824 | tf_op jit(solution)/shard_map/while/body/eval_jaxpr/reduce_scatter | solution.py:240
  1445.6 461.5 %all-gather.24.cloned.1.call-start = ((), (), s32[]{:S(2)}) async-start(), calls=%async_computation.18 | async-start | bytes 3145728 | tf_op jit(solution)/shard_map/while/body/eval_jaxpr/all_gather | solution.py:221
  1865.6 48.0 %all-gather.22.cloned.1.call-start = ((), (), s32[]{:S(2)}) async-start(), calls=%async_computation.16 | async-start | bytes 9437184 | tf_op jit(solution)/shard_map/while/body/eval_jaxpr/all_gather | solution.py:264
  1872.7 59.1 %all-gather.32.cloned.1.call-start = ((), (), s32[]{:S(2)}) async-start(), calls=%async_computation.25 | async-start | bytes 12582912 | tf_op jit(solution)/shard_map/while/body/eval_jaxpr/all_gather | solution.py:265
  1896.8 47.0 %all-gather.34.cloned.1.call-start = ((), (), s32[]{:S(2)}) async-start(), calls=%async_computation.27 | async-start | bytes 12582912 | tf_op jit(solution)/shard_map/while/body/eval_jaxpr/all_gather | solution.py:222
  1907.0 101.5 %reduce-scatter.28.cloned.1.call-start = ((), (), s32[]{:S(2)}) async-start(), calls=%async_computation.19 | async-start | bytes 589824 | tf_op jit(solution)/shard_map/while
  1913.0 163.1 %reduce-scatter.26.cloned.1.call-start = ((), (), s32[]{:S(2)}) async-start(), calls=%async_computation.17 | async-start | bytes 1769472 | tf_op jit(solution)/shard_map/while
  1923.5 185.7 %reduce-scatter.40.cloned.1.call-start = ((), (), s32[]{:S(2)}) async-start(), calls=%async_computation.30 | async-start | bytes 3145728 | tf_op jit(solution)/shard_map/while/body/eval_jaxpr/reduce_scatter | solution.py:280
  1931.7 211.4 %reduce-scatter.38.cloned.1.call-start = ((), (), s32[]{:S(2)}) async-start(), calls=%async_computation.29 | async-start | bytes 3145728 | tf_op jit(solution)/shard_map/while/body/eval_jaxpr/reduce_scatter | solution.py:283
  1943.5 271.3 %reduce-scatter.36.cloned.1.call-start = ((), (), s32[]{:S(2)}) async-start(), calls=%async_computation.28 | async-start | bytes 2359296 | tf_op jit(solution)/shard_map/while/body/eval_jaxpr/reduce_scatter | solution.py:131
  1953.3 332.7 %reduce-scatter.34.cloned.1.call-start = ((), (), s32[]{:S(2)}) async-start(), calls=%async_computation.26 | async-start | bytes 2359296 | tf_op jit(solution)/shard_map/while/body/eval_jaxpr/reduce_scatter | solution.py:128
  1963.3 378.4 %reduce-scatter.42.cloned.1.call-start = ((), (), s32[]{:S(2)}) async-start(), calls=%async_computation.31 | async-start | bytes 6291456 | tf_op jit(solution)/shard_map/while/body/eval_jaxpr/reduce_scatter | solution.py:224
  1978.6 309.3 %copy-start.8 = (bf16[1,1024,512]{2,1,0:T(8,128)(2,1)S(1)}, bf16[1,1024,512]{2,1,0:T(8,128)(2,1)}, u32[]{:S(2)}) copy-start(bf16[1,1024,512]{2,1,0:T(8,128)(2,1)} %get-tuple-element.1104) | copy-start | bytes 3145732 | tf_op jit(solution)/shard_map/while
  (98 other events, 3984.8 us)
Sparse Core Ops, SparseCore 0:
  17.2 35.8 all-gather.19
  54.6 33.1 all-gather.15
  90.0 44.1 all-gather.17
  135.7 31.9 all-gather.25
  169.5 51.0 all-gather.29
  222.8 47.4 all-gather.27
  272.6 10.5 reduce-scatter.23
  285.5 22.7 reduce-scatter.21
  310.6 27.3 reduce-scatter.31
  340.3 27.5 reduce-scatter.29
  701.6 11.8 all-gather.23
  715.0 17.9 all-gather.21
  734.6 21.0 all-gather.31
  757.1 21.0 all-gather.33
  781.3 63.0 reduce-scatter.27
  848.1 63.7 reduce-scatter.25
  914.0 30.7 reduce-scatter.39
  947.0 31.8 reduce-scatter.37
  982.9 67.6 reduce-scatter.35
  1054.4 67.2 reduce-scatter.33
  1124.1 53.2 reduce-scatter.41
  1184.0 33.1 all-gather.19
  1218.7 33.1 all-gather.15
  1253.9 44.1 all-gather.17
  1299.8 31.9 all-gather.25
  1333.6 51.0 all-gather.29
  1386.9 47.4 all-gather.27
  1436.7 10.5 reduce-scatter.23
  1449.6 22.7 reduce-scatter.21
  1474.6 27.3 reduce-scatter.31
  1504.4 27.5 reduce-scatter.29
  1865.7 11.7 all-gather.23
  1879.0 17.9 all-gather.21
  1898.5 21.0 all-gather.31
  1921.2 21.0 all-gather.33
  1945.5 63.0 reduce-scatter.27
  2012.2 63.8 reduce-scatter.25
  2078.3 30.7 reduce-scatter.39
  2111.3 31.8 reduce-scatter.37
  2147.1 67.6 reduce-scatter.35
  2218.7 67.2 reduce-scatter.33
  2288.4 53.2 reduce-scatter.41
where the time goes:
time: 2410 us; the launch traced here: 2400 us
  waiting for transfers between devices  1090 us (45%)
  matrix products  636 us (26%)
  other arithmetic  322 us (13%)
  local copies, waits for them, and re-layouts  181 us (8%)
  blocking collectives  117 us (5%)
  loops' own time  37.3 us (2%)
    while x46, waiting for transfers between devices  190 us
    reduce_scatter x2, waiting for transfers between devices, reduce_tiles(): lax.psum_scatter(third_tile.astype(jnp.bfloat16), 'dp', scatter_dimension...  138 us
    reduce_scatter x2, waiting for transfers between devices, reduce_tiles(): lax.psum_scatter(fourth_tile.astype(jnp.bfloat16), 'dp', scatter_dimensio...  122 us
    dot_general x16, matrix products, causal_scores(): jnp.einsum('qhe,khe->hqk', query_block, keys_all, preferred_element_type=...  111 us
    all_gather x2, waiting for transfers between devices, gather_tiles(): lax.all_gather(expand_weight, 'dp', axis=1, tiled=True)  106 us
    dot_general x8, matrix products, one_block(): jnp.einsum('qhe,khe->hqk', grad_block, values, preferred_element_type=jnp...  101 us
    reduce_scatter x2, waiting for transfers between devices, micro_step(): lax.psum_scatter(jnp.dot(attended_full, output_flat, preferred_element_ty...  100 us
    dot_general x8, matrix products, one_block(): jnp.einsum('hqk,qhe->khe', probability.astype(jnp.bfloat16), grad_block,...  98.5 us
  transfers between devices with their start and end apart: 42, of which 28 were waited for; matrix products, arithmetic and copies ran while one was open for 46% of the time, Pallas kernels for 0%

commit v1 on v0

v1 whole, which is shorter than its diff:
```python
from functools import partial

import jax
import jax.numpy as jnp
import numpy as np
from jax import lax
from jax.experimental import pallas as pl
from jax.experimental.pallas import tpu as pltpu
from jax.sharding import PartitionSpec as P

D = 1024
HS = 64
ROT = 16
HALF = ROT // 2
EPSILON = 1e-05
MASKED = -1e30
NN = (((1,), (0,)), ((), ()))
NT = (((1,), (1,)), ((), ()))
TN = (((0,), (0,)), ((), ()))
VMEM_LIMIT = 56 << 20
F32 = jnp.float32
BF16 = jnp.bfloat16


def mm(a, b, dims):
    return lax.dot_general(a, b, dims, preferred_element_type=F32)


def params(**extra):
    return pltpu.CompilerParams(vmem_limit_bytes=VMEM_LIMIT, **extra)


def cost(flops, nbytes):
    return pl.CostEstimate(flops=int(flops), bytes_accessed=int(nbytes), transcendentals=0)


def whole(shape):
    return pl.BlockSpec(shape, lambda *_: (0,) * len(shape))


def project_kernel(xa, xc, weight, bias, vectors, cosine, sine, first, second, triple):
    wide = xa.shape[1]
    near = xa[...].astype(F32)
    far = xc[...].astype(F32)
    total = jnp.sum(near + far, axis=1, keepdims=True)
    squares = jnp.sum(near * near + far * far, axis=1, keepdims=True)
    width = 2 * wide
    center = total / width
    inv = lax.rsqrt(squares / width - center * center + EPSILON)
    for part, values in ((0, near), (1, far)):
        cols = slice(part * wide, (part + 1) * wide)
        normed = (values - center) * inv
        first[:, cols] = (normed * vectors[0:1, cols] + vectors[1:2, cols]).astype(BF16)
        second[:, cols] = (normed * vectors[2:3, cols] + vectors[3:4, cols]).astype(BF16)
    heads = weight.shape[0] // (3 * HS)
    cos, sin = cosine[...], sine[...]
    for head in range(heads):
        base = head * 3 * HS
        rows = mm(weight[base : base + 3 * HS, :], first[...], NT) + bias[base : base + 3 * HS, :]
        for which in range(3):
            lo = which * HS
            scale = HS ** (-0.5) if which == 0 else 1.0
            out = base + lo
            if which < 2:
                u1, u2 = rows[lo : lo + HALF], rows[lo + HALF : lo + ROT]
                spun = jnp.concatenate([u1 * cos - u2 * sin, u2 * cos + u1 * sin], axis=0)
                triple[out : out + ROT, :] = (spun * scale).astype(BF16)
                triple[out + ROT : out + HS, :] = (rows[lo + ROT : lo + HS] * scale).astype(BF16)
            else:
                triple[out : out + HS, :] = rows[lo : lo + HS].astype(BF16)


def project(xa, xc, weight, bias, vectors, cosine, sine, block=512):
    tokens, wide = xa.shape
    rows = weight.shape[0]
    block = min(block, tokens)
    tile = pl.BlockSpec((block, wide), lambda i: (i, 0))
    full = pl.BlockSpec((block, 2 * wide), lambda i: (i, 0))
    table = pl.BlockSpec((HALF, block), lambda i: (0, i))
    return pl.pallas_call(
        project_kernel,
        grid=(tokens // block,),
        in_specs=[tile, tile, whole(weight.shape), whole(bias.shape), whole(vectors.shape), table, table],
        out_specs=[full, full, pl.BlockSpec((rows, block), lambda i: (0, i))],
        out_shape=[
            jax.ShapeDtypeStruct((tokens, 2 * wide), BF16),
            jax.ShapeDtypeStruct((tokens, 2 * wide), BF16),
            jax.ShapeDtypeStruct((rows, tokens), BF16),
        ],
        compiler_params=params(),
        cost_estimate=cost(3 * tokens * rows * wide * 2, tokens * wide * 2 * 2 * 3),
        name="project",
    )(xa, xc, weight, bias, vectors, cosine, sine)


def causal_tile(size):
    keys = lax.broadcasted_iota(jnp.int32, (size, size), 0)
    places = lax.broadcasted_iota(jnp.int32, (size, size), 1)
    return keys <= places


def lanes(index, tokens):
    return pl.ds(pl.multiple_of(index * tokens, tokens), tokens)


def attend_kernel(row, own, far, out_own, out_far, logsum, q_s, k_s, v_s, o_s, *, step):
    tokens = own.shape[1]
    length = 2 * tokens
    here = row[0]
    there = 1 - here
    for ref, place in ((own, here), (far, there)):
        at = lanes(place, tokens)
        q_s[:, at] = ref[0:HS, :]
        k_s[:, at] = ref[HS : 2 * HS, :]
        v_s[0:HS, at] = ref[2 * HS : 3 * HS, :]
    extra = lax.broadcasted_iota(jnp.int32, (16, length), 0)
    v_s[HS : HS + 16, :] = jnp.where(extra == 0, 1.0, 0.0).astype(BF16)
    allowed = causal_tile(step)
    for i in range(length // step):
        lo, hi = i * step, (i + 1) * step
        query = q_s[:, lo:hi]
        diag = jnp.where(allowed, mm(k_s[:, lo:hi], query, TN), MASKED)
        highest = jnp.max(diag, axis=0, keepdims=True)
        if i:
            past = mm(k_s[:, :lo], query, TN)
            highest = jnp.maximum(highest, jnp.max(past, axis=0, keepdims=True))
        raised = jnp.exp(diag - highest).astype(BF16)
        result = mm(v_s[:, lo:hi], raised, NN)
        if i:
            raised = jnp.exp(past - highest).astype(BF16)
            result = result + mm(v_s[:, :lo], raised, NN)
        total = result[HS : HS + 1]
        o_s[:, lo:hi] = (result[:HS] / total).astype(BF16)
        logsum[0, :, lo:hi] = highest + jnp.log(total)
    out_own[...] = o_s[:, lanes(here, tokens)]
    out_far[...] = o_s[:, lanes(there, tokens)]


def attend(row, own, far, step=256):
    rows, tokens = own.shape
    heads = rows // (3 * HS)
    length = 2 * tokens
    source = pl.BlockSpec((3 * HS, tokens), lambda h: (h, 0))
    result = pl.BlockSpec((HS, tokens), lambda h: (h, 0))
    return pl.pallas_call(
        partial(attend_kernel, step=min(step, length)),
        grid=(heads,),
        in_specs=[pl.BlockSpec(memory_space=pltpu.SMEM), source, source],
        out_specs=[result, result, pl.BlockSpec((1, 1, length), lambda h: (h, 0, 0))],
        out_shape=[
            jax.ShapeDtypeStruct((heads * HS, tokens), BF16),
            jax.ShapeDtypeStruct((heads * HS, tokens), BF16),
            jax.ShapeDtypeStruct((heads, 1, length), F32),
        ],
        scratch_shapes=[
            pltpu.VMEM((HS, length), BF16),
            pltpu.VMEM((HS, length), BF16),
            pltpu.VMEM((HS + 16, length), BF16),
            pltpu.VMEM((HS, length), BF16),
        ],
        compiler_params=params(),
        cost_estimate=cost(heads * length * length * 256 * 2, 8 * rows * tokens),
        name="attend",
    )(row, own, far)


def attend_back_kernel(
    row, own, far, grad_own, grad_far, att_own, att_far, logsum, cosine, sine,
    out_own, out_far, bias_grad, q_s, k_s, v_s, g_s, delta_s, dq_s, dk_s, dv_s, t_s, *, step,
):
    tokens = own.shape[1]
    length = 2 * tokens
    here = row[0]
    there = 1 - here
    for ref, grad, att, place in (
        (own, grad_own, att_own, here),
        (far, grad_far, att_far, there),
    ):
        at = lanes(place, tokens)
        q_s[:, at] = ref[0:HS, :]
        k_s[:, at] = ref[HS : 2 * HS, :]
        v_s[:, at] = ref[2 * HS : 3 * HS, :]
        g_s[:, at] = grad[...]
        delta_s[:, at] = jnp.sum(
            grad[...].astype(F32) * att[...].astype(F32), axis=0, keepdims=True
        )
    dk_s[...] = jnp.zeros_like(dk_s)
    dv_s[...] = jnp.zeros_like(dv_s)
    allowed = causal_tile(step)
    for i in range(length // step):
        lo, hi = i * step, (i + 1) * step
        query, grad = q_s[:, lo:hi], g_s[:, lo:hi]
        base, delta = logsum[0, :, lo:hi], delta_s[:, lo:hi]
        query_grad = None
        for begin, end in ((0, lo), (lo, hi)):
            if end == begin:
                continue
            raised = jnp.exp(mm(k_s[:, begin:end], query, TN) - base)
            if begin == lo:
                raised = jnp.where(allowed, raised, 0.0)
            prob_grad = mm(v_s[:, begin:end], grad, TN)
            score_grad = (raised * (prob_grad - delta)).astype(BF16)
            dv_s[:, begin:end] += mm(grad, raised.astype(BF16), NT)
            dk_s[:, begin:end] += mm(query, score_grad, NT)
            term = mm(k_s[:, begin:end], score_grad, NN)
            query_grad = term if query_grad is None else query_grad + term
        dq_s[:, lo:hi] = query_grad * HS ** (-0.5)
    cos, sin = cosine[...], sine[...]
    for which, ref in ((0, dq_s), (1, dk_s)):
        g1, g2 = ref[0:HALF, :], ref[HALF:ROT, :]
        spun = jnp.concatenate([g1 * cos + g2 * sin, g2 * cos - g1 * sin], axis=0)
        t_s[which * HS : which * HS + ROT, :] = spun.astype(BF16)
        t_s[which * HS + ROT : (which + 1) * HS, :] = ref[ROT:HS, :].astype(BF16)
    t_s[2 * HS : 3 * HS, :] = dv_s[...].astype(BF16)
    bias_grad[...] = jnp.sum(t_s[...].astype(F32), axis=1, keepdims=True)
    out_own[...] = t_s[:, lanes(here, tokens)]
    out_far[...] = t_s[:, lanes(there, tokens)]


def attend_back(row, own, far, grad_own, grad_far, att_own, att_far, logsum, cosine, sine, step=256):
    rows, tokens = own.shape
    heads = rows // (3 * HS)
    length = 2 * tokens
    source = pl.BlockSpec((3 * HS, tokens), lambda h: (h, 0))
    narrow = pl.BlockSpec((HS, tokens), lambda h: (h, 0))
    table = whole((HALF, length))
    return pl.pallas_call(
        partial(attend_back_kernel, step=min(step, length)),
        grid=(heads,),
        in_specs=[
            pl.BlockSpec(memory_space=pltpu.SMEM), source, source, narrow, narrow, narrow, narrow,
            pl.BlockSpec((1, 1, length), lambda h: (h, 0, 0)), table, table,
        ],
        out_specs=[source, source, pl.BlockSpec((3 * HS, 1), lambda h: (h, 0))],
        out_shape=[
            jax.ShapeDtypeStruct((rows, tokens), BF16),
            jax.ShapeDtypeStruct((rows, tokens), BF16),
            jax.ShapeDtypeStruct((rows, 1), F32),
        ],
        scratch_shapes=[
            pltpu.VMEM((HS, length), BF16),
            pltpu.VMEM((HS, length), BF16),
            pltpu.VMEM((HS, length), BF16),
            pltpu.VMEM((HS, length), BF16),
            pltpu.VMEM((1, length), F32),
            pltpu.VMEM((HS, length), F32),
            pltpu.VMEM((HS, length), F32),
            pltpu.VMEM((HS, length), F32),
            pltpu.VMEM((3 * HS, length), BF16),
        ],
        compiler_params=params(),
        cost_estimate=cost(heads * length * length * 256 * 5, 16 * rows * tokens),
        name="attend_back",
    )(row, own, far, grad_own, grad_far, att_own, att_far, logsum, cosine, sine)


POLY = (0.254829592, -0.284496736, 1.421413741, -1.453152027, 1.061405429)


def gelu_pair(value):
    magnitude = jnp.abs(value)
    t = 1.0 / (1.0 + magnitude * (0.3275911 * 0.5**0.5))
    bell = jnp.exp(value * value * -0.5)
    series = POLY[4]
    for term in (POLY[3], POLY[2], POLY[1], POLY[0]):
        series = series * t + term
    tail = 0.5 * series * t * bell
    cumulative = jnp.where(value >= 0.0, 1.0 - tail, tail)
    return value * cumulative, cumulative + value * bell * (1.0 / (2.0 * np.pi) ** 0.5)


def middle_kernel(
    second_own, second_far, ca, cb, cc, cd, att_own, att_far, w1, w2, wo, bias,
    out_near, out_other, heads_own, heads_far, part_own, part_far, dw1, dw2, dwo, dbias,
    s_s, c_s, a_s, act_s, eg_s, h_s, *, chunk,
):
    half, at = pl.program_id(0), pl.program_id(1)
    wide = ca.shape[1]

    @pl.when((half == 0) & (at == 0))
    def _():
        dw1[...] = jnp.zeros_like(dw1)
        dw2[...] = jnp.zeros_like(dw2)
        dwo[...] = jnp.zeros_like(dwo)
        dbias[...] = jnp.zeros_like(dbias)

    for this, second, near, other, att in (
        (0, second_far, cb, cd, att_far),
        (1, second_own, ca, cc, att_own),
    ):
        @pl.when(half == this)
        def _():
            s_s[...] = second[...]
            c_s[:, :wide] = near[...]
            c_s[:, wide:] = other[...]
            a_s[...] = att[...]

    hidden = w1.shape[0]
    for lo in range(0, hidden, chunk):
        hi = lo + chunk
        expanded = mm(s_s[...], w1[lo:hi, :], NT) + bias[:, lo:hi]
        active, slope = gelu_pair(expanded)
        act_s[:, lo:hi] = active.astype(BF16)
        expand_grad = mm(c_s[...], w2[lo:hi, :], NT) * slope
        rounded = expand_grad.astype(BF16)
        eg_s[:, lo:hi] = rounded
        dbias[:, lo:hi] += jnp.sum(rounded.astype(F32), axis=0, keepdims=True)
    for lo in range(0, hidden, chunk):
        hi = lo + chunk
        dw2[lo:hi, :] += mm(act_s[:, lo:hi], c_s[...], TN)
        dw1[lo:hi, :] += mm(eg_s[:, lo:hi], s_s[...], TN)
    dwo[...] += mm(a_s[...], c_s[...], NN)
    h_s[...] = mm(wo[...], c_s[...], NT).astype(BF16)
    near = mm(act_s[...], w2[:, :wide], NN) + mm(a_s[...], wo[:, :wide], TN)
    out_near[0] = near.astype(BF16)
    other = mm(act_s[...], w2[:, wide:], NN) + mm(a_s[...], wo[:, wide:], TN)
    out_other[0] = other.astype(BF16)
    part = mm(eg_s[...], w1[...], NN).astype(BF16)
    for this, heads, ref in ((0, heads_far, part_far), (1, heads_own, part_own)):
        @pl.when(half == this)
        def _():
            heads[...] = h_s[...]
            ref[...] = part


def middle(second_own, second_far, ca, cb, cc, cd, att_own, att_far, w1, w2, wo, bias, block=256, chunk=256):
    tokens, wide = ca.shape
    width = 2 * wide
    block = min(block, tokens)
    steps = tokens // block
    hidden, head_rows = w1.shape[0], wo.shape[0]
    last = steps - 1
    far_at = lambda h, i: i * (1 - h) + last * h
    own_at = lambda h, i: i * h
    rows_far = lambda n: pl.BlockSpec((block, n), lambda h, i: (far_at(h, i), 0))
    rows_own = lambda n: pl.BlockSpec((block, n), lambda h, i: (own_at(h, i), 0))
    cols_far = pl.BlockSpec((head_rows, block), lambda h, i: (0, far_at(h, i)))
    cols_own = pl.BlockSpec((head_rows, block), lambda h, i: (0, own_at(h, i)))
    both = pl.BlockSpec((1, block, wide), lambda h, i: (h, i, 0))
    return pl.pallas_call(
        partial(middle_kernel, chunk=min(chunk, hidden)),
        grid=(2, steps),
        in_specs=[
            rows_own(width), rows_far(width), rows_own(wide), rows_far(wide), rows_own(wide), rows_far(wide),
            cols_own, cols_far, whole(w1.shape), whole(w2.shape), whole(wo.shape), whole(bias.shape),
        ],
        out_specs=[
            both, both, cols_own, cols_far, rows_own(width), rows_far(width),
            whole(w1.shape), whole(w2.shape), whole(wo.shape), whole(bias.shape),
        ],
        out_shape=[
            jax.ShapeDtypeStruct((2, tokens, wide), BF16),
            jax.ShapeDtypeStruct((2, tokens, wide), BF16),
            jax.ShapeDtypeStruct((head_rows, tokens), BF16),
            jax.ShapeDtypeStruct((head_rows, tokens), BF16),
            jax.ShapeDtypeStruct((tokens, width), BF16),
            jax.ShapeDtypeStruct((tokens, width), BF16),
            jax.ShapeDtypeStruct(w1.shape, F32),
            jax.ShapeDtypeStruct(w2.shape, F32),
            jax.ShapeDtypeStruct(wo.shape, F32),
            jax.ShapeDtypeStruct(bias.shape, F32),
        ],
        scratch_shapes=[
            pltpu.VMEM((block, width), BF16),
            pltpu.VMEM((block, width), BF16),
            pltpu.VMEM((head_rows, block), BF16),
            pltpu.VMEM((block, hidden), BF16),
            pltpu.VMEM((block, hidden), BF16),
            pltpu.VMEM((head_rows, block), BF16),
        ],
        compiler_params=params(),
        cost_estimate=cost(2 * tokens * 2 * width * (6 * hidden + 3 * head_rows), 2 * tokens * width * 10),
        name="middle",
    )(second_own, second_far, ca, cb, cc, cd, att_own, att_far, w1, w2, wo, bias)


def last_kernel(
    t_own, t_far, first_own, first_far, part_own, part_far, xa, xb, xc, xd, weight, vectors,
    ng_near, ng_other, sums, dweight, dvec, t_s, f_s, p_s, x_s,
):
    half, at = pl.program_id(0), pl.program_id(1)
    wide = xa.shape[1]

    @pl.when((half == 0) & (at == 0))
    def _():
        dweight[...] = jnp.zeros_like(dweight)
        dvec[...] = jnp.zeros_like(dvec)

    for this, t, first, part, near, other in (
        (0, t_far, first_far, part_far, xb, xd),
        (1, t_own, first_own, part_own, xa, xc),
    ):
        @pl.when(half == this)
        def _():
            t_s[...] = t[...]
            f_s[...] = first[...]
            p_s[...] = part[...]
            x_s[:, :wide] = near[...]
            x_s[:, wide:] = other[...]

    values = x_s[...].astype(F32)
    width = 2 * wide
    center = jnp.sum(values, axis=1, keepdims=True) / width
    spread = jnp.sum(values * values, axis=1, keepdims=True) / width - center * center
    inv = lax.rsqrt(spread + EPSILON)
    dweight[...] += mm(t_s[...], f_s[...], NN)
    first_sum = second_sum = 0.0
    for part, ref in ((0, ng_near), (1, ng_other)):
        cols = slice(part * wide, (part + 1) * wide)
        normed = (x_s[:, cols].astype(F32) - center) * inv
        first_grad = mm(t_s[...], weight[:, cols], TN)
        second_grad = p_s[:, cols].astype(F32)
        dvec[0:1, cols] += jnp.sum(first_grad * normed, axis=0, keepdims=True)
        dvec[1:2, cols] += jnp.sum(first_grad, axis=0, keepdims=True)
        dvec[2:3, cols] += jnp.sum(second_grad * normed, axis=0, keepdims=True)
        dvec[3:4, cols] += jnp.sum(second_grad, axis=0, keepdims=True)
        grad = first_grad * vectors[0:1, cols] + second_grad * vectors[2:3, cols]
        first_sum = first_sum + jnp.sum(grad, axis=1, keepdims=True)
        second_sum = second_sum + jnp.sum(grad * normed, axis=1, keepdims=True)
        ref[0] = grad.astype(BF16)
    column = lax.broadcasted_iota(jnp.int32, (x_s.shape[0], 128), 1)
    sums[0] = jnp.where(column == 0, first_sum, jnp.where(column == 1, second_sum, 0.0))


def last(t_own, t_far, first_own, first_far, part_own, part_far, xa, xb, xc, xd, weight, vectors, block=512):
    tokens, wide = xa.shape
    width = 2 * wide
    block = min(block, tokens)
    steps = tokens // block
    rows = weight.shape[0]
    end = steps - 1
    far_at = lambda h, i: i * (1 - h) + end * h
    own_at = lambda h, i: i * h
    rows_far = lambda n: pl.BlockSpec((block, n), lambda h, i: (far_at(h, i), 0))
    rows_own = lambda n: pl.BlockSpec((block, n), lambda h, i: (own_at(h, i), 0))
    cols_far = pl.BlockSpec((rows, block), lambda h, i: (0, far_at(h, i)))
    cols_own = pl.BlockSpec((rows, block), lambda h, i: (0, own_at(h, i)))
    both = pl.BlockSpec((1, block, wide), lambda h, i: (h, i, 0))
    return pl.pallas_call(
        last_kernel,
        grid=(2, steps),
        in_specs=[
            cols_own, cols_far, rows_own(width), rows_far(width), rows_own(width), rows_far(width),
            rows_own(wide), rows_far(wide), rows_own(wide), rows_far(wide),
            whole(weight.shape), whole(vectors.shape),
        ],
        out_specs=[
            both, both, pl.BlockSpec((1, block, 128), lambda h, i: (h, i, 0)),
            whole(weight.shape), whole((8, width)),
        ],
        out_shape=[
            jax.ShapeDtypeStruct((2, tokens, wide), BF16),
            jax.ShapeDtypeStruct((2, tokens, wide), BF16),
            jax.ShapeDtypeStruct((2, tokens, 128), F32),
            jax.ShapeDtypeStruct(weight.shape, F32),
            jax.ShapeDtypeStruct((8, width), F32),
        ],
        scratch_shapes=[
            pltpu.VMEM((rows, block), BF16),
            pltpu.VMEM((block, width), BF16),
            pltpu.VMEM((block, width), BF16),
            pltpu.VMEM((block, width), BF16),
        ],
        compiler_params=params(),
        cost_estimate=cost(2 * tokens * 2 * width * 2 * rows, 2 * tokens * width * 10),
        name="last",
    )(t_own, t_far, first_own, first_far, part_own, part_far, xa, xb, xc, xd, weight, vectors)


def swap(value, axis):
    return lax.ppermute(value, axis, [(0, 1), (1, 0)])


def across(value, count):
    return lax.ppermute(value, "dp", [(i, i ^ 1) for i in range(count)])


def shifted(value, steps, count):
    return lax.ppermute(value, "dp", [(i, (i + 2 * steps) % count) for i in range(count)])


def spread(piece, count):
    pieces = []
    for s in range(count // 2):
        here = shifted(piece, s, count) if s else piece
        pieces += [here, across(here, count)]
    return pieces


def collect(tiles, count):
    depth = count // 2
    kept = tiles[:, 0].astype(F32) + across(tiles[:, 1], count).astype(F32)
    total = kept[0]
    for s in range(1, depth):
        total = total + shifted(kept[s].astype(BF16), -s, count).astype(F32)
    return total


def rows_from_cores(mine, col):
    wide = mine.shape[-1] // 2
    other = swap(mine[..., wide:], "col")
    mine = mine[..., :wide]
    return jnp.where(col == 0, jnp.concatenate([mine, other], 0), jnp.concatenate([other, mine], 0))


def part_of(value, index, size):
    return lax.dynamic_slice_in_dim(value, index * size, size, 0)


def body(
    residual, attend_norm_gain, attend_norm_bias, expand_norm_gain, expand_norm_bias,
    attend_weight, attend_bias, output_weight, output_bias, expand_weight, expand_bias,
    shrink_weight, shrink_bias, cotangent,
):
    count = lax.axis_size("dp")
    depth = count // 2
    row, col, dp = lax.axis_index("row"), lax.axis_index("col"), lax.axis_index("dp")
    place_z, place_x = dp // 2, dp % 2
    micros, tokens, wide = residual.shape
    length = 2 * tokens
    heads = attend_weight.shape[1] // 2
    head_part, out_part = attend_weight.shape[2], output_weight.shape[1]
    hid = expand_weight.shape[1] // 2
    order = (((place_z - jnp.arange(depth)) % depth)[:, None] * 2 + (place_x ^ jnp.arange(2))[None]).reshape(-1)

    xs = [[residual[m]] for m in range(micros)]
    cs = [[cotangent[m]] for m in range(micros)]
    for group in (xs, cs):
        for entry in group:
            entry.append(swap(entry[0], "row"))
    for group in (xs, cs):
        for entry in group:
            entry += [swap(entry[0], "col"), swap(entry[1], "col")]

    by_rows = (
        attend_weight.transpose(1, 2, 0).reshape(2, heads * head_part, wide),
        output_weight.reshape(2, heads * out_part, wide),
        expand_weight.T.reshape(2, hid, wide),
        shrink_weight.reshape(2, hid, wide),
    )
    first_rows = by_rows[0]
    rest_rows = jnp.concatenate(by_rows[1:], axis=1)

    def piece_of(rows):
        mine = lax.dynamic_index_in_dim(rows, col, 0, keepdims=False)
        theirs = lax.dynamic_index_in_dim(rows, 1 - col, 0, keepdims=False)
        return jnp.concatenate([mine, swap(theirs, "col")], axis=1)

    width = 2 * wide
    attend_all = jnp.stack(spread(piece_of(first_rows), count))
    wq = attend_all[order].reshape(count, heads, head_part, width).transpose(1, 0, 2, 3)
    wq = wq.reshape(heads * 3 * HS, width)
    rest = spread(piece_of(rest_rows), count)
    lo = heads * out_part
    wo = jnp.stack([piece[:lo] for piece in rest])[order]
    wo = wo.reshape(count, heads, out_part, width).transpose(1, 0, 2, 3).reshape(heads * HS, width)
    w1 = jnp.concatenate([piece[lo : lo + hid] for piece in rest])
    w2 = jnp.concatenate([piece[lo + hid :] for piece in rest])

    vectors = jnp.stack([attend_norm_gain, attend_norm_bias, expand_norm_gain, expand_norm_bias])
    vectors = jnp.concatenate([jnp.roll(vectors, -col * wide, axis=1), jnp.zeros((4, width), F32)])
    head_begin = row * 2 * heads + col * heads
    bias_q = lax.dynamic_slice_in_dim(attend_bias, head_begin, heads, 0).reshape(-1, 1)
    bias_1 = expand_bias.reshape(count, 4, hid)
    bias_1 = lax.dynamic_index_in_dim(bias_1, row * 2 + col, 1, keepdims=False)[order].reshape(1, -1)
    out_bias = part_of(output_bias + shrink_bias, col, wide)

    powers = 10000.0 ** (-np.arange(HALF) * (2.0 / ROT))
    angles = powers[:, None] * np.arange(length)[None, :]
    cosine, sine = jnp.asarray(np.cos(angles), F32), jnp.asarray(np.sin(angles), F32)
    tables = [
        (lax.dynamic_slice_in_dim(cosine, at * tokens, tokens, 1), lax.dynamic_slice_in_dim(sine, at * tokens, tokens, 1))
        for at in (row, 1 - row)
    ]
    where = row.astype(jnp.int32).reshape(1)

    outputs, input_grads, vector_grads = [], [], []
    tile_grads, dq_grads = [], []
    saved = []
    for m in range(micros):
        xa, xb, xc, xd = xs[m]
        first_own, second_own, own = project(xa, xc, wq, bias_q, vectors, *tables[0])
        first_far, second_far, far = project(xb, xd, wq, bias_q, vectors, *tables[1])
        att_own, att_far, logsum = attend(where, own, far)
        saved.append((first_own, first_far, second_own, second_far, own, far, att_own, att_far, logsum))
    middles = []
    for m in range(micros):
        first_own, first_far, second_own, second_far, own, far, att_own, att_far, logsum = saved[m]
        ca, cb, cc, cd = cs[m]
        middles.append(middle(second_own, second_far, ca, cb, cc, cd, att_own, att_far, w1, w2, wo, bias_1))
        near, other = middles[m][:2]
        crossed = swap(other, "col")
        moved = swap((near[0].astype(F32) + crossed[0].astype(F32)).astype(BF16), "row")
        outputs.append(
            (
                xs[m][0].astype(F32) + near[1].astype(F32) + crossed[1].astype(F32) + moved.astype(F32) + out_bias
            ).astype(BF16)
        )
    tile_grads = [sum(middles[m][6 + i] for m in range(micros)) for i in range(3)]
    dw1, dw2, dwo = tile_grads
    dwo = dwo.reshape(heads, count, out_part, width).transpose(1, 0, 2, 3)[order].reshape(count, -1, width)
    tiles = jnp.concatenate(
        [dwo.astype(BF16), dw1.astype(BF16).reshape(count, hid, width), dw2.astype(BF16).reshape(count, hid, width)], axis=1
    )
    rest_sum = collect(tiles.reshape(depth, 2, -1, width), count)
    for m in range(micros):
        first_own, first_far, second_own, second_far, own, far, att_own, att_far, logsum = saved[m]
        xa, xb, xc, xd = xs[m]
        heads_own, heads_far, part_own, part_far = middles[m][2:6]
        t_own, t_far, bias_grad = attend_back(
            where, own, far, heads_own, heads_far, att_own, att_far, logsum, cosine, sine
        )
        near, other, sums, dweight, dvec = last(
            t_own, t_far, first_own, first_far, part_own, part_far, xa, xb, xc, xd, wq, vectors
        )
        dq_grads.append(dweight)
        vector_grads.append((dvec, bias_grad, middles[m][9]))
        crossed = swap(other, "col")
        moved = swap((near[0].astype(F32) + crossed[0].astype(F32)).astype(BF16), "row")
        sums = sums[:, :, :2].transpose(0, 2, 1)
        sums = sums + swap(sums, "col")
        sums = sums[1] + swap(sums[0], "row")
        grad = near[1].astype(F32) + crossed[1].astype(F32) + moved.astype(F32)
        near_x, far_x = xa.astype(F32), xc.astype(F32)
        center = (jnp.sum(near_x, 1) + jnp.sum(far_x, 1)) / width
        spread_x = (jnp.sum(near_x * near_x, 1) + jnp.sum(far_x * far_x, 1)) / width - center * center
        inv = lax.rsqrt(spread_x + EPSILON)[:, None]
        normed = (near_x - center[:, None]) * inv
        input_grads.append(
            cs[m][0].astype(F32) + inv * (grad - sums[0][:, None] / width - normed * sums[1][:, None] / width)
        )
    dq = sum(dq_grads).reshape(heads, count, head_part, width).transpose(1, 0, 2, 3)[order]
    dq_sum = collect(dq.astype(BF16).reshape(depth, 2, -1, width), count)

    attend_weight_grad = rows_from_cores(dq_sum.reshape(heads, head_part, width), col).transpose(2, 0, 1)
    output_weight_grad = rows_from_cores(rest_sum[:lo].reshape(heads, out_part, width), col)
    expand_weight_grad = rows_from_cores(rest_sum[lo : lo + hid], col).T
    shrink_weight_grad = rows_from_cores(rest_sum[lo + hid :], col)

    dvec, dbq, db1 = (sum(v[i] for v in vector_grads) for i in range(3))
    dvec = jnp.roll(dvec[:4], col * wide, axis=1)
    dout = jnp.sum(cotangent.astype(F32), axis=(0, 1))
    dout = lax.dynamic_update_slice_in_dim(jnp.zeros((width,), F32), dout, col * wide, 0)
    dbq = lax.dynamic_update_slice_in_dim(jnp.zeros(attend_bias.shape, F32), dbq.reshape(heads, -1), head_begin, 0)
    db1 = db1.reshape(count, 1, hid)[order]
    db1 = lax.dynamic_update_slice_in_dim(jnp.zeros((count, 4, hid), F32), db1, row * 2 + col, 1).reshape(-1)
    dvec, dout, dbq, db1 = lax.psum((dvec, dout, dbq, db1), ("dp", "row", "col"))
    return (
        jnp.stack(outputs), jnp.stack(input_grads), dvec[0], dvec[1], dvec[2], dvec[3],
        attend_weight_grad, dbq, output_weight_grad, dout, expand_weight_grad, db1, shrink_weight_grad, dout,
    )


def solution(mesh):
    tokens = P(None, ("dp", "row"), "col")
    weights = (P("col", "row", "dp"), P("row", "dp", "col"), P("col", ("dp", "row")), P(("dp", "row"), "col"))
    one = P()
    in_specs = (tokens, one, one, one, one, weights[0], one, weights[1], one, weights[2], one, weights[3], one, tokens)
    out_specs = (tokens, tokens, one, one, one, one, weights[0], one, weights[1], one, weights[2], one, weights[3], one)
    return jax.shard_map(body, mesh=mesh, in_specs=in_specs, out_specs=out_specs, check_vma=False)
```

time: 2410 us -> 631 us (0.26)
  waiting for transfers between devices: 1090 us -> 160 us
  matrix products: 636 us -> 0 us
  other arithmetic: 322 us -> 46.8 us
  Pallas kernels: 0 us -> 268 us
  local copies, waits for them, and re-layouts: 181 us -> 46.2 us
  blocking collectives: 117 us -> 41.7 us
  starting transfers between devices: 3.87 us -> 58.8 us
  loops' own time: 37.3 us -> 0 us
    dot_general x80 -> x0, matrix products: 636 us -> none  [the longest x16 111 us: causal_scores(): jnp.einsum('qhe,khe->hqk', query_block, keys_all, preferred_element_type=...]
    reduce_scatter x18 -> x0, waiting for transfers between devices: 537 us -> none  [the longest x2 138 us: reduce_tiles(): lax.psum_scatter(third_tile.astype(jnp.bfloat16), 'dp', scatter_dimension...]
    all_gather x20 -> x0, waiting for transfers between devices: 363 us -> none  [the longest x2 106 us: gather_tiles(): lax.all_gather(expand_weight, 'dp', axis=1, tiled=True)]
    pallas_call x0 -> x12, Pallas kernels: none -> 268 us  [the longest x2 93.8 us: middle(): pl.pallas_call(partial(middle_kernel, chunk=min(chunk, hidden)), grid=(2,...]
    while x46 -> x0, waiting for transfers between devices: 190 us -> none
    ppermute x0 -> x52, waiting for transfers between devices: none -> 160 us  [the longest x12 74.3 us: shifted(): lax.ppermute(value, 'dp', [(i, (i + 2 * steps) % count) for i in range(co...]
    convert_element_type x14 -> x6, other arithmetic: 125 us -> 9.08 us  [the longest x1 4.34 us: body(): dw2.astype(BF16).reshape(count, hid, width)]
    dynamic_update_slice x23 -> x3, local copies, waits for them, and re-layouts: 98.1 us -> 0.23 us  [the longest x1 0.18 us: body(): lax.dynamic_update_slice_in_dim(jnp.zeros((width,), F32), dout, col * wid...]
  transfers between devices with their start and end apart: 42 -> 52, of which waited for: 28 -> 17; matrix products, arithmetic and copies ran while one was open for 46% -> 14% of each run, Pallas kernels for 0% -> 43%
where the time goes in v1:
time: 631 us; the launch traced here: 623 us
  Pallas kernels  268 us (42%)
  waiting for transfers between devices  160 us (25%)
  starting transfers between devices  58.8 us (9%)
  other arithmetic  46.8 us (7%)
  local copies, waits for them, and re-layouts  46.2 us (7%)
  blocking collectives  41.7 us (7%)
    pallas_call x2, Pallas kernels, middle(): pl.pallas_call(partial(middle_kernel, chunk=min(chunk, hidden)), grid=(2,...  93.8 us
    ppermute x12, waiting for transfers between devices, shifted(): lax.ppermute(value, 'dp', [(i, (i + 2 * steps) % count) for i in range(co...  74.3 us
    pallas_call x2, Pallas kernels, attend_back(): pl.pallas_call(partial(attend_back_kernel, step=min(step, length)), grid=...  59.9 us
    ppermute x30, waiting for transfers between devices, swap(): return lax.ppermute(value, axis, [(0, 1), (1, 0)])  57.6 us
    pallas_call x2, Pallas kernels, attend(): pl.pallas_call(partial(attend_kernel, step=min(step, length)), grid=(head...  46.2 us
    psum x1, blocking collectives, body(): lax.psum((dvec, dout, dbq, db1), ('dp', 'row', 'col'))  41.7 us
    pallas_call x2, Pallas kernels, last(): pl.pallas_call(last_kernel, grid=(2, steps), in_specs=[cols_own, cols_far...  38.5 us
    pallas_call x4, Pallas kernels, project(): pl.pallas_call(project_kernel, grid=(tokens // block,), in_specs=[tile, t...  29.3 us
  transfers between devices with their start and end apart: 52, of which 17 were waited for; matrix products, arithmetic and copies ran while one was open for 14% of the time, Pallas kernels for 43%

profile of v1, /device:TPU:0, one launch (start us, length us, event | category | flops | bytes accessed | tf_op | source)
XLA Modules:
  0.0 623.3 jit_solution(11402311961904897815)
XLA Ops:
  0.7 3.0 slice_bitcast_fusion.10
  3.8 3.0 collective-permute-start.9
  15.1 2.7 collective-permute-start.5
  23.2 5.4 collective-permute-done.3
  31.7 7.8 %collective-permute-start.16 = (bf16[288,1024]{1,0:T(8,128)(2,1)}, bf16[288,1024]{1,0:T(8,128)(2,1)}, u32[]{:S(2)}, u32[]{:S(2)}) collective-permute-start(bf16[288,1024]{1,0:T(8,128)(2,1)} %pad_maximum_fusion.3), channel_id=1, source_target_pairs={{0,8},{4,12},{8,16},{12,20},{16,24},{20,28},{24,0},{28,4},{1,9},{5... | collective-permute-start | bytes 1769480 | tf_op jit(solution)/shard_map/ppermute | solution.py:479
  43.2 4.1 collective-permute-done.6
  48.7 13.9 %collective-permute-done.8 = bf16[96,1024]{1,0:T(8,128)(2,1)S(1)} collective-permute-done((bf16[96,1024]{1,0:T(8,128)(2,1)S(1)}, bf16[96,1024]{1,0:T(8,128)(2,1)S(1)}, u32[]{:S(2)}, u32[]{:S(2)}) %collective-permute-start.8) | collective-permute-done | bytes 196640 | tf_op jit(solution)/shard_map/ppermute | solution.py:475
  63.4 2.1 gather_fusion
  68.1 5.6 collective-permute-start.18
  74.5 1.7 slice_dynamic-update-slice_fusion.6
  76.3 1.8 slice_dynamic-update-slice_fusion.5
  79.7 7.3 %project.6 = (bf16[1024,1024]{1,0:T(8,128)(2,1)}, bf16[1024,1024]{1,0:T(8,128)(2,1)}, bf16[768,1024]{1,0:T(8,128)(2,1)}) custom-call(bf16[1024,512]{1,0:T(8,128)(2,1)} %get-tuple-element.201.xa, bf16[1024,512]{1,0:T(8,128)(2,1)} %copy-done.16, bf16[768,1024]{1,0:T(8,128)(2,1)} %bitcast.263, f32[768,1]{1,0:T(8,128)} %reshape.327.bias, ...), custom_call_target="tpu_custom_call" | custom-call | flops 2415919104 | bytes 6291456 | tf_op jit(solution)/shard_map/project/pallas_call | solution.py:80
  87.0 2.2 fusion.1
  90.8 2.2 fusion
  93.0 7.3 %project.4 = (bf16[1024,1024]{1,0:T(8,128)(2,1)}, bf16[1024,1024]{1,0:T(8,128)(2,1)}, bf16[768,1024]{1,0:T(8,128)(2,1)}) custom-call(bf16[1024,512]{1,0:T(8,128)(2,1)} %get-tuple-element.200.xa, bf16[1024,512]{1,0:T(8,128)(2,1)} %collective-permute-done.xc, bf16[768,1024]{1,0:T(8,128)(2,1)} %bitcast.264, f32[768,1]{1,0:T(8,128)} %reshape.327.bias, ...), custom_call_target="tpu_custom_call" | custom-call | flops 2415919104 | bytes 6291456 | tf_op jit(solution)/shard_map/project/pallas_call | solution.py:80
  100.3 3.4 collective-permute-start.20
  106.0 10.8 %collective-permute-done.20 = bf16[288,1024]{1,0:T(8,128)(2,1)S(1)} collective-permute-done((bf16[288,1024]{1,0:T(8,128)(2,1)}, bf16[288,1024]{1,0:T(8,128)(2,1)S(1)}, u32[]{:S(2)}, u32[]{:S(2)}) %collective-permute-start.20) | collective-permute-done | bytes 589856 | tf_op jit(solution)/shard_map/ppermute | solution.py:479
  122.5 9.9 %collective-permute-done.21 = bf16[288,1024]{1,0:T(8,128)(2,1)S(1)} collective-permute-done((bf16[288,1024]{1,0:T(8,128)(2,1)S(1)}, bf16[288,1024]{1,0:T(8,128)(2,1)S(1)}, u32[]{:S(2)}, u32[]{:S(2)}) %collective-permute-start.21) | collective-permute-done | bytes 589856 | tf_op jit(solution)/shard_map/ppermute | solution.py:475
  136.4 4.6 collective-permute-done.27.cb
  141.6 7.4 %project.5 = (bf16[1024,1024]{1,0:T(8,128)(2,1)}, bf16[1024,1024]{1,0:T(8,128)(2,1)}, bf16[768,1024]{1,0:T(8,128)(2,1)}) custom-call(bf16[1024,512]{1,0:T(8,128)(2,1)} %collective-permute-done.9.xa.xb, bf16[1024,512]{1,0:T(8,128)(2,1)} %collective-permute-done.10.xc.xd, bf16[768,1024]{1,0:T(8,128)(2,1)} %bitcast.265, f32[768,1]{1,0:T(8,128)} %reshape.327.bias, ...), custom_call_target="tpu_custom_call" | custom-call | flops 2415919104 | bytes 6291456 | tf_op jit(solution)/shard_map/project/pallas_call | solution.py:80
  149.0 23.0 %attend.2 = (bf16[256,1024]{1,0:T(8,128)(2,1)}, bf16[256,1024]{1,0:T(8,128)(2,1)}, f32[4,1,2048]{2,1,0:T(1,128)}) custom-call(s32[1]{0:T(128)} %bitcast.23.row, bf16[768,1024]{1,0:T(8,128)(2,1)} %get-tuple-element.71.own, bf16[768,1024]{1,0:T(8,128)(2,1)} %get-tuple-element.72.far), custom_call_target="tpu_custom_call" | custom-call | flops 8589934592 | bytes 6291456 | tf_op jit(solution)/shard_map/attend/pallas_call | solution.py:145
  172.1 46.9 %middle.2 = (bf16[2,1024,512]{2,1,0:T(8,128)(2,1)}, bf16[2,1024,512]{2,1,0:T(8,128)(2,1)}, bf16[256,1024]{1,0:T(8,128)(2,1)}, bf16[256,1024]{1,0:T(8,128)(2,1)},...) custom-call(bf16[1024,1024]{1,0:T(8,128)(2,1)} %get-tuple-element.69, ...), custom_call_target="tpu_custom_call" | custom-call | flops 28991029248 | bytes 20971520 | tf_op jit(solution)/shard_map/middle/pallas_call | solution.py:340
  219.0 30.1 %attend_back.2 = (bf16[768,1024]{1,0:T(8,128)(2,1)}, bf16[768,1024]{1,0:T(8,128)(2,1)}, f32[768,1]{1,0:T(8,128)}) custom-call(s32[1]{0:T(128)} %bitcast.23.row, bf16[768,1024]{1,0:T(8,128)(2,1)} %get-tuple-element.71.own, bf16[768,1024]{1,0:T(8,128)(2,1)} %get-tuple-element.72.far, bf16[256,1024]{1,0:T(8,128)(2,1)} %get-tuple-element.85.grad_own, ...), custom_call_target="tpu_custom_call" | custom-call | flops 21474836480 | bytes 12582912 | tf_op jit(solution)/shard_map/attend_back/pallas_call | solution.py:227
  249.1 19.2 %last.2 = (bf16[2,1024,512]{2,1,0:T(8,128)(2,1)}, bf16[2,1024,512]{2,1,0:T(8,128)(2,1)}, f32[2,1024,128]{2,1,0:T(8,128)}, f32[768,1024]{1,0:T(8,128)}, f32[8,1024]{1,0:T(8,128)}) custom-call(bf16[768,1024]{1,0:T(8,128)(2,1)} %get-tuple-element.88.t_own, bf16[768,1024]{1,0:T(8,128)(2,1)} %get-tuple-element.89.t_far, ...), custom_call_target="tpu_custom_call" | custom-call | flops 6442450944 | bytes 20971520 | tf_op jit(solution)/shard_map/last/pallas_call | solution.py:439
  270.5 7.3 %project.7 = (bf16[1024,1024]{1,0:T(8,128)(2,1)}, bf16[1024,1024]{1,0:T(8,128)(2,1)}, bf16[768,1024]{1,0:T(8,128)(2,1)}) custom-call(bf16[1024,512]{1,0:T(8,128)(2,1)} %collective-permute-done.25.xa.xb, bf16[1024,512]{1,0:T(8,128)(2,1)} %collective-permute-done.26.xc.xd, bf16[768,1024]{1,0:T(8,128)(2,1)} %bitcast.267, f32[768,1]{1,0:T(8,128)} %reshape.327.bias, ...), custom_call_target="tpu_custom_call" | custom-call | flops 2415919104 | bytes 6291456 | tf_op jit(solution)/shard_map/project/pallas_call | solution.py:80
  277.8 23.2 %attend.3 = (bf16[256,1024]{1,0:T(8,128)(2,1)}, bf16[256,1024]{1,0:T(8,128)(2,1)}, f32[4,1,2048]{2,1,0:T(1,128)}) custom-call(s32[1]{0:T(128)} %bitcast.23.row, bf16[768,1024]{1,0:T(8,128)(2,1)} %get-tuple-element.79.own, bf16[768,1024]{1,0:T(8,128)(2,1)} %get-tuple-element.80.far), custom_call_target="tpu_custom_call" | custom-call | flops 8589934592 | bytes 6291456 | tf_op jit(solution)/shard_map/attend/pallas_call | solution.py:145
  301.0 46.9 %middle.3 = (bf16[2,1024,512]{2,1,0:T(8,128)(2,1)}, bf16[2,1024,512]{2,1,0:T(8,128)(2,1)}, bf16[256,1024]{1,0:T(8,128)(2,1)}, bf16[256,1024]{1,0:T(8,128)(2,1)},...) custom-call(bf16[1024,1024]{1,0:T(8,128)(2,1)} %get-tuple-element.77, ...), custom_call_target="tpu_custom_call" | custom-call | flops 28991029248 | bytes 20971520 | tf_op jit(solution)/shard_map/middle/pallas_call | solution.py:340
  351.9 29.8 %attend_back.3 = (bf16[768,1024]{1,0:T(8,128)(2,1)}, bf16[768,1024]{1,0:T(8,128)(2,1)}, f32[768,1]{1,0:T(8,128)}) custom-call(s32[1]{0:T(128)} %bitcast.23.row, bf16[768,1024]{1,0:T(8,128)(2,1)} %get-tuple-element.79.own, bf16[768,1024]{1,0:T(8,128)(2,1)} %get-tuple-element.80.far, bf16[256,1024]{1,0:T(8,128)(2,1)} %get-tuple-element.97.grad_own, ...), custom_call_target="tpu_custom_call" | custom-call | flops 21474836480 | bytes 12582912 | tf_op jit(solution)/shard_map/attend_back/pallas_call | solution.py:227
  383.0 19.3 %last.3 = (bf16[2,1024,512]{2,1,0:T(8,128)(2,1)}, bf16[2,1024,512]{2,1,0:T(8,128)(2,1)}, f32[2,1024,128]{2,1,0:T(8,128)}, f32[768,1024]{1,0:T(8,128)}, f32[8,1024]{1,0:T(8,128)}) custom-call(bf16[768,1024]{1,0:T(8,128)(2,1)} %get-tuple-element.100.t_own, bf16[768,1024]{1,0:T(8,128)(2,1)} %get-tuple-element.101.t_far, ...), custom_call_target="tpu_custom_call" | custom-call | flops 6442450944 | bytes 20971520 | tf_op jit(solution)/shard_map/last/pallas_call | solution.py:439
  402.3 2.4 add.340
  405.6 41.7 %all-reduce.1 = (f32[4,1024]{1,0:T(4,128)S(1)}, f32[16,192]{1,0:T(8,128)}, f32[1024]{0:T(1024)S(1)}, f32[4096]{0:T(1024)}) all-reduce(f32[4,1024]{1,0:T(4,128)S(1)} %fusion.58, f32[16,192]{1,0:T(8,128)S(1)} %constant_dynamic-update-slice_fusion.1, ...), channel_id=1, replica_groups=mesh['dp'=8,'row'=2,'col'=2] {'dp','row','col'}, use_global_device_ids=true, to_apply=%region_8.10 | all-reduce | flops 12288 | bytes 98304 | tf_op jit(solution)/shard_map/psum | solution.py:647
  447.4 2.3 collective-permute-start.40
  450.7 4.3 add_convert_fusion
  466.1 2.1 collective-permute-start.35
  469.5 1.6 fusion.70
  472.8 1.7 collective-permute-start.41
  474.5 6.2 collective-permute-done.35
  480.7 2.1 collective-permute-start.43
  484.9 5.5 collective-permute-done.43
  490.4 7.0 %collective-permute-done.42 = bf16[96,1024]{1,0:T(8,128)(2,1)S(1)} collective-permute-done((bf16[96,1024]{1,0:T(8,128)(2,1)S(1)}, bf16[96,1024]{1,0:T(8,128)(2,1)S(1)}, u32[]{:S(2)}, u32[]{:S(2)}) %collective-permute-start.42) | collective-permute-done | bytes 196640 | tf_op jit(solution)/shard_map/ppermute | solution.py:479
  499.0 12.3 %collective-permute-done.39 = f32[2,1024]{0,1:T(8,128)S(1)} collective-permute-done((f32[2,1024]{0,1:T(8,128)S(1)}, f32[2,1024]{0,1:T(8,128)S(1)}, u32[]{:S(2)}, u32[]{:S(2)}) %collective-permute-start.39) | collective-permute-done | bytes 8224 | tf_op jit(solution)/shard_map/ppermute | solution.py:471
  519.2 2.9 fusion.72
  526.9 24.5 %collective-permute-done.46 = bf16[288,1024]{1,0:T(8,128)(2,1)S(1)} collective-permute-done((bf16[288,1024]{1,0:T(8,128)(2,1)S(1)}, bf16[288,1024]{1,0:T(8,128)(2,1)S(1)}, u32[]{:S(2)}, u32[]{:S(2)}) %collective-permute-start.46) | collective-permute-done | bytes 589856 | tf_op jit(solution)/shard_map/ppermute | solution.py:479
  553.4 20.7 %collective-permute-done.47 = bf16[288,1024]{1,0:T(8,128)(2,1)S(1)} collective-permute-done((bf16[288,1024]{1,0:T(8,128)(2,1)S(1)}, bf16[288,1024]{1,0:T(8,128)(2,1)S(1)}, u32[]{:S(2)}, u32[]{:S(2)}) %collective-permute-start.47) | collective-permute-done | bytes 589856 | tf_op jit(solution)/shard_map/ppermute | solution.py:479
  577.2 31.9 %collective-permute-done.31 = bf16[1024,512]{1,0:T(8,128)(2,1)S(1)} collective-permute-done((bf16[1024,512]{1,0:T(8,128)(2,1)S(1)}, bf16[1024,512]{1,0:T(8,128)(2,1)S(1)}, u32[]{:S(2)}, u32[]{:S(2)}) %collective-permute-start.31) | collective-permute-done | bytes 1048608 | tf_op jit(solution)/shard_map/ppermute | solution.py:471
  609.1 3.4 fusion.6
  612.5 3.8 fusion.13
  616.4 2.5 pad_maximum_fusion.1
  (286 shorter events, 90.4 us)
Async XLA Ops:
  3.8 114.6 %collective-permute-start.9 = (bf16[1024,512]{1,0:T(8,128)(2,1)}, bf16[1024,512]{1,0:T(8,128)(2,1)}, u32[]{:S(2)}, u32[]{:S(2)}) collective-permute-start(bf16[1024,512]{1,0:T(8,128)(2,1)} %get-tuple-element.200.xa), channel_id=1, source_target_pairs={{0,2},{2,0},{1,3},{3,1},{4,6},{6,4},{5,7},{7,5},{8,10},{10,8},{9,1... | collective-permute-start | bytes 3145736 | tf_op jit(solution)/shard_map/ppermute | solution.py:471
  6.7 82.5 %collective-permute-start = (bf16[1024,512]{1,0:T(8,128)(2,1)}, bf16[1024,512]{1,0:T(8,128)(2,1)}, u32[]{:S(2)}, u32[]{:S(2)}) collective-permute-start(bf16[1024,512]{1,0:T(8,128)(2,1)} %get-tuple-element.200.xa), channel_id=1, source_target_pairs={{0,1},{1,0},{2,3},{3,2},{4,5},{5,4},{6,7},{7,6},{8,9},{9,8},{10,11... | collective-permute-start | bytes 3145736 | tf_op jit(solution)/shard_map/ppermute | solution.py:471
  6.7 8.3 %collective-permute-start.1 = (bf16[96,512]{1,0:T(8,128)(2,1)S(1)}, bf16[96,512]{1,0:T(8,128)(2,1)S(1)}, u32[]{:S(2)}, u32[]{:S(2)}) collective-permute-start(bf16[96,512]{1,0:T(8,128)(2,1)S(1)} %get-tuple-element.230), channel_id=1, source_target_pairs={{0,1},{1,0},{2,3},{3,2},{4,5},{5,4},{6,7},{7,6},{8,9},{9,8},{10,11... | collective-permute-start | bytes 294920 | tf_op jit(solution)/shard_map/ppermute | solution.py:471
  7.6 12.4 %collective-permute-start.14 = (bf16[288,512]{1,0:T(8,128)(2,1)S(1)}, bf16[288,512]{1,0:T(8,128)(2,1)S(1)}, u32[]{:S(2)}, u32[]{:S(2)}) collective-permute-start(bf16[288,512]{1,0:T(8,128)(2,1)S(1)} %get-tuple-element.225), channel_id=1, source_target_pairs={{0,1},{1,0},{2,3},{3,2},{4,5},{5,4},{6,7},{7,6},{8,9},{9,8},{10,11... | collective-permute-start | bytes 884744 | tf_op jit(solution)/shard_map/ppermute | solution.py:471
  15.1 16.6 %collective-permute-start.5 = (bf16[96,1024]{1,0:T(8,128)(2,1)S(1)}, bf16[96,1024]{1,0:T(8,128)(2,1)S(1)}, u32[]{:S(2)}, u32[]{:S(2)}) collective-permute-start(bf16[96,1024]{1,0:T(8,128)(2,1)S(1)} %pad_maximum_fusion.5), channel_id=1, source_target_pairs={{0,16},{4,20},{8,24},{12,28},{16,0},{20,4},{24,8},{28,12},{1,17},{... | collective-permute-start | bytes 589832 | tf_op jit(solution)/shard_map/ppermute | solution.py:479
  17.7 10.9 %collective-permute-start.3 = (bf16[96,1024]{1,0:T(8,128)(2,1)S(1)}, bf16[96,1024]{1,0:T(8,128)(2,1)S(1)}, u32[]{:S(2)}, u32[]{:S(2)}) collective-permute-start(bf16[96,1024]{1,0:T(8,128)(2,1)S(1)} %pad_maximum_fusion.5), channel_id=1, source_target_pairs={{0,8},{4,12},{8,16},{12,20},{16,24},{20,28},{24,0},{28,4},{1,9},{5... | collective-permute-start | bytes 589832 | tf_op jit(solution)/shard_map/ppermute | solution.py:479
  20.0 8.6 %collective-permute-start.2 = (bf16[96,1024]{1,0:T(8,128)(2,1)S(1)}, bf16[96,1024]{1,0:T(8,128)(2,1)S(1)}, u32[]{:S(2)}, u32[]{:S(2)}) collective-permute-start(bf16[96,1024]{1,0:T(8,128)(2,1)S(1)} %pad_maximum_fusion.5), channel_id=1, source_target_pairs={{0,4},{4,0},{8,12},{12,8},{16,20},{20,16},{24,28},{28,24},{1,5},{5... | collective-permute-start | bytes 589832 | tf_op jit(solution)/shard_map/ppermute | solution.py:475
  28.6 13.1 %collective-permute-start.7 = (bf16[96,1024]{1,0:T(8,128)(2,1)S(1)}, bf16[96,1024]{1,0:T(8,128)(2,1)S(1)}, u32[]{:S(2)}, u32[]{:S(2)}) collective-permute-start(bf16[96,1024]{1,0:T(8,128)(2,1)S(1)} %pad_maximum_fusion.5), channel_id=1, source_target_pairs={{0,24},{4,28},{8,0},{12,4},{16,8},{20,12},{24,16},{28,20},{1,25},{... | collective-permute-start | bytes 589832 | tf_op jit(solution)/shard_map/ppermute | solution.py:479
  28.6 10.9 %collective-permute-start.4 = (bf16[96,1024]{1,0:T(8,128)(2,1)S(1)}, bf16[96,1024]{1,0:T(8,128)(2,1)S(1)}, u32[]{:S(2)}, u32[]{:S(2)}) collective-permute-start(bf16[96,1024]{1,0:T(8,128)(2,1)S(1)} %collective-permute-done.3), channel_id=1, source_target_pairs={{0,4},{4,0},{8,12},{12,8},{16,20},{20,16},{24,28},{28,24},{1,5},{5... | collective-permute-start | bytes 589832 | tf_op jit(solution)/shard_map/ppermute | solution.py:475
  31.7 36.4 %collective-permute-start.16 = (bf16[288,1024]{1,0:T(8,128)(2,1)}, bf16[288,1024]{1,0:T(8,128)(2,1)}, u32[]{:S(2)}, u32[]{:S(2)}) collective-permute-start(bf16[288,1024]{1,0:T(8,128)(2,1)} %pad_maximum_fusion.3), channel_id=1, source_target_pairs={{0,8},{4,12},{8,16},{12,20},{16,24},{20,28},{24,0},{28,4},{1,9},{5... | collective-permute-start | bytes 1769480 | tf_op jit(solution)/shard_map/ppermute | solution.py:479
  41.7 25.0 %collective-permute-start.15 = (bf16[288,1024]{1,0:T(8,128)(2,1)}, bf16[288,1024]{1,0:T(8,128)(2,1)}, u32[]{:S(2)}, u32[]{:S(2)}) collective-permute-start(bf16[288,1024]{1,0:T(8,128)(2,1)} %pad_maximum_fusion.3), channel_id=1, source_target_pairs={{0,4},{4,0},{8,12},{12,8},{16,20},{20,16},{24,28},{28,24},{1,5},{5... | collective-permute-start | bytes 1769480 | tf_op jit(solution)/shard_map/ppermute | solution.py:475
  47.3 15.3 %collective-permute-start.8 = (bf16[96,1024]{1,0:T(8,128)(2,1)S(1)}, bf16[96,1024]{1,0:T(8,128)(2,1)S(1)}, u32[]{:S(2)}, u32[]{:S(2)}) collective-permute-start(bf16[96,1024]{1,0:T(8,128)(2,1)S(1)} %collective-permute-done.7), channel_id=1, source_target_pairs={{0,4},{4,0},{8,12},{12,8},{16,20},{20,16},{24,28},{28,24},{1,5},{5... | collective-permute-start | bytes 589832 | tf_op jit(solution)/shard_map/ppermute | solution.py:475
  62.7 15.4 %collective-permute-start.24 = (bf16[1024,512]{1,0:T(8,128)(2,1)}, bf16[1024,512]{1,0:T(8,128)(2,1)S(1)}, u32[]{:S(2)}, u32[]{:S(2)}) collective-permute-start(bf16[1024,512]{1,0:T(8,128)(2,1)} %get-tuple-element.201.xa), channel_id=1, source_target_pairs={{0,1},{1,0},{2,3},{3,2},{4,5},{5,4},{6,7},{7,6},{8,9},{9,8},{10,11... | collective-permute-start | bytes 3145736 | tf_op jit(solution)/shard_map/ppermute | solution.py:471
  66.7 69.2 %collective-permute-start.25 = (bf16[1024,512]{1,0:T(8,128)(2,1)}, bf16[1024,512]{1,0:T(8,128)(2,1)}, u32[]{:S(2)}, u32[]{:S(2)}) collective-permute-start(bf16[1024,512]{1,0:T(8,128)(2,1)} %get-tuple-element.201.xa), channel_id=1, source_target_pairs={{0,2},{2,0},{1,3},{3,1},{4,6},{6,4},{5,7},{7,5},{8,10},{10,8},{9,1... | collective-permute-start | bytes 3145736 | tf_op jit(solution)/shard_map/ppermute | solution.py:471
  68.1 32.3 %collective-permute-start.18 = (bf16[288,1024]{1,0:T(8,128)(2,1)}, bf16[288,1024]{1,0:T(8,128)(2,1)S(1)}, u32[]{:S(2)}, u32[]{:S(2)}) collective-permute-start(bf16[288,1024]{1,0:T(8,128)(2,1)} %pad_maximum_fusion.3), channel_id=1, source_target_pairs={{0,16},{4,20},{8,24},{12,28},{16,0},{20,4},{24,8},{28,12},{1,17},{... | collective-permute-start | bytes 1769480 | tf_op jit(solution)/shard_map/ppermute | solution.py:479
  78.1 25.7 %collective-permute-start.17 = (bf16[288,1024]{1,0:T(8,128)(2,1)}, bf16[288,1024]{1,0:T(8,128)(2,1)S(1)}, u32[]{:S(2)}, u32[]{:S(2)}) collective-permute-start(bf16[288,1024]{1,0:T(8,128)(2,1)} %collective-permute-done.16), channel_id=1, source_target_pairs={{0,4},{4,0},{8,12},{12,8},{16,20},{20,16},{24,28},{28,24},{1,5},{5... | collective-permute-start | bytes 1769480 | tf_op jit(solution)/shard_map/ppermute | solution.py:475
  89.2 32.8 %collective-permute-start.11 = (bf16[1024,512]{1,0:T(8,128)(2,1)S(1)}, bf16[1024,512]{1,0:T(8,128)(2,1)}, u32[]{:S(2)}, u32[]{:S(2)}) collective-permute-start(bf16[1024,512]{1,0:T(8,128)(2,1)S(1)} %copy-done.19), channel_id=1, source_target_pairs={{0,2},{2,0},{1,3},{3,1},{4,6},{6,4},{5,7},{7,5},{8,10},{10,8},{9,1... | collective-permute-start | bytes 3145736 | tf_op jit(solution)/shard_map/ppermute | solution.py:471
  100.3 16.5 %collective-permute-start.20 = (bf16[288,1024]{1,0:T(8,128)(2,1)}, bf16[288,1024]{1,0:T(8,128)(2,1)S(1)}, u32[]{:S(2)}, u32[]{:S(2)}) collective-permute-start(bf16[288,1024]{1,0:T(8,128)(2,1)} %pad_maximum_fusion.3), channel_id=1, source_target_pairs={{0,24},{4,28},{8,0},{12,4},{16,8},{20,12},{24,16},{28,20},{1,25},{... | collective-permute-start | bytes 1769480 | tf_op jit(solution)/shard_map/ppermute | solution.py:479
  103.8 16.0 %collective-permute-start.19 = (bf16[288,1024]{1,0:T(8,128)(2,1)S(1)}, bf16[288,1024]{1,0:T(8,128)(2,1)S(1)}, u32[]{:S(2)}, u32[]{:S(2)}) collective-permute-start(bf16[288,1024]{1,0:T(8,128)(2,1)S(1)} %collective-permute-done.18), channel_id=1, source_target_pairs={{0,4},{4,0},{8,12},{12,8},{16,20},{20,16},{24,28},{28,24},{1,5},{5... | collective-permute-start | bytes 1769480 | tf_op jit(solution)/shard_map/ppermute | solution.py:475
  116.8 24.3 %collective-permute-start.27 = (bf16[1024,512]{1,0:T(8,128)(2,1)S(1)}, bf16[1024,512]{1,0:T(8,128)(2,1)}, u32[]{:S(2)}, u32[]{:S(2)}) collective-permute-start(bf16[1024,512]{1,0:T(8,128)(2,1)S(1)} %copy-done.18), channel_id=1, source_target_pairs={{0,2},{2,0},{1,3},{3,1},{4,6},{6,4},{5,7},{7,5},{8,10},{10,8},{9,1... | collective-permute-start | bytes 3145736 | tf_op jit(solution)/shard_map/ppermute | solution.py:471
  118.4 14.1 %collective-permute-start.21 = (bf16[288,1024]{1,0:T(8,128)(2,1)S(1)}, bf16[288,1024]{1,0:T(8,128)(2,1)S(1)}, u32[]{:S(2)}, u32[]{:S(2)}) collective-permute-start(bf16[288,1024]{1,0:T(8,128)(2,1)S(1)} %collective-permute-done.20), channel_id=1, source_target_pairs={{0,4},{4,0},{8,12},{12,8},{16,20},{20,16},{24,28},{28,24},{1,5},{5... | collective-permute-start | bytes 1769480 | tf_op jit(solution)/shard_map/ppermute | solution.py:475
  119.7 21.3 %collective-permute-start.10 = (bf16[1024,512]{1,0:T(8,128)(2,1)}, bf16[1024,512]{1,0:T(8,128)(2,1)}, u32[]{:S(2)}, u32[]{:S(2)}) collective-permute-start(bf16[1024,512]{1,0:T(8,128)(2,1)} %collective-permute-done.9.xa.xb), channel_id=1, source_target_pairs={{0,1},{1,0},{2,3},{3,2},{4,5},{5,4},{6,7},{7,6},{8,9},{9,8},{10,11... | collective-permute-start | bytes 3145736 | tf_op jit(solution)/shard_map/ppermute | solution.py:471
  122.0 50.0 %collective-permute-start.12 = (bf16[1024,512]{1,0:T(8,128)(2,1)S(1)}, bf16[1024,512]{1,0:T(8,128)(2,1)}, u32[]{:S(2)}, u32[]{:S(2)}) collective-permute-start(bf16[1024,512]{1,0:T(8,128)(2,1)S(1)} %copy-done.19), channel_id=1, source_target_pairs={{0,1},{1,0},{2,3},{3,2},{4,5},{5,4},{6,7},{7,6},{8,9},{9,8},{10,11... | collective-permute-start | bytes 3145736 | tf_op jit(solution)/shard_map/ppermute | solution.py:471
  132.4 39.6 %collective-permute-start.13 = (bf16[1024,512]{1,0:T(8,128)(2,1)}, bf16[1024,512]{1,0:T(8,128)(2,1)}, u32[]{:S(2)}, u32[]{:S(2)}) collective-permute-start(bf16[1024,512]{1,0:T(8,128)(2,1)} %collective-permute-done.11.cb), channel_id=1, source_target_pairs={{0,1},{1,0},{2,3},{3,2},{4,5},{5,4},{6,7},{7,6},{8,9},{9,8},{10,11... | collective-permute-start | bytes 3145736 | tf_op jit(solution)/shard_map/ppermute | solution.py:471
  135.9 165.0 %collective-permute-start.28 = (bf16[1024,512]{1,0:T(8,128)(2,1)S(1)}, bf16[1024,512]{1,0:T(8,128)(2,1)}, u32[]{:S(2)}, u32[]{:S(2)}) collective-permute-start(bf16[1024,512]{1,0:T(8,128)(2,1)S(1)} %copy-done.18), channel_id=1, source_target_pairs={{0,1},{1,0},{2,3},{3,2},{4,5},{5,4},{6,7},{7,6},{8,9},{9,8},{10,11... | collective-permute-start | bytes 3145736 | tf_op jit(solution)/shard_map/ppermute | solution.py:471
  141.1 129.4 %collective-permute-start.26 = (bf16[1024,512]{1,0:T(8,128)(2,1)}, bf16[1024,512]{1,0:T(8,128)(2,1)}, u32[]{:S(2)}, u32[]{:S(2)}) collective-permute-start(bf16[1024,512]{1,0:T(8,128)(2,1)} %collective-permute-done.25.xa.xb), channel_id=1, source_target_pairs={{0,1},{1,0},{2,3},{3,2},{4,5},{5,4},{6,7},{7,6},{8,9},{9,8},{10,11... | collective-permute-start | bytes 3145736 | tf_op jit(solution)/shard_map/ppermute | solution.py:471
  141.1 159.9 %collective-permute-start.29 = (bf16[1024,512]{1,0:T(8,128)(2,1)}, bf16[1024,512]{1,0:T(8,128)(2,1)}, u32[]{:S(2)}, u32[]{:S(2)}) collective-permute-start(bf16[1024,512]{1,0:T(8,128)(2,1)} %collective-permute-done.27.cb), channel_id=1, source_target_pairs={{0,1},{1,0},{2,3},{3,2},{4,5},{5,4},{6,7},{7,6},{8,9},{9,8},{10,11... | collective-permute-start | bytes 3145736 | tf_op jit(solution)/shard_map/ppermute | solution.py:471
  269.9 192.3 %collective-permute-start.34 = (f32[2,2,1024]{2,1,0:T(2,128)S(1)}, f32[2,2,1024]{2,1,0:T(2,128)S(1)}, u32[]{:S(2)}, u32[]{:S(2)}) collective-permute-start(f32[2,2,1024]{2,1,0:T(2,128)S(1)} %copy.58), channel_id=1, source_target_pairs={{0,1},{1,0},{2,3},{3,2},{4,5},{5,4},{6,7},{7,6},{8,9},{9,8},{10,11... | collective-permute-start | bytes 49160 | tf_op jit(solution)/shard_map/ppermute | solution.py:471
  269.9 244.7 %collective-permute-start.32 = (bf16[2,1024,512]{2,1,0:T(8,128)(2,1)}, bf16[2,1024,512]{2,1,0:T(8,128)(2,1)}, u32[]{:S(2)}, u32[]{:S(2)}) collective-permute-start(bf16[2,1024,512]{2,1,0:T(8,128)(2,1)} %get-tuple-element.95), channel_id=1, source_target_pairs={{0,1},{1,0},{2,3},{3,2},{4,5},{5,4},{6,7},{7,6},{8,9},{9,8},{10,11... | collective-permute-start | bytes 6291464 | tf_op jit(solution)/shard_map/ppermute | solution.py:471
  270.4 247.2 %collective-permute-start.22 = (bf16[2,1024,512]{2,1,0:T(8,128)(2,1)}, bf16[2,1024,512]{2,1,0:T(8,128)(2,1)}, u32[]{:S(2)}, u32[]{:S(2)}) collective-permute-start(bf16[2,1024,512]{2,1,0:T(8,128)(2,1)} %get-tuple-element.76), channel_id=1, source_target_pairs={{0,1},{1,0},{2,3},{3,2},{4,5},{5,4},{6,7},{7,6},{8,9},{9,8},{10,11... | collective-permute-start | bytes 6291464 | tf_op jit(solution)/shard_map/ppermute | solution.py:471
  447.4 23.7 %collective-permute-start.40 = (bf16[4,96,1024]{2,1,0:T(8,128)(2,1)S(1)}, bf16[4,96,1024]{2,1,0:T(8,128)(2,1)}, u32[]{:S(2)}, u32[]{:S(2)}) collective-permute-start(bf16[4,96,1024]{2,1,0:T(8,128)(2,1)S(1)} %slice_bitcast_fusion.11), channel_id=1, source_target_pairs={{0,4},{4,0},{8,12},{12,8},{16,20},{20,16},{24,28},{28,24},{1,5},{5... | collective-permute-start | bytes 2359304 | tf_op jit(solution)/shard_map/ppermute | solution.py:475
  462.2 57.0 %collective-permute-start.45 = (bf16[4,288,1024]{2,1,0:T(8,128)(2,1)}, bf16[4,288,1024]{2,1,0:T(8,128)(2,1)}, u32[]{:S(2)}, u32[]{:S(2)}) collective-permute-start(bf16[4,288,1024]{2,1,0:T(8,128)(2,1)} %slice_bitcast_fusion), channel_id=1, source_target_pairs={{0,4},{4,0},{8,12},{12,8},{16,20},{20,16},{24,28},{28,24},{1,5},{5... | collective-permute-start | bytes 7077896 | tf_op jit(solution)/shard_map/ppermute | solution.py:475
  466.1 14.6 %collective-permute-start.35 = (f32[2,1024]{0,1:T(8,128)}, f32[2,1024]{0,1:T(8,128)}, u32[]{:S(2)}, u32[]{:S(2)}) collective-permute-start(f32[2,1024]{0,1:T(8,128)} %slice_bitcast_fusion.18), channel_id=1, source_target_pairs={{0,2},{2,0},{1,3},{3,1},{4,6},{6,4},{5,7},{7,5},{8,10},{10,8},{9,1... | collective-permute-start | bytes 24584 | tf_op jit(solution)/shard_map/ppermute | solution.py:471
  472.8 10.0 %collective-permute-start.41 = (bf16[96,1024]{1,0:T(8,128)(2,1)S(1)}, bf16[96,1024]{1,0:T(8,128)(2,1)S(1)}, u32[]{:S(2)}, u32[]{:S(2)}) collective-permute-start(bf16[96,1024]{1,0:T(8,128)(2,1)S(1)} %get-tuple-element.206), channel_id=1, source_target_pairs={{0,24},{4,28},{8,0},{12,4},{16,8},{20,12},{24,16},{28,20},{1,25},{... | collective-permute-start | bytes 589832 | tf_op jit(solution)/shard_map/ppermute | solution.py:479
  480.7 9.7 %collective-permute-start.43 = (bf16[96,1024]{1,0:T(8,128)(2,1)S(1)}, bf16[96,1024]{1,0:T(8,128)(2,1)S(1)}, u32[]{:S(2)}, u32[]{:S(2)}) collective-permute-start(bf16[96,1024]{1,0:T(8,128)(2,1)S(1)} %get-tuple-element.207), channel_id=1, source_target_pairs={{0,8},{4,12},{8,16},{12,20},{16,24},{20,28},{24,0},{28,4},{1,9},{5... | collective-permute-start | bytes 589832 | tf_op jit(solution)/shard_map/ppermute | solution.py:479
  482.8 14.5 %collective-permute-start.42 = (bf16[96,1024]{1,0:T(8,128)(2,1)S(1)}, bf16[96,1024]{1,0:T(8,128)(2,1)S(1)}, u32[]{:S(2)}, u32[]{:S(2)}) collective-permute-start(bf16[96,1024]{1,0:T(8,128)(2,1)S(1)} %get-tuple-element.208), channel_id=1, source_target_pairs={{0,16},{4,20},{8,24},{12,28},{16,0},{20,4},{24,8},{28,12},{1,17},{... | collective-permute-start | bytes 589832 | tf_op jit(solution)/shard_map/ppermute | solution.py:479
  490.4 33.9 %collective-permute-start.36 = (bf16[2,1024,512]{2,1,0:T(8,128)(2,1)S(1)}, bf16[2,1024,512]{2,1,0:T(8,128)(2,1)S(1)}, u32[]{:S(2)}, u32[]{:S(2)}) collective-permute-start(bf16[2,1024,512]{2,1,0:T(8,128)(2,1)S(1)} %copy-done.47), channel_id=1, source_target_pairs={{0,1},{1,0},{2,3},{3,2},{4,5},{5,4},{6,7},{7,6},{8,9},{9,8},{10,11... | collective-permute-start | bytes 6291464 | tf_op jit(solution)/shard_map/ppermute | solution.py:471
  497.4 13.8 %collective-permute-start.39 = (f32[2,1024]{0,1:T(8,128)S(1)}, f32[2,1024]{0,1:T(8,128)S(1)}, u32[]{:S(2)}, u32[]{:S(2)}) collective-permute-start(f32[2,1024]{0,1:T(8,128)S(1)} %slice_bitcast_fusion.16), channel_id=1, source_target_pairs={{0,2},{2,0},{1,3},{3,1},{4,6},{6,4},{5,7},{7,5},{8,10},{10,8},{9,1... | collective-permute-start | bytes 24584 | tf_op jit(solution)/shard_map/ppermute | solution.py:471
  512.7 12.3 %collective-permute-start.30 = (bf16[2,1024,512]{2,1,0:T(8,128)(2,1)S(1)}, bf16[2,1024,512]{2,1,0:T(8,128)(2,1)S(1)}, u32[]{:S(2)}, u32[]{:S(2)}) collective-permute-start(bf16[2,1024,512]{2,1,0:T(8,128)(2,1)S(1)} %copy-done.46), channel_id=1, source_target_pairs={{0,1},{1,0},{2,3},{3,2},{4,5},{5,4},{6,7},{7,6},{8,9},{9,8},{10,11... | collective-permute-start | bytes 6291464 | tf_op jit(solution)/shard_map/ppermute | solution.py:471
  516.1 96.4 %collective-permute-start.33 = (bf16[1024,512]{1,0:T(8,128)(2,1)S(1)}, bf16[1024,512]{1,0:T(8,128)(2,1)S(1)}, u32[]{:S(2)}, u32[]{:S(2)}) collective-permute-start(bf16[1024,512]{1,0:T(8,128)(2,1)S(1)} %fusion.33), channel_id=1, source_target_pairs={{0,2},{2,0},{1,3},{3,1},{4,6},{6,4},{5,7},{7,5},{8,10},{10,8},{9,1... | collective-permute-start | bytes 3145736 | tf_op jit(solution)/shard_map/ppermute | solution.py:471
  522.3 29.1 %collective-permute-start.46 = (bf16[288,1024]{1,0:T(8,128)(2,1)S(1)}, bf16[288,1024]{1,0:T(8,128)(2,1)S(1)}, u32[]{:S(2)}, u32[]{:S(2)}) collective-permute-start(bf16[288,1024]{1,0:T(8,128)(2,1)S(1)} %get-tuple-element.189), channel_id=1, source_target_pairs={{0,24},{4,28},{8,0},{12,4},{16,8},{20,12},{24,16},{28,20},{1,25},{... | collective-permute-start | bytes 1769480 | tf_op jit(solution)/shard_map/ppermute | solution.py:479
  522.8 29.3 %collective-permute-start.48 = (bf16[288,1024]{1,0:T(8,128)(2,1)S(1)}, bf16[288,1024]{1,0:T(8,128)(2,1)S(1)}, u32[]{:S(2)}, u32[]{:S(2)}) collective-permute-start(bf16[288,1024]{1,0:T(8,128)(2,1)S(1)} %get-tuple-element.190), channel_id=1, source_target_pairs={{0,8},{4,12},{8,16},{12,20},{16,24},{20,28},{24,0},{28,4},{1,9},{5... | collective-permute-start | bytes 1769480 | tf_op jit(solution)/shard_map/ppermute | solution.py:479
  524.3 49.8 %collective-permute-start.47 = (bf16[288,1024]{1,0:T(8,128)(2,1)S(1)}, bf16[288,1024]{1,0:T(8,128)(2,1)S(1)}, u32[]{:S(2)}, u32[]{:S(2)}) collective-permute-start(bf16[288,1024]{1,0:T(8,128)(2,1)S(1)} %get-tuple-element.191), channel_id=1, source_target_pairs={{0,16},{4,20},{8,24},{12,28},{16,0},{20,4},{24,8},{28,12},{1,17},{... | collective-permute-start | bytes 1769480 | tf_op jit(solution)/shard_map/ppermute | solution.py:479
  525.0 51.7 %collective-permute-start.23 = (bf16[1024,512]{1,0:T(8,128)(2,1)S(1)}, bf16[1024,512]{1,0:T(8,128)(2,1)S(1)}, u32[]{:S(2)}, u32[]{:S(2)}) collective-permute-start(bf16[1024,512]{1,0:T(8,128)(2,1)S(1)} %fusion.31), channel_id=1, source_target_pairs={{0,2},{2,0},{1,3},{3,1},{4,6},{6,4},{5,7},{7,5},{8,10},{10,8},{9,1... | collective-permute-start | bytes 3145736 | tf_op jit(solution)/shard_map/ppermute | solution.py:471
  551.4 61.2 %collective-permute-start.37 = (bf16[1024,512]{1,0:T(8,128)(2,1)S(1)}, bf16[1024,512]{1,0:T(8,128)(2,1)S(1)}, u32[]{:S(2)}, u32[]{:S(2)}) collective-permute-start(bf16[1024,512]{1,0:T(8,128)(2,1)S(1)} %fusion.34), channel_id=1, source_target_pairs={{0,2},{2,0},{1,3},{3,1},{4,6},{6,4},{5,7},{7,5},{8,10},{10,8},{9,1... | collective-permute-start | bytes 3145736 | tf_op jit(solution)/shard_map/ppermute | solution.py:471
  552.0 57.0 %collective-permute-start.31 = (bf16[1024,512]{1,0:T(8,128)(2,1)S(1)}, bf16[1024,512]{1,0:T(8,128)(2,1)S(1)}, u32[]{:S(2)}, u32[]{:S(2)}) collective-permute-start(bf16[1024,512]{1,0:T(8,128)(2,1)S(1)} %fusion.32), channel_id=1, source_target_pairs={{0,2},{2,0},{1,3},{3,1},{4,6},{6,4},{5,7},{7,5},{8,10},{10,8},{9,1... | collective-permute-start | bytes 3145736 | tf_op jit(solution)/shard_map/ppermute | solution.py:471
  575.9 45.5 %collective-permute-start.51 = (f32[128,512]{1,0:T(8,128)S(1)}, f32[128,512]{1,0:T(8,128)S(1)}, u32[]{:S(2)}, u32[]{:S(2)}) collective-permute-start(f32[128,512]{1,0:T(8,128)S(1)} %get-tuple-element.203), channel_id=1, source_target_pairs={{0,1},{1,0},{2,3},{3,2},{4,5},{5,4},{6,7},{7,6},{8,9},{9,8},{10,11... | collective-permute-start | bytes 786440 | tf_op jit(solution)/shard_map/ppermute | solution.py:471
  576.8 43.6 %collective-permute-start.50 = (f32[128,512]{1,0:T(8,128)S(1)}, f32[128,512]{1,0:T(8,128)S(1)}, u32[]{:S(2)}, u32[]{:S(2)}) collective-permute-start(f32[128,512]{1,0:T(8,128)S(1)} %get-tuple-element.204), channel_id=1, source_target_pairs={{0,1},{1,0},{2,3},{3,2},{4,5},{5,4},{6,7},{7,6},{8,9},{9,8},{10,11... | collective-permute-start | bytes 786440 | tf_op jit(solution)/shard_map/ppermute | solution.py:471
  (54 other events, 907.7 us)

commit v2 on v1

v2 whole, which is shorter than its diff:
```python
from functools import partial

import jax
import jax.numpy as jnp
import numpy as np
from jax import lax
from jax.experimental import pallas as pl
from jax.experimental.pallas import tpu as pltpu
from jax.sharding import PartitionSpec as P

D = 1024
HS = 64
ROT = 16
HALF = ROT // 2
EPSILON = 1e-05
MASKED = -1e30
NN = (((1,), (0,)), ((), ()))
NT = (((1,), (1,)), ((), ()))
TN = (((0,), (0,)), ((), ()))
VMEM_LIMIT = 56 << 20
F32 = jnp.float32
BF16 = jnp.bfloat16


def mm(a, b, dims):
    return lax.dot_general(a, b, dims, preferred_element_type=F32)


def params(**extra):
    return pltpu.CompilerParams(vmem_limit_bytes=VMEM_LIMIT, **extra)


def cost(flops, nbytes):
    return pl.CostEstimate(flops=int(flops), bytes_accessed=int(nbytes), transcendentals=0)


def whole(shape):
    return pl.BlockSpec(shape, lambda *_: (0,) * len(shape))


MESH = pl.DeviceIdType.MESH
ANYWHERE = pl.BlockSpec(memory_space=pl.ANY)


class Spot:
    def __init__(self):
        self.count = lax.axis_size("dp")
        self.depth = self.count // 2
        self.dp, self.row, self.col = (lax.axis_index(a) for a in ("dp", "row", "col"))
        self.z, self.x = self.dp // 2, self.dp % 2

    def along(self, steps):
        return ((self.z + steps) % self.depth) * 2 + self.x

    def device(self, which):
        return {
            "row": {"row": 1 - self.row},
            "col": {"col": 1 - self.col},
            "x": {"dp": self.z * 2 + (1 - self.x)},
            "right": {"dp": self.along(1)},
            "left": {"dp": self.along(self.depth - 1)},
        }[which]

    def greet(self, *names):
        barrier = pltpu.get_barrier_semaphore()
        for name in names:
            pl.semaphore_signal(barrier, inc=1, device_id=self.device(name), device_id_type=MESH)
        pl.semaphore_wait(barrier, len(names))


def remote(spot, which, source, target, send, recv):
    return pltpu.make_async_remote_copy(
        src_ref=source, dst_ref=target, send_sem=send, recv_sem=recv,
        device_id=spot.device(which), device_id_type=MESH,
    )


class Gather:
    def __init__(self, spot, mine, theirs, all_ref, local, send, recv):
        self.spot, self.all = spot, all_ref
        wide = mine.shape[1]
        here = all_ref.at[spot.dp]
        depth = spot.depth
        self.local = pltpu.make_async_copy(mine, here.at[:, pl.ds(0, wide)], local)
        self.core = remote(spot, "col", theirs, here.at[:, pl.ds(wide, wide)], send.at[0], recv.at[0])
        self.ring, self.cross = [], []
        for k in range(depth):
            slot = all_ref.at[spot.along(depth - k)]
            self.cross.append(remote(spot, "x", slot, slot, send.at[1 + k], recv.at[1 + k]))
            if k < depth - 1:
                at = 1 + depth + k
                self.ring.append(remote(spot, "right", slot, slot, send.at[at], recv.at[at]))

    @staticmethod
    def sems(count):
        return pltpu.SemaphoreType.DMA((count,))

    def begin(self):
        self.local.start()
        self.core.start()

    def first(self):
        self.local.wait()
        self.core.wait_recv()
        self.ring[0].start()
        self.cross[0].start()

    def forward(self, k):
        self.ring[k - 1].wait_recv()
        if k < len(self.ring):
            self.ring[k].start()
        self.cross[k].start()

    def finish(self):
        for copy in self.cross:
            copy.wait_recv()
        for copy in (self.core, *self.ring, *self.cross):
            copy.wait_send()


def enter_kernel(mine, theirs, tokens, all_ref, xb, xc, xd, local, send, recv, y_send, y_recv, c_send, c_recv, *, chunks):
    spot = Spot()
    spot.greet("row", "col", "x", "right", "left")
    gather = Gather(spot, mine, theirs, all_ref, local, send, recv)
    size = xb.shape[0] // chunks
    part = lambda k: pl.ds(k * size, size)
    over_row = [
        remote(spot, "row", tokens.at[0, part(k)], xb.at[part(k)], y_send.at[k], y_recv.at[k]) for k in range(chunks)
    ]
    over_col = [
        remote(spot, "col", xb.at[part(k)], xd.at[part(k)], c_send.at[k], c_recv.at[k]) for k in range(chunks)
    ]
    core = remote(spot, "col", tokens, xc, c_send.at[chunks], c_recv.at[chunks])
    gather.begin()
    for copy in over_row:
        copy.start()
    gather.first()
    core.start()
    depth = spot.depth
    for k in range(max(depth - 1, chunks)):
        if k + 1 < depth:
            gather.forward(k + 1)
        if k < chunks:
            over_row[k].wait_recv()
            over_col[k].start()
    gather.finish()
    core.wait()
    for k in range(chunks):
        over_col[k].wait()
        over_row[k].wait_send()


def enter(mine, theirs, tokens, count, chunks=4):
    rows, wide = mine.shape
    micros, length, _ = tokens.shape
    depth = count // 2
    half = jax.ShapeDtypeStruct((length, wide), BF16)
    return pl.pallas_call(
        partial(enter_kernel, chunks=chunks),
        in_specs=[ANYWHERE] * 3,
        out_specs=[ANYWHERE] * 4,
        out_shape=[
            jax.ShapeDtypeStruct((count, rows, 2 * wide), BF16), half,
            jax.ShapeDtypeStruct(tokens.shape, BF16), half,
        ],
        scratch_shapes=[
            pltpu.SemaphoreType.DMA, Gather.sems(2 * depth), Gather.sems(2 * depth),
            Gather.sems(chunks), Gather.sems(chunks), Gather.sems(chunks + 1), Gather.sems(chunks + 1),
        ],
        compiler_params=pltpu.CompilerParams(collective_id=0, has_side_effects=True),
        name="enter",
    )(mine, theirs, tokens)


def forward_kernel(
    xa, xc, xb0, xd0, weight, bias, vectors, cosine, sine, mine, theirs, tokens, grads,
    first, second, triple, att_own, att_far, logsum, all_ref, xb1, xd1, cb0, cc, cd0,
    x_s, q_s, v_s, o_s, n_s, f_s, local, send, recv, y_send, y_recv, c_send, c_recv, t_sem, l_sem, *, block, step,
):
    spot = Spot()
    now = pl.program_id(0)
    wide = xa.shape[2]
    width = 2 * wide
    own_tokens = tokens.shape[1]
    length = 2 * own_tokens
    blocks = own_tokens // block
    heads = weight.shape[0] // (3 * HS)
    depth = spot.depth
    attend0, far1, attend1 = 3 * blocks, 3 * blocks + heads, 4 * blocks + heads
    end = attend1 + heads - 1
    here, there = spot.row, 1 - spot.row

    gather = Gather(spot, mine, theirs, all_ref, local, send, recv)
    x_row = remote(spot, "row", tokens.at[1], xb1, y_send.at[0], y_recv.at[0])
    x_col = remote(spot, "col", xb1, xd1, c_send.at[0], c_recv.at[0])
    g_row = remote(spot, "row", grads.at[0], cb0, y_send.at[1], y_recv.at[1])
    g_col = remote(spot, "col", cb0, cd0, c_send.at[1], c_recv.at[1])
    g_core = remote(spot, "col", grads, cc, c_send.at[2], c_recv.at[2])
    load_near = pltpu.make_async_copy(xb1, n_s, l_sem.at[0])
    load_far = pltpu.make_async_copy(xd1, f_s, l_sem.at[1])
    keep = [pltpu.make_async_copy(q_s.at[m], triple.at[m], t_sem.at[m]) for m in range(2)]

    at = lambda k: pl.when(now == k)

    @at(0)
    def _():
        spot.greet("row", "col", "x", "right", "left")
        gather.begin()
        x_row.start()

    @at(1)
    def _():
        gather.first()
        g_core.start()

    for k in range(1, depth):
        moment = attend0 + 1 + (k - 1) * 5 // 2 if depth == 4 else far1 + blocks

        @at(moment)
        def _():
            gather.forward(k)

    @at(attend0)
    def _():
        keep_row = x_row
        keep_row.wait_recv()
        x_col.start()
        g_row.start()

    @at(attend0 + 1)
    def _():
        x_col.wait_recv()
        load_near.start()
        load_far.start()

    @at(far1)
    def _():
        load_near.wait()
        load_far.wait()

    @at(end - 1)
    def _():
        g_row.wait_recv()
        g_col.start()

    @pl.when(now < 2 * blocks)
    def _():
        x_s[:, :wide] = xa[0]
        x_s[:, wide:] = xc[0]

    @pl.when((now >= 2 * blocks) & (now < attend0))
    def _():
        x_s[:, :wide] = xb0[...]
        x_s[:, wide:] = xd0[...]

    for k in range(blocks):
        @at(far1 + k)
        def _():
            x_s[:, :wide] = n_s[k * block : (k + 1) * block]
            x_s[:, wide:] = f_s[k * block : (k + 1) * block]

    project = (now < attend0) | ((now >= far1) & (now < attend1))

    @pl.when(project)
    def _():
        micro = jnp.where(now < blocks, 0, jnp.where(now < 2 * blocks, 1, jnp.where(now < attend0, 0, 1)))
        half = jnp.where(now < 2 * blocks, here, there)
        number = jnp.where(now < attend0, now % blocks, (now - far1) % blocks)
        lane = pl.ds(pl.multiple_of(half * own_tokens + number * block, block), block)
        values = x_s[...].astype(F32)
        center = jnp.sum(values, axis=1, keepdims=True) / width
        spread = jnp.sum(values * values, axis=1, keepdims=True) / width - center * center
        normed = (values - center) * lax.rsqrt(spread + EPSILON)
        first[0, 0] = (normed * vectors[0:1, :] + vectors[1:2, :]).astype(BF16)
        second[0, 0] = (normed * vectors[2:3, :] + vectors[3:4, :]).astype(BF16)
        cos, sin = cosine[:, lane], sine[:, lane]
        for head in range(heads):
            base = head * 3 * HS
            rows = mm(weight[base : base + 3 * HS, :], first[0, 0], NT) + bias[base : base + 3 * HS, :]
            pieces = []
            for which in range(2):
                lo = which * HS
                scale = HS ** (-0.5) if which == 0 else 1.0
                u1, u2 = rows[lo : lo + HALF], rows[lo + HALF : lo + ROT]
                pieces += [(u1 * cos - u2 * sin) * scale, (u2 * cos + u1 * sin) * scale, rows[lo + ROT : lo + HS] * scale]
            pieces.append(rows[2 * HS :])
            q_s[micro, base : base + 3 * HS, lane] = jnp.concatenate(pieces, axis=0).astype(BF16)

    @at(attend0)
    def _():
        keep[0].start()

    @at(attend1)
    def _():
        keep[1].start()

    attending = ((now >= attend0) & (now < far1)) | (now >= attend1)

    @pl.when(attending)
    def _():
        micro = jnp.where(now < far1, 0, 1)
        head = jnp.where(now < far1, now - attend0, now - attend1)
        base = pl.multiple_of(head * 3 * HS, HS)
        query_of = lambda lo, hi: q_s[micro, pl.ds(base, HS), lo:hi]
        keys_of = lambda lo, hi: q_s[micro, pl.ds(pl.multiple_of(base + HS, HS), HS), lo:hi]
        v_s[0:HS, :] = q_s[micro, pl.ds(pl.multiple_of(base + 2 * HS, HS), HS), :]
        extra = lax.broadcasted_iota(jnp.int32, (16, length), 0)
        v_s[HS : HS + 16, :] = jnp.where(extra == 0, 1.0, 0.0).astype(BF16)
        allowed = causal_tile(step)
        for i in range(length // step):
            lo, hi = i * step, (i + 1) * step
            query = query_of(lo, hi)
            diag = jnp.where(allowed, mm(keys_of(lo, hi), query, TN), MASKED)
            highest = jnp.max(diag, axis=0, keepdims=True)
            if i:
                past = mm(keys_of(0, lo), query, TN)
                highest = jnp.maximum(highest, jnp.max(past, axis=0, keepdims=True))
            raised = jnp.exp(diag - highest).astype(BF16)
            result = mm(v_s[:, lo:hi], raised, NN)
            if i:
                raised = jnp.exp(past - highest).astype(BF16)
                result = result + mm(v_s[:, :lo], raised, NN)
            total = result[HS : HS + 1]
            o_s[:, lo:hi] = (result[:HS] / total).astype(BF16)
            logsum[0, 0, :, lo:hi] = highest + jnp.log(total)
        att_own[0] = o_s[:, lanes(here, own_tokens)]
        att_far[0] = o_s[:, lanes(there, own_tokens)]

    @at(end)
    def _():
        gather.finish()
        g_col.wait()
        g_core.wait()
        x_col.wait_send()
        x_row.wait_send()
        g_row.wait_send()
        keep[0].wait()
        keep[1].wait()


def lanes(index, tokens):
    return pl.ds(pl.multiple_of(index * tokens, tokens), tokens)


def forward(residual, xc, xb0, xd0, weight, bias, vectors, cosine, sine, mine, theirs, cotangent, count, block=512, step=512):
    micros, tokens, wide = residual.shape
    width, length = 2 * wide, 2 * tokens
    block, step = min(block, tokens), min(step, length)
    blocks = tokens // block
    rows = weight.shape[0]
    heads = rows // (3 * HS)
    depth = count // 2
    a0, f1, a1 = 3 * blocks, 3 * blocks + heads, 4 * blocks + heads
    steps = a1 + heads
    clip = lambda v, lo, hi: jnp.minimum(jnp.maximum(v, lo), hi)
    own = pl.BlockSpec((1, block, wide), lambda i: (jnp.where(i < blocks, 0, 1), jnp.where(i < 2 * blocks, i % blocks, blocks - 1), 0))
    far = pl.BlockSpec((block, wide), lambda i: (clip(i - 2 * blocks, 0, blocks - 1), 0))

    def place(i):
        late = i >= f1
        micro = jnp.where(i < blocks, 0, jnp.where(i < 2 * blocks, 1, jnp.where(late, 1, 0)))
        half = jnp.where(i < 2 * blocks, 1, 0)
        number = jnp.where(i < 2 * blocks, i % blocks, jnp.where(late, clip(i - f1, 0, blocks - 1), clip(i - 2 * blocks, 0, blocks - 1)))
        return micro, half, number, 0

    def head_of(i):
        late = i >= a1
        return jnp.where(late, 1, 0), jnp.where(late, i - a1, clip(i - a0, 0, heads - 1))

    normal = pl.BlockSpec((1, 1, block, width), place)
    att = pl.BlockSpec((1, HS, tokens), lambda i: (*head_of(i), 0))
    half = jax.ShapeDtypeStruct((tokens, wide), BF16)
    piece = mine.shape[0]
    return pl.pallas_call(
        partial(forward_kernel, block=block, step=step),
        grid=(steps,),
        in_specs=[
            own, own, far, far, whole(weight.shape), whole(bias.shape), whole(vectors.shape),
            whole(cosine.shape), whole(sine.shape), ANYWHERE, ANYWHERE, ANYWHERE, ANYWHERE,
        ],
        out_specs=[
            normal, normal, ANYWHERE, att, att, pl.BlockSpec((1, 1, 1, length), lambda i: (*head_of(i), 0, 0)),
            *[ANYWHERE] * 6,
        ],
        out_shape=[
            jax.ShapeDtypeStruct((micros, 2, tokens, width), BF16),
            jax.ShapeDtypeStruct((micros, 2, tokens, width), BF16),
            jax.ShapeDtypeStruct((micros, rows, length), BF16),
            jax.ShapeDtypeStruct((micros, heads * HS, tokens), BF16),
            jax.ShapeDtypeStruct((micros, heads * HS, tokens), BF16),
            jax.ShapeDtypeStruct((micros, heads, 1, length), F32),
            jax.ShapeDtypeStruct((count, piece, width), BF16),
            half, half, half, jax.ShapeDtypeStruct(cotangent.shape, BF16), half,
        ],
        scratch_shapes=[
            pltpu.VMEM((block, width), BF16),
            pltpu.VMEM((micros, rows, length), BF16),
            pltpu.VMEM((HS + 16, length), BF16),
            pltpu.VMEM((HS, length), BF16),
            pltpu.VMEM((tokens, wide), BF16),
            pltpu.VMEM((tokens, wide), BF16),
            pltpu.SemaphoreType.DMA, Gather.sems(2 * depth), Gather.sems(2 * depth),
            Gather.sems(2), Gather.sems(2), Gather.sems(3), Gather.sems(3), Gather.sems(2), Gather.sems(2),
        ],
        compiler_params=params(collective_id=1, has_side_effects=True),
        cost_estimate=cost(micros * length * width * rows * 2 + micros * heads * length * length * 256 * 2, 40 << 20),
        name="forward",
    )(residual, xc, xb0, xd0, weight, bias, vectors, cosine, sine, mine, theirs, residual, cotangent)
def causal_tile(size):
    keys = lax.broadcasted_iota(jnp.int32, (size, size), 0)
    places = lax.broadcasted_iota(jnp.int32, (size, size), 1)
    return keys <= places


def lanes(index, tokens):
    return pl.ds(pl.multiple_of(index * tokens, tokens), tokens)


POLY = (0.254829592, -0.284496736, 1.421413741, -1.453152027, 1.061405429)


def gelu_pair(value):
    magnitude = jnp.abs(value)
    t = 1.0 / (1.0 + magnitude * (0.3275911 * 0.5**0.5))
    bell = jnp.exp(value * value * -0.5)
    series = POLY[4]
    for term in (POLY[3], POLY[2], POLY[1], POLY[0]):
        series = series * t + term
    tail = 0.5 * series * t * bell
    cumulative = jnp.where(value >= 0.0, 1.0 - tail, tail)
    return value * cumulative, cumulative + value * bell * (1.0 / (2.0 * np.pi) ** 0.5)


def middle_kernel(
    second, ca, cc, cb0, cd0, att_own, att_far, pieces, wo, bias, grads,
    out_near, out_other, heads_own, heads_far, part, tiles, dbias, cb1, cd1,
    w1, w2, dw1, dw2, dwo, n_s, f_s, c_s, a_s, act_s, eg_s, w_sem, l_sem, y_send, y_recv, c_send, c_recv,
    *, block, chunk, out_part,
):
    spot = Spot()
    micro, half, at = pl.program_id(0), pl.program_id(1), pl.program_id(2)
    wide = ca.shape[2]
    count, rows, width = pieces.shape
    hid = w1.shape[0] // count
    heads = wo.shape[0] // HS
    steps = pl.num_programs(2)
    starting = (micro == 0) & (half == 0) & (at == 0)
    moment = micro * 2 * steps + half * steps + at
    g_row = remote(spot, "row", grads.at[1], cb1, y_send, y_recv)
    g_col = remote(spot, "col", cb1, cd1, c_send, c_recv)
    load_near = pltpu.make_async_copy(cb1, n_s, l_sem.at[0])
    load_far = pltpu.make_async_copy(cd1, f_s, l_sem.at[1])

    @pl.when(starting)
    def _():
        spot.greet("row", "col")
        g_row.start()
        lo = heads * out_part
        copies = []
        for p in range(count):
            here = slice(p * hid, (p + 1) * hid)
            copies.append(pltpu.make_async_copy(pieces.at[p, lo : lo + hid], w1.at[here], w_sem.at[2 * p]))
            copies.append(pltpu.make_async_copy(pieces.at[p, lo + hid :], w2.at[here], w_sem.at[2 * p + 1]))
        for copy in copies:
            copy.start()
        dw1[...] = jnp.zeros_like(dw1)
        dw2[...] = jnp.zeros_like(dw2)
        dwo[...] = jnp.zeros_like(dwo)
        dbias[...] = jnp.zeros_like(dbias)
        for copy in copies:
            copy.wait()

    @pl.when(moment == 2 * steps - 2)
    def _():
        g_row.wait_recv()
        g_col.start()

    @pl.when(moment == 2 * steps - 1)
    def _():
        g_col.wait_recv()
        load_near.start()
        load_far.start()

    @pl.when(moment == 2 * steps)
    def _():
        load_near.wait()
        load_far.wait()

    @pl.when((half == 0) & (micro == 0))
    def _():
        c_s[:, :wide] = cb0[...]
        c_s[:, wide:] = cd0[...]

    @pl.when((half == 0) & (micro == 1))
    def _():
        here = pl.ds(pl.multiple_of(at * block, block), block)
        c_s[:, :wide] = n_s[here, :]
        c_s[:, wide:] = f_s[here, :]

    @pl.when(half == 1)
    def _():
        c_s[:, :wide] = ca[0]
        c_s[:, wide:] = cc[0]
        a_s[...] = att_own[0]

    @pl.when(half == 0)
    def _():
        a_s[...] = att_far[0]

    hidden = w1.shape[0]
    for lo in range(0, hidden, chunk):
        hi = lo + chunk
        expanded = mm(second[0, 0], w1[lo:hi, :], NT) + bias[:, lo:hi]
        active, slope = gelu_pair(expanded)
        act_s[:, lo:hi] = active.astype(BF16)
        rounded = (mm(c_s[...], w2[lo:hi, :], NT) * slope).astype(BF16)
        eg_s[:, lo:hi] = rounded
        dbias[:, lo:hi] += jnp.sum(rounded.astype(F32), axis=0, keepdims=True)
    for lo in range(0, hidden, chunk):
        hi = lo + chunk
        dw2[lo:hi, :] += mm(act_s[:, lo:hi], c_s[...], TN)
        dw1[lo:hi, :] += mm(eg_s[:, lo:hi], second[0, 0], TN)
    dwo[...] += mm(a_s[...], c_s[...], NN)
    out_near[0, 0] = (mm(act_s[...], w2[:, :wide], NN) + mm(a_s[...], wo[:, :wide], TN)).astype(BF16)
    out_other[0, 0] = (mm(act_s[...], w2[:, wide:], NN) + mm(a_s[...], wo[:, wide:], TN)).astype(BF16)
    part[0, 0] = mm(eg_s[...], w1[...], NN).astype(BF16)
    heads_grad = mm(wo[...], c_s[...], NT).astype(BF16)

    @pl.when(half == 0)
    def _():
        heads_far[0] = heads_grad

    @pl.when(half == 1)
    def _():
        heads_own[0] = heads_grad

    @pl.when(moment == 4 * steps - 1)
    def _():
        lo = heads * out_part
        for p in range(count):
            here = slice(p * hid, (p + 1) * hid)
            small = [dwo[h * HS + p * out_part : h * HS + (p + 1) * out_part, :] for h in range(heads)]
            tiles[p, :lo] = jnp.concatenate(small, axis=0).astype(BF16)
            tiles[p, lo : lo + hid] = dw1[here, :].astype(BF16)
            tiles[p, lo + hid :] = dw2[here, :].astype(BF16)
        g_row.wait_send()
        g_col.wait_send()


def middle(second, cotangent, cc, cb0, cd0, att_own, att_far, pieces, wo, bias, block=256, chunk=256):
    micros, tokens, wide = cotangent.shape
    count, rows, width = pieces.shape
    block = min(block, tokens)
    steps = tokens // block
    hidden, head_rows = bias.shape[1], wo.shape[0]
    hid = hidden // count
    out_part = (rows - 2 * hid) * HS // head_rows
    end = steps - 1
    both = lambda n: pl.BlockSpec((1, 1, block, n), lambda m, h, i: (m, h, i, 0))
    own_at = lambda m, h, i: (m, h * i)
    far_at = lambda m, h, i: (m, i * (1 - h) + end * h)
    own = pl.BlockSpec((1, block, wide), lambda m, h, i: (*own_at(m, h, i), 0))
    far0 = pl.BlockSpec((block, wide), lambda m, h, i: (jnp.where((m == 0) & (h == 0), i, end), 0))
    cols_own = pl.BlockSpec((1, head_rows, block), lambda m, h, i: (m, 0, h * i))
    cols_far = pl.BlockSpec((1, head_rows, block), lambda m, h, i: (m, 0, i * (1 - h) + end * h))
    halves = jax.ShapeDtypeStruct((tokens, wide), BF16)
    return pl.pallas_call(
        partial(middle_kernel, block=block, chunk=min(chunk, hidden), out_part=out_part),
        grid=(micros, 2, steps),
        in_specs=[
            both(width), own, own, far0, far0, cols_own, cols_far, ANYWHERE, whole(wo.shape), whole(bias.shape), ANYWHERE,
        ],
        out_specs=[
            both(wide), both(wide), cols_own, cols_far, both(width), whole(pieces.shape), whole(bias.shape),
            ANYWHERE, ANYWHERE,
        ],
        out_shape=[
            jax.ShapeDtypeStruct((micros, 2, tokens, wide), BF16),
            jax.ShapeDtypeStruct((micros, 2, tokens, wide), BF16),
            jax.ShapeDtypeStruct((micros, head_rows, tokens), BF16),
            jax.ShapeDtypeStruct((micros, head_rows, tokens), BF16),
            jax.ShapeDtypeStruct((micros, 2, tokens, width), BF16),
            jax.ShapeDtypeStruct(pieces.shape, BF16),
            jax.ShapeDtypeStruct(bias.shape, F32),
            halves, halves,
        ],
        scratch_shapes=[
            pltpu.VMEM((hidden, width), BF16),
            pltpu.VMEM((hidden, width), BF16),
            pltpu.VMEM((hidden, width), F32),
            pltpu.VMEM((hidden, width), F32),
            pltpu.VMEM((head_rows, width), F32),
            pltpu.VMEM((tokens, wide), BF16),
            pltpu.VMEM((tokens, wide), BF16),
            pltpu.VMEM((block, width), BF16),
            pltpu.VMEM((head_rows, block), BF16),
            pltpu.VMEM((block, hidden), BF16),
            pltpu.VMEM((block, hidden), BF16),
            Gather.sems(2 * count), Gather.sems(2),
            pltpu.SemaphoreType.DMA, pltpu.SemaphoreType.DMA, pltpu.SemaphoreType.DMA, pltpu.SemaphoreType.DMA,
        ],
        compiler_params=params(collective_id=2, has_side_effects=True),
        cost_estimate=cost(2 * micros * tokens * 2 * width * (6 * hidden + 3 * head_rows), 80 << 20),
        name="middle",
    )(second, cotangent, cc, cb0, cd0, att_own, att_far, pieces, wo, bias, cotangent)


def attend_back_kernel(
    triple, grad_own, grad_far, att_own, att_far, logsum, cosine, sine,
    out_own, out_far, bias_grad, g_s, delta_s, dq_s, dk_s, dv_s, t_s, *, step,
):
    tokens = grad_own.shape[2]
    length = 2 * tokens
    here = lax.axis_index("row")
    there = 1 - here
    for grad, att, place in ((grad_own, att_own, here), (grad_far, att_far, there)):
        at = lanes(place, tokens)
        g_s[:, at] = grad[0]
        delta_s[:, at] = jnp.sum(grad[0].astype(F32) * att[0].astype(F32), axis=0, keepdims=True)
    q_s, k_s, v_s = (triple.at[0, i * HS : (i + 1) * HS] for i in range(3))
    dk_s[...] = jnp.zeros_like(dk_s)
    dv_s[...] = jnp.zeros_like(dv_s)
    allowed = causal_tile(step)
    for i in range(length // step):
        lo, hi = i * step, (i + 1) * step
        query, grad = q_s[:, lo:hi], g_s[:, lo:hi]
        base, delta = logsum[0, 0, :, lo:hi], delta_s[:, lo:hi]
        query_grad = None
        for begin, end in ((0, lo), (lo, hi)):
            if end == begin:
                continue
            raised = jnp.exp(mm(k_s[:, begin:end], query, TN) - base)
            if begin == lo:
                raised = jnp.where(allowed, raised, 0.0)
            prob_grad = mm(v_s[:, begin:end], grad, TN)
            score_grad = (raised * (prob_grad - delta)).astype(BF16)
            dv_s[:, begin:end] += mm(grad, raised.astype(BF16), NT)
            dk_s[:, begin:end] += mm(query, score_grad, NT)
            term = mm(k_s[:, begin:end], score_grad, NN)
            query_grad = term if query_grad is None else query_grad + term
        dq_s[:, lo:hi] = query_grad * HS ** (-0.5)
    cos, sin = cosine[...], sine[...]
    for which, ref in ((0, dq_s), (1, dk_s)):
        g1, g2 = ref[0:HALF, :], ref[HALF:ROT, :]
        spun = jnp.concatenate([g1 * cos + g2 * sin, g2 * cos - g1 * sin], axis=0)
        t_s[which * HS : which * HS + ROT, :] = spun.astype(BF16)
        t_s[which * HS + ROT : (which + 1) * HS, :] = ref[ROT:HS, :].astype(BF16)
    t_s[2 * HS : 3 * HS, :] = dv_s[...].astype(BF16)
    bias_grad[...] = jnp.sum(t_s[...].astype(F32), axis=1, keepdims=True)
    out_own[...] = t_s[:, lanes(here, tokens)]
    out_far[...] = t_s[:, lanes(there, tokens)]


def attend_back(micro, triple, grad_own, grad_far, att_own, att_far, logsum, cosine, sine, step=256):
    _, rows, length = triple.shape
    tokens = length // 2
    heads = rows // (3 * HS)
    narrow = pl.BlockSpec((1, HS, tokens), lambda h: (micro, h, 0))
    result = pl.BlockSpec((3 * HS, tokens), lambda h: (h, 0))
    table = whole((HALF, length))
    return pl.pallas_call(
        partial(attend_back_kernel, step=min(step, length)),
        grid=(heads,),
        in_specs=[
            pl.BlockSpec((1, 3 * HS, length), lambda h: (micro, h, 0)), narrow, narrow, narrow, narrow,
            pl.BlockSpec((1, 1, 1, length), lambda h: (micro, h, 0, 0)), table, table,
        ],
        out_specs=[result, result, pl.BlockSpec((3 * HS, 1), lambda h: (h, 0))],
        out_shape=[
            jax.ShapeDtypeStruct((rows, tokens), BF16),
            jax.ShapeDtypeStruct((rows, tokens), BF16),
            jax.ShapeDtypeStruct((rows, 1), F32),
        ],
        scratch_shapes=[
            pltpu.VMEM((HS, length), BF16),
            pltpu.VMEM((1, length), F32),
            pltpu.VMEM((HS, length), F32),
            pltpu.VMEM((HS, length), F32),
            pltpu.VMEM((HS, length), F32),
            pltpu.VMEM((3 * HS, length), BF16),
        ],
        compiler_params=params(),
        cost_estimate=cost(heads * length * length * 256 * 5, 16 * rows * tokens),
        name="attend_back",
    )(triple, grad_own, grad_far, att_own, att_far, logsum, cosine, sine)


def last_kernel(
    t_own, t_far, first, part, xa, xb, xc, xd, weight, vectors, before,
    ng_near, ng_other, sums, result, dvec, total, t_s, x_s, *, final, count,
):
    half, at = pl.program_id(0), pl.program_id(1)
    wide = xb.shape[1]
    width = 2 * wide
    steps = pl.num_programs(1)

    @pl.when((half == 0) & (at == 0))
    def _():
        if final:
            total[...] = before[...]
        else:
            total[...] = jnp.zeros_like(total)
        dvec[...] = jnp.zeros_like(dvec)

    @pl.when(half == 0)
    def _():
        t_s[...] = t_far[...]
        x_s[:, :wide] = xb[...]
        x_s[:, wide:] = xd[...]

    @pl.when(half == 1)
    def _():
        t_s[...] = t_own[...]
        x_s[:, :wide] = xa[0]
        x_s[:, wide:] = xc[0]

    total[...] += mm(t_s[...], first[0, 0], NN)
    values = x_s[...].astype(F32)
    center = jnp.sum(values, axis=1, keepdims=True) / width
    spread = jnp.sum(values * values, axis=1, keepdims=True) / width - center * center
    inv = lax.rsqrt(spread + EPSILON)
    first_sum = second_sum = 0.0
    for side, ref in ((0, ng_near), (1, ng_other)):
        cols = slice(side * wide, (side + 1) * wide)
        normed = (x_s[:, cols].astype(F32) - center) * inv
        first_grad = mm(t_s[...], weight[:, cols], TN)
        second_grad = part[0, 0, :, cols].astype(F32)
        dvec[0:1, cols] += jnp.sum(first_grad * normed, axis=0, keepdims=True)
        dvec[1:2, cols] += jnp.sum(first_grad, axis=0, keepdims=True)
        dvec[2:3, cols] += jnp.sum(second_grad * normed, axis=0, keepdims=True)
        dvec[3:4, cols] += jnp.sum(second_grad, axis=0, keepdims=True)
        grad = first_grad * vectors[0:1, cols] + second_grad * vectors[2:3, cols]
        first_sum = first_sum + jnp.sum(grad, axis=1, keepdims=True)
        second_sum = second_sum + jnp.sum(grad * normed, axis=1, keepdims=True)
        ref[0] = grad.astype(BF16)
    column = lax.broadcasted_iota(jnp.int32, (x_s.shape[0], 128), 1)
    both = jnp.where(column == 0, first_sum, jnp.where(column == 1, second_sum, 0.0))
    sums[0] = jnp.transpose(both)[0:8, :]

    @pl.when((half == 1) & (at == steps - 1))
    def _():
        if final:
            heads = total.shape[0] // (3 * HS)
            size = 3 * HS // count
            for p in range(count):
                small = [total[h * 3 * HS + p * size : h * 3 * HS + (p + 1) * size, :] for h in range(heads)]
                result[p] = jnp.concatenate(small, axis=0).astype(BF16)
        else:
            result[...] = total[...]


def last(micro, t_own, t_far, first, part, residual, xb, xc, xd, weight, vectors, before, count, block=256):
    _, tokens, wide = residual.shape
    width = 2 * wide
    block = min(block, tokens)
    steps = tokens // block
    rows = weight.shape[0]
    end = steps - 1
    far_at = lambda h, i: i * (1 - h) + end * h
    own_at = lambda h, i: i * h
    own = pl.BlockSpec((1, block, wide), lambda h, i: (micro, own_at(h, i), 0))
    far = pl.BlockSpec((block, wide), lambda h, i: (far_at(h, i), 0))
    both = lambda n: pl.BlockSpec((1, 1, block, n), lambda h, i: (micro, h, i, 0))
    out = pl.BlockSpec((1, block, wide), lambda h, i: (h, i, 0))
    final = before is not None
    shape = jax.ShapeDtypeStruct((count, rows // count, width), BF16) if final else jax.ShapeDtypeStruct((rows, width), F32)
    before = before if final else jnp.zeros((8, 128), F32)
    return pl.pallas_call(
        partial(last_kernel, final=final, count=count),
        grid=(2, steps),
        in_specs=[
            pl.BlockSpec((rows, block), lambda h, i: (0, own_at(h, i))),
            pl.BlockSpec((rows, block), lambda h, i: (0, far_at(h, i))),
            both(width), both(width), own, far, own, far,
            whole(weight.shape), whole(vectors.shape), whole(before.shape),
        ],
        out_specs=[
            out, out, pl.BlockSpec((1, 8, block), lambda h, i: (h, 0, i)), whole(shape.shape), whole((8, width)),
        ],
        out_shape=[
            jax.ShapeDtypeStruct((2, tokens, wide), BF16),
            jax.ShapeDtypeStruct((2, tokens, wide), BF16),
            jax.ShapeDtypeStruct((2, 8, tokens), F32),
            shape,
            jax.ShapeDtypeStruct((8, width), F32),
        ],
        scratch_shapes=[
            pltpu.VMEM((rows, width), F32),
            pltpu.VMEM((rows, block), BF16),
            pltpu.VMEM((block, width), BF16),
        ],
        compiler_params=params(),
        cost_estimate=cost(2 * tokens * 2 * width * 2 * rows, 2 * tokens * width * 10),
        name="last",
    )(t_own, t_far, first, part, residual, xb, xc, xd, weight, vectors, before)


def total_kernel(value, out, held, arrived, send, recv):
    spot = Spot()
    partners = [{"col": 1 - spot.col}, {"row": 1 - spot.row}, {"dp": spot.z * 2 + (1 - spot.x)}]
    stride = 1
    while stride < spot.depth:
        other = spot.z + stride * (1 - 2 * ((spot.z // stride) % 2))
        partners.append({"dp": other * 2 + spot.x})
        stride *= 2
    barrier = pltpu.get_barrier_semaphore()
    for partner in partners:
        pl.semaphore_signal(barrier, inc=1, device_id=partner, device_id_type=MESH)
    pl.semaphore_wait(barrier, len(partners))
    held[0] = value[...]
    for k, partner in enumerate(partners):
        copy = pltpu.make_async_remote_copy(
            src_ref=held.at[k], dst_ref=arrived.at[k], send_sem=send.at[k], recv_sem=recv.at[k],
            device_id=partner, device_id_type=MESH,
        )
        copy.start()
        copy.wait()
        if k + 1 < len(partners):
            held[k + 1] = held[k] + arrived[k]
        else:
            out[...] = held[k] + arrived[k]


def total_of(value, count):
    hops = 3 + max(count // 2 - 1, 0).bit_length()
    vmem = pl.BlockSpec(memory_space=pltpu.VMEM)
    return pl.pallas_call(
        total_kernel,
        in_specs=[vmem],
        out_specs=vmem,
        out_shape=jax.ShapeDtypeStruct(value.shape, F32),
        scratch_shapes=[
            pltpu.VMEM((hops, *value.shape), F32), pltpu.VMEM((hops, *value.shape), F32),
            Gather.sems(hops), Gather.sems(hops),
        ],
        compiler_params=pltpu.CompilerParams(collective_id=3, has_side_effects=True),
        name="total",
    )(value)


def swap(value, axis):
    return lax.ppermute(value, axis, [(0, 1), (1, 0)])


def across(value, count):
    return lax.ppermute(value, "dp", [(i, i ^ 1) for i in range(count)])


def shifted(value, steps, count):
    return lax.ppermute(value, "dp", [(i, (i + 2 * steps) % count) for i in range(count)])


def pick(value, index, axis=0):
    return lax.dynamic_index_in_dim(value, index, axis, keepdims=False)


def rows_from_cores(mine, col):
    wide = mine.shape[-1] // 2
    other = swap(mine[..., wide:], "col")
    mine = mine[..., :wide]
    return jnp.where(col == 0, jnp.concatenate([mine, other], 0), jnp.concatenate([other, mine], 0))


def body(
    residual, attend_norm_gain, attend_norm_bias, expand_norm_gain, expand_norm_bias,
    attend_weight, attend_bias, output_weight, output_bias, expand_weight, expand_bias,
    shrink_weight, shrink_bias, cotangent,
):
    count = lax.axis_size("dp")
    depth = count // 2
    row, col, dp = lax.axis_index("row"), lax.axis_index("col"), lax.axis_index("dp")
    place_z, place_x = dp // 2, dp % 2
    micros, tokens, wide = residual.shape
    width, length = 2 * wide, 2 * tokens
    heads = attend_weight.shape[1] // 2
    head_part, out_part = attend_weight.shape[2], output_weight.shape[1]
    hid = expand_weight.shape[1] // 2

    def sides(rows):
        return pick(rows, col), pick(rows, 1 - col)

    head_mine, head_theirs = sides(attend_weight.transpose(1, 2, 0).reshape(2, heads * head_part, wide))
    rest_mine, rest_theirs = sides(
        jnp.concatenate(
            [
                output_weight.reshape(2, heads * out_part, wide),
                expand_weight.T.reshape(2, hid, wide),
                shrink_weight.reshape(2, hid, wide),
            ],
            axis=1,
        )
    )
    head_all, xb0, xc, xd0 = enter(head_mine, head_theirs, residual, count)
    wq = head_all.reshape(count, heads, head_part, width).transpose(1, 0, 2, 3).reshape(heads * 3 * HS, width)

    vectors = jnp.stack([attend_norm_gain, attend_norm_bias, expand_norm_gain, expand_norm_bias])
    vectors = jnp.concatenate([jnp.roll(vectors, -col * wide, axis=1), jnp.zeros((4, width), F32)])
    head_begin = row * 2 * heads + col * heads
    bias_q = lax.dynamic_slice_in_dim(attend_bias, head_begin, heads, 0).reshape(-1, 1)
    bias_1 = pick(expand_bias.reshape(count, 4, hid), row * 2 + col, 1).reshape(1, -1)
    out_bias = lax.dynamic_slice_in_dim(output_bias + shrink_bias, col * wide, wide, 0)
    powers = 10000.0 ** (-np.arange(HALF) * (2.0 / ROT))
    angles = powers[:, None] * np.arange(length)[None, :]
    cosine, sine = jnp.asarray(np.cos(angles), F32), jnp.asarray(np.sin(angles), F32)

    first, second, triple, att_own, att_far, logsum, pieces, xb1, xd1, cb0, cc, cd0 = forward(
        residual, xc, xb0, xd0, wq, bias_q, vectors, cosine, sine, rest_mine, rest_theirs, cotangent, count
    )
    lo = heads * out_part
    wo = pieces[:, :lo].reshape(count, heads, out_part, width).transpose(1, 0, 2, 3).reshape(heads * HS, width)
    near, other, heads_own, heads_far, part, tiles, db1, cb1, cd1 = middle(
        second, cotangent, cc, cb0, cd0, att_own, att_far, pieces, wo, bias_1
    )

    crossed = swap(other, "col")
    tiles = tiles.reshape(depth, 2, *tiles.shape[1:])
    tiles_away = pick(tiles, 1 - place_x, 1)
    heads_own, tiles_away = lax.optimization_barrier((heads_own, tiles_away))
    moved = swap((near[:, 0].astype(F32) + crossed[:, 0].astype(F32)).astype(BF16), "row")
    tiles_back = across(tiles_away, count)

    def norm_back(micro, xb, xd, before, heads_own):
        t_own, t_far, bias_grad = attend_back(
            micro, triple, heads_own, heads_far, att_own, att_far, logsum, cosine, sine
        )
        return bias_grad, last(micro, t_own, t_far, first, part, residual, xb, xc, xd, wq, vectors, before, count)

    def input_grad(micro, near, other, sums):
        crossed = swap(other, "col")
        moved = swap((near[0].astype(F32) + crossed[0].astype(F32)).astype(BF16), "row")
        sums = sums + swap(sums, "col")
        sums = sums[1] + swap(sums[0], "row")
        grad = near[1].astype(F32) + crossed[1].astype(F32) + moved.astype(F32)
        near_x, far_x = residual[micro].astype(F32), xc[micro].astype(F32)
        center = (jnp.sum(near_x, 1) + jnp.sum(far_x, 1)) / width
        spread = (jnp.sum(near_x * near_x, 1) + jnp.sum(far_x * far_x, 1)) / width - center * center
        inv = lax.rsqrt(spread + EPSILON)[:, None]
        normed = (near_x - center[:, None]) * inv
        return cotangent[micro].astype(F32) + inv * (
            grad - sums[0][:, None] / width - normed * sums[1][:, None] / width
        )

    def along_z(kept):
        total = pick(kept, place_z)
        for s in range(1, depth):
            total = total + shifted(pick(kept, (place_z + s) % depth).astype(BF16), s, count).astype(F32)
        return total

    bias_0, (near_0, other_0, sums_0, dq, dvec_0) = norm_back(0, xb0, xd0, None, heads_own)
    kept = pick(tiles, place_x, 1).astype(F32) + tiles_back.astype(F32)
    dq, kept = lax.optimization_barrier((dq, kept))
    rest_sum = along_z(kept)
    outputs = (
        residual.astype(F32) + near[:, 1].astype(F32) + crossed[:, 1].astype(F32) + moved.astype(F32) + out_bias
    ).astype(BF16)
    grad_0 = input_grad(0, near_0, other_0, sums_0)
    heads_own, dq = lax.optimization_barrier((heads_own, dq))
    bias_1_, (near_1, other_1, sums_1, dq_tiles, dvec_1) = norm_back(1, xb1, xd1, dq, heads_own)
    grad_1 = input_grad(1, near_1, other_1, sums_1)
    dq_tiles = dq_tiles.reshape(depth, 2, *dq_tiles.shape[1:])
    dq_back = across(pick(dq_tiles, 1 - place_x, 1), count)
    dq_sum = along_z(pick(dq_tiles, place_x, 1).astype(F32) + dq_back.astype(F32))

    attend_weight_grad = rows_from_cores(dq_sum.reshape(heads, head_part, width), col).transpose(2, 0, 1)
    output_weight_grad = rows_from_cores(rest_sum[:lo].reshape(heads, out_part, width), col)
    expand_weight_grad = rows_from_cores(rest_sum[lo : lo + hid], col).T
    shrink_weight_grad = rows_from_cores(rest_sum[lo + hid :], col)

    dvec = jnp.roll((dvec_0 + dvec_1)[:4], col * wide, axis=1)
    dout = jnp.sum(cotangent.astype(F32), axis=(0, 1))
    dout = lax.dynamic_update_slice_in_dim(jnp.zeros((width,), F32), dout, col * wide, 0)
    dbq = (bias_0 + bias_1_).reshape(heads, -1)
    dbq = lax.dynamic_update_slice_in_dim(jnp.zeros(attend_bias.shape, F32), dbq, head_begin, 0)
    db1 = lax.dynamic_update_slice_in_dim(
        jnp.zeros((count, 4, hid), F32), db1.reshape(count, 1, hid), row * 2 + col, 1
    )
    flat = [dvec.reshape(-1), dout, dbq.reshape(-1), db1.reshape(-1)]
    ends = np.cumsum([part.size for part in flat])
    summed = total_of(jnp.concatenate(flat).reshape(-1, 128), count).reshape(-1)
    dvec, dout, dbq, db1 = jnp.split(summed, ends[:-1])
    dvec = dvec.reshape(4, width)
    return (
        outputs, jnp.stack([grad_0, grad_1]), dvec[0], dvec[1], dvec[2], dvec[3],
        attend_weight_grad, dbq.reshape(attend_bias.shape), output_weight_grad, dout, expand_weight_grad, db1,
        shrink_weight_grad, dout,
    )


def solution(mesh):
    tokens = P(None, ("dp", "row"), "col")
    weights = (P("col", "row", "dp"), P("row", "dp", "col"), P("col", ("dp", "row")), P(("dp", "row"), "col"))
    one = P()
    in_specs = (tokens, one, one, one, one, weights[0], one, weights[1], one, weights[2], one, weights[3], one, tokens)
    out_specs = (tokens, tokens, one, one, one, one, weights[0], one, weights[1], one, weights[2], one, weights[3], one)
    return jax.shard_map(body, mesh=mesh, in_specs=in_specs, out_specs=out_specs, check_vma=False)
```

time: 631 us -> 523 us (0.83)
  Pallas kernels: 268 us -> 312 us
  blocking collectives: 41.7 us -> 0 us
  starting transfers between devices: 58.8 us -> 18 us
  waiting for transfers between devices: 160 us -> 120 us
  local copies, waits for them, and re-layouts: 46.2 us -> 25.7 us
  other arithmetic: 46.8 us -> 35.5 us
    ppermute x12 -> x6, waiting for transfers between devices: 74.3 us -> 4.2 us  [shifted(): lax.ppermute(value, 'dp', [(i, (i + 2 * steps) % count) for i in range(co...]
    pallas_call x10 -> x6, Pallas kernels: 208 us -> 252 us  [the longest x1 84.7 us: middle(): pl.pallas_call(partial(middle_kernel, block=block, chunk=min(chunk, hidde...]
    psum x1 -> x0, blocking collectives: 41.7 us -> none  [body(): lax.psum((dvec, dout, dbq, db1), ('dp', 'row', 'col'))]
    ppermute x10 -> x2, waiting for transfers between devices: 28 us -> 57.2 us  [across(): return lax.ppermute(value, 'dp', [(i, i ^ 1) for i in range(count)])]
    ppermute x12 -> x6, starting transfers between devices: 28.1 us -> 9.25 us  [shifted(): lax.ppermute(value, 'dp', [(i, (i + 2 * steps) % count) for i in range(co...]
    unnamed x120 -> x67, local copies, waits for them, and re-layouts: 18.3 us -> 5.36 us
    ppermute x30 -> x14, starting transfers between devices: 18.8 us -> 6.31 us  [swap(): return lax.ppermute(value, axis, [(0, 1), (1, 0)])]
    ppermute x10 -> x2, starting transfers between devices: 11.9 us -> 2.49 us  [across(): return lax.ppermute(value, 'dp', [(i, i ^ 1) for i in range(count)])]
  transfers between devices with their start and end apart: 52 -> 22, of which waited for: 17 -> 8; matrix products, arithmetic and copies ran while one was open for 14% -> 8% of each run, Pallas kernels for 43% -> 13%
where the time goes in v2:
time: 523 us; the launch traced here: 513 us
  Pallas kernels  312 us (60%)
  waiting for transfers between devices  120 us (23%)
  other arithmetic  35.5 us (7%)
  local copies, waits for them, and re-layouts  25.7 us (5%)
  starting transfers between devices  18 us (3%)
    pallas_call x1, Pallas kernels, middle(): pl.pallas_call(partial(middle_kernel, block=block, chunk=min(chunk, hidde...  84.7 us
    pallas_call x1, Pallas kernels, forward(): pl.pallas_call(partial(forward_kernel, block=block, step=step), grid=(ste...  79.9 us
    pallas_call x2, Pallas kernels, attend_back(): pl.pallas_call(partial(attend_back_kernel, step=min(step, length)), grid=...  59.8 us
    ppermute x14, waiting for transfers between devices, swap(): return lax.ppermute(value, axis, [(0, 1), (1, 0)])  59 us
    ppermute x2, waiting for transfers between devices, across(): return lax.ppermute(value, 'dp', [(i, i ^ 1) for i in range(count)])  57.2 us
    pallas_call x2, Pallas kernels, last(): pl.pallas_call(partial(last_kernel, final=final, count=count), grid=(2, s...  38.1 us
    pallas_call x1, Pallas kernels, enter(): pl.pallas_call(partial(enter_kernel, chunks=chunks), in_specs=[ANYWHERE]...  31.6 us
    pallas_call x1, Pallas kernels, total_of(): pl.pallas_call(total_kernel, in_specs=[vmem], out_specs=vmem, out_shape=j...  17.7 us
  transfers between devices with their start and end apart: 22, of which 8 were waited for; matrix products, arithmetic and copies ran while one was open for 8% of the time, Pallas kernels for 13%

profile of v2, /device:TPU:0, one launch (start us, length us, event | category | flops | bytes accessed | tf_op | source)
XLA Modules:
  0.0 513.3 jit_solution(13931384780396548659)
XLA Ops:
  0.7 1.6 dynamic-slice_bitcast_fusion.4
  2.3 31.6 %enter.1 = (bf16[8,96,1024]{2,1,0:T(8,128)(2,1)}, bf16[1024,512]{1,0:T(8,128)(2,1)}, bf16[2,1024,512]{2,1,0:T(8,128)(2,1)}, bf16[1024,512]{1,0:T(8,128)(2,1)}) custom-call(bf16[96,512]{1,0:T(8,128)(2,1)} %get-tuple-element.162.mine, bf16[96,512]{1,0:T(8,128)(2,1)} %get-tuple-element.161.theirs, bf16[2,1024,512]{2,1,0:T(8,128)(2,1)} %xa.5), custom_call_target="tpu_custom_call" | custom-call | tf_op jit(solution)/shard_map/enter/pallas_call | solution.py:158
  34.0 2.8 copy.37
  37.0 0.9 dynamic-slice_bitcast_fusion.2
  38.5 1.0 reshape.242.bias
  40.3 79.9 %forward.1 = (bf16[2,2,1024,1024]{3,2,1,0:T(8,128)(2,1)}, bf16[2,2,1024,1024]{3,2,1,0:T(8,128)(2,1)}, bf16[2,768,2048]{2,1,0:T(8,128)(2,1)}, bf16[2,256,1024]{2,...) custom-call(bf16[2,1024,512]{2,1,0:T(8,128)(2,1)} %xa.5, ...), custom_call_target="tpu_custom_call" | custom-call | flops 23622320128 | bytes 41943040 | tf_op jit(solution)/shard_map/forward/pallas_call | solution.py:374
  120.3 1.1 slice_bitcast_fusion.2
  122.8 84.7 %middle.1 = (bf16[2,2,1024,512]{3,2,1,0:T(8,128)(2,1)}, bf16[2,2,1024,512]{3,2,1,0:T(8,128)(2,1)}, bf16[2,256,1024]{2,1,0:T(8,128)(2,1)}, bf16[2,256,1024]{2,1,0...) custom-call(bf16[2,2,1024,1024]{3,2,1,0:T(8,128)(2,1)} %get-tuple-el, ...), custom_call_target="tpu_custom_call" | custom-call | flops 57982058496 | bytes 83886080 | tf_op jit(solution)/shard_map/middle/pallas_call | solution.py:567
  207.5 1.9 dynamic-slice_bitcast_fusion
  209.3 29.9 %attend_back.2 = (bf16[768,1024]{1,0:T(8,128)(2,1)}, bf16[768,1024]{1,0:T(8,128)(2,1)}, f32[768,1]{1,0:T(8,128)}) custom-call(bf16[2,768,2048]{2,1,0:T(8,128)(2,1)} %get-tuple-element.73.triple, bf16[2,256,1024]{2,1,0:T(8,128)(2,1)} %get-tuple-element.89.grad_own, bf16[2,256,1024]{2,1,0:T(8,128)(2,1)} %get-tuple-element.77.grad_far, ...), custom_call_target="tpu_custom_call" | custom-call | flops 21474836480 | bytes 12582912 | tf_op jit(solution)/shard_map/attend_back/pallas_call | solution.py:661
  239.8 18.9 %last.2 = (bf16[2,1024,512]{2,1,0:T(8,128)(2,1)}, bf16[2,1024,512]{2,1,0:T(8,128)(2,1)}, f32[2,8,1024]{2,1,0:T(8,128)}, f32[768,1024]{1,0:T(8,128)}, f32[8,1024]{1,0:T(8,128)}) custom-call(bf16[768,1024]{1,0:T(8,128)(2,1)} %get-tuple-element.79.t_own, bf16[768,1024]{1,0:T(8,128)(2,1)} %get-tuple-element.80.t_far, ...), custom_call_target="tpu_custom_call" | custom-call | flops 6442450944 | bytes 20971520 | tf_op jit(solution)/shard_map/last/pallas_call | solution.py:768
  258.9 1.5 collective-permute-start.6
  263.4 1.6 collective-permute-start.5
  268.0 2.9 fusion.30
  270.9 41.7 %collective-permute-done.6 = bf16[4,288,1024]{2,1,0:T(8,128)(2,1)} collective-permute-done((bf16[4,288,1024]{2,1,0:T(8,128)(2,1)S(1)}, bf16[4,288,1024]{2,1,0:T(8,128)(2,1)}, u32[]{:S(2)}, u32[]{:S(2)}) %collective-permute-start.6) | collective-permute-done | bytes 2359328 | tf_op jit(solution)/shard_map/ppermute | solution.py:846
  312.6 3.4 convert_add_fusion
  316.0 2.1 copy-done.5
  318.2 1.3 fusion.32
  319.5 2.1 collective-permute-start.16
  321.6 2.4 collective-permute-start.18
  323.9 29.9 %attend_back.3 = (bf16[768,1024]{1,0:T(8,128)(2,1)}, bf16[768,1024]{1,0:T(8,128)(2,1)}, f32[768,1]{1,0:T(8,128)}) custom-call(bf16[2,768,2048]{2,1,0:T(8,128)(2,1)} %get-tuple-element.73.triple, bf16[2,256,1024]{2,1,0:T(8,128)(2,1)} %get-tuple-element.89.grad_own, bf16[2,256,1024]{2,1,0:T(8,128)(2,1)} %get-tuple-element.77.grad_far, ...), custom_call_target="tpu_custom_call" | custom-call | flops 21474836480 | bytes 12582912 | tf_op jit(solution)/shard_map/attend_back/pallas_call | solution.py:661
  353.9 19.3 %last.3 = (bf16[2,1024,512]{2,1,0:T(8,128)(2,1)}, bf16[2,1024,512]{2,1,0:T(8,128)(2,1)}, f32[2,8,1024]{2,1,0:T(8,128)}, bf16[8,96,1024]{2,1,0:T(8,128)(2,1)}, f32[8,1024]{1,0:T(8,128)}) custom-call(bf16[768,1024]{1,0:T(8,128)(2,1)} %get-tuple-element.90.t_own, bf16[768,1024]{1,0:T(8,128)(2,1)} %get-tuple-element.91.t_far, ...), custom_call_target="tpu_custom_call" | custom-call | flops 6442450944 | bytes 20971520 | tf_op jit(solution)/shard_map/last/pallas_call | solution.py:768
  373.1 0.9 slice_add_fusion
  375.1 17.7 %total.1 = f32[96,128]{1,0:T(8,128)} custom-call(f32[96,128]{1,0:T(8,128)} %maximum_bitcast_fusion.value), custom_call_target="tpu_custom_call" | custom-call | tf_op jit(solution)/shard_map/total/pallas_call | solution.py:827
  392.9 1.3 slice_bitcast_fusion.8
  394.3 0.9 add.280
  395.3 1.3 slice_bitcast_fusion.9
  398.0 1.2 collective-permute-done.10
  399.2 1.0 collective-permute-start.11
  400.9 1.1 collective-permute-start.3
  401.9 1.6 fusion.29
  403.7 15.6 %collective-permute-done.11 = bf16[4,96,1024]{2,1,0:T(8,128)(2,1)S(1)} collective-permute-done((bf16[4,96,1024]{2,1,0:T(8,128)(2,1)S(1)}, bf16[4,96,1024]{2,1,0:T(8,128)(2,1)S(1)}, u32[]{:S(2)}, u32[]{:S(2)}) %collective-permute-start.11) | collective-permute-done | bytes 786464 | tf_op jit(solution)/shard_map/ppermute | solution.py:846
  420.4 1.3 collective-permute-start.13
  421.7 3.7 fusion.25
  425.4 2.7 collective-permute-start.14
  428.1 1.3 fusion.31
  429.3 1.2 collective-permute-start.1
  430.5 0.8 collective-permute-start.8
  432.8 4.2 collective-permute-done.13
  437.7 1.2 collective-permute-done.20
  439.1 1.0 copy.45
  440.1 0.8 maximum_select_fusion.1
  441.0 1.8 fusion.36
  442.8 55.8 %collective-permute-done.8 = bf16[1024,512]{1,0:T(8,128)(2,1)} collective-permute-done((bf16[1024,512]{1,0:T(8,128)(2,1)}, bf16[1024,512]{1,0:T(8,128)(2,1)}, u32[]{:S(2)}, u32[]{:S(2)}) %collective-permute-start.8) | collective-permute-done | bytes 1048608 | tf_op jit(solution)/shard_map/ppermute | solution.py:842
  498.6 5.2 %fusion.14 = (f32[1,1024,512]{2,1,0:T(8,128)S(1)}, f32[1,1024,512]{2,1,0:T(8,128)S(1)}) fusion(bf16[1024,512]{1,0:T(8,128)(2,1)} %collective-permute-done.3, bf16[2,1024,512]{2,1,0:T(8,128)(2,1)} %collective-permute-done.2, f32[1024]{0:T(1024)} %bitcast.218, f32[1024]{0:T(1024)S(1)} %copy-done.21, f32[1024]{0:T(1024)} %bitcast.217, ...), kind=kLoop, calls=%fused_computation.29 | loop fusion | flops 15728640 | bytes 14712832 | tf_op jit(solution)/shard_map/stack | solution.py:983
  503.8 2.6 pad_maximum_fusion
  506.4 1.1 copy-done.8
  507.5 4.7 fusion.2
  (137 shorter events, 17.3 us)
Async XLA Ops:
  0.6 121.6 %copy-start = (f32[4096]{0:T(1024)S(1)}, f32[4096]{0:T(1024)}, u32[]{:S(2)}) copy-start(f32[4096]{0:T(1024)} %param.28) | copy-start | bytes 49156
  33.9 3.0 copy-start.15
  33.9 3.0 copy-start.16
  36.7 2.8 copy-start.30
  36.7 2.8 copy-start.31
  239.8 21.0 %copy-start.2 = (bf16[2,1024,512]{2,1,0:T(8,128)(2,1)S(1)}, bf16[2,1024,512]{2,1,0:T(8,128)(2,1)}, u32[]{:S(2)}) copy-start(bf16[2,1024,512]{2,1,0:T(8,128)(2,1)} %xa.5) | copy-start | bytes 6291460
  258.7 9.3 %collective-permute-start.2 = (bf16[2,1024,512]{2,1,0:T(8,128)(2,1)}, bf16[2,1024,512]{2,1,0:T(8,128)(2,1)}, u32[]{:S(2)}, u32[]{:S(2)}) collective-permute-start(bf16[2,1024,512]{2,1,0:T(8,128)(2,1)} %get-tuple-element.84), channel_id=1, source_target_pairs={{0,1},{1,0},{2,3},{3,2},{4,5},{5,4},{6,7},{7,6},{8,9},{9,8},{10,11... | collective-permute-start | bytes 6291464 | tf_op jit(solution)/shard_map/ppermute | solution.py:842
  258.9 53.7 %collective-permute-start.6 = (bf16[4,288,1024]{2,1,0:T(8,128)(2,1)S(1)}, bf16[4,288,1024]{2,1,0:T(8,128)(2,1)}, u32[]{:S(2)}, u32[]{:S(2)}) collective-permute-start(bf16[4,288,1024]{2,1,0:T(8,128)(2,1)S(1)} %dynamic-slice_bitcast_fusion), channel_id=1, source_target_pairs={{0,4},{4,0},{8,12},{12,8},{16,20},{20,16},{24,28},{28,24},{1,5},{5... | collective-permute-start | bytes 7077896 | tf_op jit(solution)/shard_map/ppermute | solution.py:846
  260.3 3.1 collective-permute-start.4
  260.5 159.9 %collective-permute-start = (bf16[2,2,1024,512]{3,2,1,0:T(8,128)(2,1)}, bf16[2,2,1024,512]{3,2,1,0:T(8,128)(2,1)}, u32[]{:S(2)}, u32[]{:S(2)}) collective-permute-start(bf16[2,2,1024,512]{3,2,1,0:T(8,128)(2,1)} %get-tuple-element.72), channel_id=1, source_target_pairs={{0,1},{1,0},{2,3},{3,2},{4,5},{5,4},{6,7},{7,6},{8,9},{9,8},{10,11... | collective-permute-start | bytes 12582920 | tf_op jit(solution)/shard_map/ppermute | solution.py:842
  261.2 3.9 copy-start.6
  262.1 3.4 copy-start.27
  262.1 3.5 copy-start.25
  262.1 3.5 copy-start.26
  263.4 4.0 collective-permute-start.5
  319.5 79.8 %collective-permute-start.16 = (bf16[288,1024]{1,0:T(8,128)(2,1)}, bf16[288,1024]{1,0:T(8,128)(2,1)S(1)}, u32[]{:S(2)}, u32[]{:S(2)}) collective-permute-start(bf16[288,1024]{1,0:T(8,128)(2,1)} %get-tuple-element.145), channel_id=1, source_target_pairs={{0,8},{4,12},{8,16},{12,20},{16,24},{20,28},{24,0},{28,4},{1,9},{5... | collective-permute-start | bytes 1769480 | tf_op jit(solution)/shard_map/ppermute | solution.py:850
  321.6 79.3 %collective-permute-start.17 = (bf16[288,1024]{1,0:T(8,128)(2,1)}, bf16[288,1024]{1,0:T(8,128)(2,1)S(1)}, u32[]{:S(2)}, u32[]{:S(2)}) collective-permute-start(bf16[288,1024]{1,0:T(8,128)(2,1)} %get-tuple-element.147), channel_id=1, source_target_pairs={{0,16},{4,20},{8,24},{12,28},{16,0},{20,4},{24,8},{28,12},{1,17},{... | collective-permute-start | bytes 1769480 | tf_op jit(solution)/shard_map/ppermute | solution.py:850
  321.6 80.4 %collective-permute-start.18 = (bf16[288,1024]{1,0:T(8,128)(2,1)}, bf16[288,1024]{1,0:T(8,128)(2,1)S(1)}, u32[]{:S(2)}, u32[]{:S(2)}) collective-permute-start(bf16[288,1024]{1,0:T(8,128)(2,1)} %get-tuple-element.146), channel_id=1, source_target_pairs={{0,24},{4,28},{8,0},{12,4},{16,8},{20,12},{24,16},{28,20},{1,25},{... | collective-permute-start | bytes 1769480 | tf_op jit(solution)/shard_map/ppermute | solution.py:850
  353.8 19.3 %copy-start.23 = (f32[8,1024]{1,0:T(8,128)S(1)}, f32[8,1024]{1,0:T(8,128)}, u32[]{:S(2)}) copy-start(f32[8,1024]{1,0:T(8,128)} %get-tuple-element.98) | copy-start | bytes 98308
  353.8 20.2 %copy-start.12 = (f32[768,1]{1,0:T(8,128)S(1)}, f32[768,1]{1,0:T(8,128)}, u32[]{:S(2)}) copy-start(f32[768,1]{1,0:T(8,128)} %get-tuple-element.100) | copy-start | bytes 9220
  353.8 20.2 %copy-start.13 = (f32[768,1]{1,0:T(8,128)S(1)}, f32[768,1]{1,0:T(8,128)}, u32[]{:S(2)}) copy-start(f32[768,1]{1,0:T(8,128)} %get-tuple-element.101) | copy-start | bytes 9220
  373.1 26.0 %copy-start.11 = (bf16[8,96,1024]{2,1,0:T(8,128)(2,1)S(1)}, bf16[8,96,1024]{2,1,0:T(8,128)(2,1)}, u32[]{:S(2)}) copy-start(bf16[8,96,1024]{2,1,0:T(8,128)(2,1)} %get-tuple-element.103) | copy-start | bytes 4718596
  392.8 1.5 collective-permute-start.9
  395.2 4.0 collective-permute-start.10
  399.2 26.2 %collective-permute-start.7 = (bf16[2,1024,512]{2,1,0:T(8,128)(2,1)}, bf16[2,1024,512]{2,1,0:T(8,128)(2,1)S(1)}, u32[]{:S(2)}, u32[]{:S(2)}) collective-permute-start(bf16[2,1024,512]{2,1,0:T(8,128)(2,1)} %get-tuple-element.96), channel_id=1, source_target_pairs={{0,1},{1,0},{2,3},{3,2},{4,5},{5,4},{6,7},{7,6},{8,9},{9,8},{10,11... | collective-permute-start | bytes 6291464 | tf_op jit(solution)/shard_map/ppermute | solution.py:842
  399.2 20.0 %collective-permute-start.11 = (bf16[4,96,1024]{2,1,0:T(8,128)(2,1)S(1)}, bf16[4,96,1024]{2,1,0:T(8,128)(2,1)S(1)}, u32[]{:S(2)}, u32[]{:S(2)}) collective-permute-start(bf16[4,96,1024]{2,1,0:T(8,128)(2,1)S(1)} %dynamic-slice_bitcast_fusion.1), channel_id=1, source_target_pairs={{0,4},{4,0},{8,12},{12,8},{16,20},{20,16},{24,28},{28,24},{1,5},{5... | collective-permute-start | bytes 2359304 | tf_op jit(solution)/shard_map/ppermute | solution.py:846
  400.9 41.9 %collective-permute-start.3 = (bf16[1024,512]{1,0:T(8,128)(2,1)}, bf16[1024,512]{1,0:T(8,128)(2,1)}, u32[]{:S(2)}, u32[]{:S(2)}) collective-permute-start(bf16[1024,512]{1,0:T(8,128)(2,1)} %fusion.30), channel_id=1, source_target_pairs={{0,2},{2,0},{1,3},{3,1},{4,6},{6,4},{5,7},{7,5},{8,10},{10,8},{9,1... | collective-permute-start | bytes 3145736 | tf_op jit(solution)/shard_map/ppermute | solution.py:842
  403.6 18.1 %copy-start.7 = (bf16[2,2,1024,512]{3,2,1,0:T(8,128)(2,1)S(1)}, bf16[2,2,1024,512]{3,2,1,0:T(8,128)(2,1)}, u32[]{:S(2)}) copy-start(bf16[2,2,1024,512]{3,2,1,0:T(8,128)(2,1)} %get-tuple-element.71) | copy-start | bytes 12582916
  403.6 25.7 %collective-permute-start.19 = (f32[4,8,512]{2,1,0:T(8,128)S(1)}, f32[4,8,512]{2,1,0:T(8,128)S(1)}, u32[]{:S(2)}, u32[]{:S(2)}) collective-permute-start(f32[4,8,512]{2,1,0:T(8,128)S(1)} %get-tuple-element.164), channel_id=1, source_target_pairs={{0,1},{1,0},{2,3},{3,2},{4,5},{5,4},{6,7},{7,6},{8,9},{9,8},{10,11... | collective-permute-start | bytes 196616 | tf_op jit(solution)/shard_map/ppermute | solution.py:842
  419.7 10.9 %collective-permute-start.12 = (bf16[96,1024]{1,0:T(8,128)(2,1)S(1)}, bf16[96,1024]{1,0:T(8,128)(2,1)S(1)}, u32[]{:S(2)}, u32[]{:S(2)}) collective-permute-start(bf16[96,1024]{1,0:T(8,128)(2,1)S(1)} %get-tuple-element.150), channel_id=1, source_target_pairs={{0,8},{4,12},{8,16},{12,20},{16,24},{20,28},{24,0},{28,4},{1,9},{5... | collective-permute-start | bytes 589832 | tf_op jit(solution)/shard_map/ppermute | solution.py:850
  420.4 16.6 %collective-permute-start.13 = (bf16[96,1024]{1,0:T(8,128)(2,1)S(1)}, bf16[96,1024]{1,0:T(8,128)(2,1)S(1)}, u32[]{:S(2)}, u32[]{:S(2)}) collective-permute-start(bf16[96,1024]{1,0:T(8,128)(2,1)S(1)} %get-tuple-element.152), channel_id=1, source_target_pairs={{0,16},{4,20},{8,24},{12,28},{16,0},{20,4},{24,8},{28,12},{1,17},{... | collective-permute-start | bytes 589832 | tf_op jit(solution)/shard_map/ppermute | solution.py:850
  421.7 6.3 %copy-start.9 = (bf16[2,1024,512]{2,1,0:T(8,128)(2,1)S(1)}, bf16[2,1024,512]{2,1,0:T(8,128)(2,1)}, u32[]{:S(2)}) copy-start(bf16[2,1024,512]{2,1,0:T(8,128)(2,1)} %get-tuple-element.95) | copy-start | bytes 6291460
  425.4 6.8 %copy-start.10 = (bf16[2,1024,512]{2,1,0:T(8,128)(2,1)}, bf16[2,1024,512]{2,1,0:T(8,128)(2,1)S(1)}, u32[]{:S(2)}) copy-start(bf16[2,1024,512]{2,1,0:T(8,128)(2,1)S(1)} %collective-permute-done.7) | copy-start | bytes 6291460
  425.4 11.6 %collective-permute-start.14 = (bf16[96,1024]{1,0:T(8,128)(2,1)S(1)}, bf16[96,1024]{1,0:T(8,128)(2,1)S(1)}, u32[]{:S(2)}, u32[]{:S(2)}) collective-permute-start(bf16[96,1024]{1,0:T(8,128)(2,1)S(1)} %get-tuple-element.151), channel_id=1, source_target_pairs={{0,24},{4,28},{8,0},{12,4},{16,8},{20,12},{24,16},{28,20},{1,25},{... | collective-permute-start | bytes 589832 | tf_op jit(solution)/shard_map/ppermute | solution.py:850
  429.3 77.1 %collective-permute-start.1 = (bf16[2,1024,512]{2,1,0:T(8,128)(2,1)}, bf16[2,1024,512]{2,1,0:T(8,128)(2,1)}, u32[]{:S(2)}, u32[]{:S(2)}) collective-permute-start(bf16[2,1024,512]{2,1,0:T(8,128)(2,1)} %fusion.25), channel_id=1, source_target_pairs={{0,2},{2,0},{1,3},{3,1},{4,6},{6,4},{5,7},{7,5},{8,10},{10,8},{9,1... | collective-permute-start | bytes 6291464 | tf_op jit(solution)/shard_map/ppermute | solution.py:842
  430.5 68.1 %collective-permute-start.8 = (bf16[1024,512]{1,0:T(8,128)(2,1)}, bf16[1024,512]{1,0:T(8,128)(2,1)}, u32[]{:S(2)}, u32[]{:S(2)}) collective-permute-start(bf16[1024,512]{1,0:T(8,128)(2,1)} %fusion.31), channel_id=1, source_target_pairs={{0,2},{2,0},{1,3},{3,1},{4,6},{6,4},{5,7},{7,5},{8,10},{10,8},{9,1... | collective-permute-start | bytes 3145736 | tf_op jit(solution)/shard_map/ppermute | solution.py:842
  437.0 3.1 collective-permute-start.21
  437.0 1.9 collective-permute-start.20
  437.7 60.9 %copy-start.3 = (bf16[2,1024,512]{2,1,0:T(8,128)(2,1)S(1)}, bf16[2,1024,512]{2,1,0:T(8,128)(2,1)}, u32[]{:S(2)}) copy-start(bf16[2,1024,512]{2,1,0:T(8,128)(2,1)} %xa.5) | copy-start | bytes 6291460
  437.7 60.9 %copy-start.18 = (f32[1024]{0:T(1024)S(1)}, f32[1024]{0:T(1024)}, u32[]{:S(2)}) copy-start(f32[1024]{0:T(1024)} %get-tuple-element.143) | copy-start | bytes 12292
  437.7 60.9 %copy-start.19 = (f32[1024]{0:T(1024)S(1)}, f32[1024]{0:T(1024)}, u32[]{:S(2)}) copy-start(f32[1024]{0:T(1024)} %get-tuple-element.144) | copy-start | bytes 12292
  437.7 60.9 %copy-start.20 = (f32[1024]{0:T(1024)S(1)}, f32[1024]{0:T(1024)}, u32[]{:S(2)}) copy-start(f32[1024]{0:T(1024)} %get-tuple-element.174) | copy-start | bytes 12292
  437.7 60.9 %copy-start.21 = (f32[1024]{0:T(1024)S(1)}, f32[1024]{0:T(1024)}, u32[]{:S(2)}) copy-start(f32[1024]{0:T(1024)} %get-tuple-element.175) | copy-start | bytes 12292
  438.9 2.0 collective-permute-start.15
  503.8 3.7 copy-start.8
  503.8 3.7 copy-start.24
  506.4 5.8 %copy-start.22 = (f32[1024]{0:T(1024)S(1)}, f32[1024]{0:T(1024)}, u32[]{:S(2)}) copy-start(f32[1024]{0:T(1024)} %get-tuple-element.203) | copy-start | bytes 12292
  507.5 5.3 %copy-start.1 = (f32[4096]{0:T(1024)S(1)}, f32[4096]{0:T(1024)}, u32[]{:S(2)}) copy-start(f32[4096]{0:T(1024)} %param.28) | copy-start | bytes 49156
  (6 other events, 14.4 us)

commit v3 on v2

v3 whole, which is shorter than its diff:
```python
from functools import partial

import jax
import jax.numpy as jnp
import numpy as np
from jax import lax
from jax.experimental import pallas as pl
from jax.experimental.pallas import tpu as pltpu
from jax.sharding import PartitionSpec as P

D = 1024
HS = 64
ROT = 16
HALF = ROT // 2
EPSILON = 1e-05
MASKED = -1e30
NN = (((1,), (0,)), ((), ()))
NT = (((1,), (1,)), ((), ()))
TN = (((0,), (0,)), ((), ()))
VMEM_LIMIT = 56 << 20
F32 = jnp.float32
BF16 = jnp.bfloat16


def mm(a, b, dims):
    return lax.dot_general(a, b, dims, preferred_element_type=F32)


def params(**extra):
    return pltpu.CompilerParams(vmem_limit_bytes=VMEM_LIMIT, **extra)


def cost(flops, nbytes):
    return pl.CostEstimate(flops=int(flops), bytes_accessed=int(nbytes), transcendentals=0)


def whole(shape):
    return pl.BlockSpec(shape, lambda *_: (0,) * len(shape))


MESH = pl.DeviceIdType.MESH
ANYWHERE = pl.BlockSpec(memory_space=pl.ANY)


class Spot:
    def __init__(self):
        self.count = lax.axis_size("dp")
        self.depth = self.count // 2
        self.dp, self.row, self.col = (lax.axis_index(a) for a in ("dp", "row", "col"))
        self.z, self.x = self.dp // 2, self.dp % 2

    def along(self, steps):
        return ((self.z + steps) % self.depth) * 2 + self.x

    def device(self, which):
        return {
            "row": {"row": 1 - self.row},
            "col": {"col": 1 - self.col},
            "x": {"dp": self.z * 2 + (1 - self.x)},
            "right": {"dp": self.along(1)},
            "left": {"dp": self.along(self.depth - 1)},
        }[which]

    def greet(self, *names):
        barrier = pltpu.get_barrier_semaphore()
        for name in names:
            pl.semaphore_signal(barrier, inc=1, device_id=self.device(name), device_id_type=MESH)
        pl.semaphore_wait(barrier, len(names))


def remote(spot, which, source, target, send, recv):
    return pltpu.make_async_remote_copy(
        src_ref=source, dst_ref=target, send_sem=send, recv_sem=recv,
        device_id=spot.device(which), device_id_type=MESH,
    )


class Gather:
    def __init__(self, spot, mine, theirs, all_ref, local, send, recv):
        self.spot, self.all = spot, all_ref
        wide = mine.shape[1]
        here = all_ref.at[spot.dp]
        depth = spot.depth
        self.local = pltpu.make_async_copy(mine, here.at[:, pl.ds(0, wide)], local)
        self.core = remote(spot, "col", theirs, here.at[:, pl.ds(wide, wide)], send.at[0], recv.at[0])
        self.ring, self.cross = [], []
        for k in range(depth):
            slot = all_ref.at[spot.along(depth - k)]
            self.cross.append(remote(spot, "x", slot, slot, send.at[1 + k], recv.at[1 + k]))
            if k < depth - 1:
                at = 1 + depth + k
                self.ring.append(remote(spot, "right", slot, slot, send.at[at], recv.at[at]))

    @staticmethod
    def sems(count):
        return pltpu.SemaphoreType.DMA((count,))

    def begin(self):
        self.local.start()
        self.core.start()

    def first(self):
        self.local.wait()
        self.core.wait_recv()
        self.ring[0].start()
        self.cross[0].start()

    def forward(self, k):
        self.ring[k - 1].wait_recv()
        if k < len(self.ring):
            self.ring[k].start()
        self.cross[k].start()

    def finish(self):
        for copy in self.cross:
            copy.wait_recv()
        for copy in (self.core, *self.ring, *self.cross):
            copy.wait_send()


def enter_kernel(mine, theirs, tokens, all_ref, xb, xc, xd, local, send, recv, y_send, y_recv, c_send, c_recv, *, chunks):
    spot = Spot()
    spot.greet("row", "col", "x", "right", "left")
    gather = Gather(spot, mine, theirs, all_ref, local, send, recv)
    size = xb.shape[0] // chunks
    part = lambda k: pl.ds(k * size, size)
    over_row = [
        remote(spot, "row", tokens.at[0, part(k)], xb.at[part(k)], y_send.at[k], y_recv.at[k]) for k in range(chunks)
    ]
    over_col = [
        remote(spot, "col", xb.at[part(k)], xd.at[part(k)], c_send.at[k], c_recv.at[k]) for k in range(chunks)
    ]
    core = remote(spot, "col", tokens, xc, c_send.at[chunks], c_recv.at[chunks])
    gather.begin()
    for copy in over_row:
        copy.start()
    gather.first()
    core.start()
    depth = spot.depth
    for k in range(max(depth - 1, chunks)):
        if k + 1 < depth:
            gather.forward(k + 1)
        if k < chunks:
            over_row[k].wait_recv()
            over_col[k].start()
    gather.finish()
    core.wait()
    for k in range(chunks):
        over_col[k].wait()
        over_row[k].wait_send()


def enter(mine, theirs, tokens, count, chunks=4):
    rows, wide = mine.shape
    micros, length, _ = tokens.shape
    depth = count // 2
    half = jax.ShapeDtypeStruct((length, wide), BF16)
    return pl.pallas_call(
        partial(enter_kernel, chunks=chunks),
        in_specs=[ANYWHERE] * 3,
        out_specs=[ANYWHERE] * 4,
        out_shape=[
            jax.ShapeDtypeStruct((count, rows, 2 * wide), BF16), half,
            jax.ShapeDtypeStruct(tokens.shape, BF16), half,
        ],
        scratch_shapes=[
            pltpu.SemaphoreType.DMA, Gather.sems(2 * depth), Gather.sems(2 * depth),
            Gather.sems(chunks), Gather.sems(chunks), Gather.sems(chunks + 1), Gather.sems(chunks + 1),
        ],
        compiler_params=pltpu.CompilerParams(collective_id=0, has_side_effects=True),
        name="enter",
    )(mine, theirs, tokens)


def forward_kernel(
    xa, xc, xb0, xd0, weight, bias, vectors, cosine, sine, mine, theirs, tokens, grads,
    plain, second, triple, att_own, att_far, logsum, all_ref, xb1, xd1, cb0, cc, cd0,
    x_s, first, q_s, v_s, o_s, n_s, f_s, local, send, recv, y_send, y_recv, c_send, c_recv, t_sem, l_sem, *, block, step,
):
    spot = Spot()
    now = pl.program_id(0)
    wide = xa.shape[2]
    width = 2 * wide
    own_tokens = tokens.shape[1]
    length = 2 * own_tokens
    blocks = own_tokens // block
    heads = weight.shape[0] // (3 * HS)
    depth = spot.depth
    attend0, far1, attend1 = 3 * blocks, 3 * blocks + heads, 4 * blocks + heads
    end = attend1 + heads - 1
    here, there = spot.row, 1 - spot.row

    gather = Gather(spot, mine, theirs, all_ref, local, send, recv)
    x_row = remote(spot, "row", tokens.at[1], xb1, y_send.at[0], y_recv.at[0])
    x_col = remote(spot, "col", xb1, xd1, c_send.at[0], c_recv.at[0])
    g_row = remote(spot, "row", grads.at[0], cb0, y_send.at[1], y_recv.at[1])
    g_col = remote(spot, "col", cb0, cd0, c_send.at[1], c_recv.at[1])
    g_core = remote(spot, "col", grads, cc, c_send.at[2], c_recv.at[2])
    load_near = pltpu.make_async_copy(xb1, n_s, l_sem.at[0])
    load_far = pltpu.make_async_copy(xd1, f_s, l_sem.at[1])
    keep = [pltpu.make_async_copy(q_s.at[m], triple.at[m], t_sem.at[m]) for m in range(2)]

    at = lambda k: pl.when(now == k)

    @at(0)
    def _():
        spot.greet("row", "col", "x", "right", "left")
        gather.begin()
        x_row.start()

    @at(1)
    def _():
        gather.first()
        g_core.start()

    moments = {1: attend0 + 1, 2: far1, 3: attend1 + 2} if depth == 4 else {}
    for k in range(1, depth):
        moment = moments.get(k, attend1 + 2)

        @at(moment)
        def _():
            gather.forward(k)

    @at(attend0 + 2)
    def _():
        x_row.wait_recv()
        x_col.start()
        g_row.start()

    @at(attend0 + 3)
    def _():
        x_col.wait_recv()
        load_near.start()
        load_far.start()

    @at(far1)
    def _():
        load_near.wait()
        load_far.wait()

    @at(end - 1)
    def _():
        g_row.wait_recv()
        g_col.start()

    @pl.when(now < 2 * blocks)
    def _():
        x_s[:, :wide] = xa[0]
        x_s[:, wide:] = xc[0]

    @pl.when((now >= 2 * blocks) & (now < attend0))
    def _():
        x_s[:, :wide] = xb0[...]
        x_s[:, wide:] = xd0[...]

    for k in range(blocks):
        @at(far1 + k)
        def _():
            x_s[:, :wide] = n_s[k * block : (k + 1) * block]
            x_s[:, wide:] = f_s[k * block : (k + 1) * block]

    project = (now < attend0) | ((now >= far1) & (now < attend1))

    @pl.when(project)
    def _():
        micro = jnp.where(now < blocks, 0, jnp.where(now < 2 * blocks, 1, jnp.where(now < attend0, 0, 1)))
        half = jnp.where(now < 2 * blocks, here, there)
        number = jnp.where(now < attend0, now % blocks, (now - far1) % blocks)
        lane = pl.ds(pl.multiple_of(half * own_tokens + number * block, block), block)
        values = x_s[...].astype(F32)
        center = jnp.sum(values, axis=1, keepdims=True) / width
        spread = jnp.sum(values * values, axis=1, keepdims=True) / width - center * center
        normed = (values - center) * lax.rsqrt(spread + EPSILON)
        plain[0, 0] = normed.astype(BF16)
        first[...] = (normed * vectors[0:1, :] + vectors[1:2, :]).astype(BF16)
        second[0, 0] = (normed * vectors[2:3, :] + vectors[3:4, :]).astype(BF16)
        cos, sin = cosine[:, lane], sine[:, lane]
        for head in range(heads):
            base = head * 3 * HS
            rows = mm(weight[base : base + 3 * HS, :], first[...], NT) + bias[base : base + 3 * HS, :]
            pieces = []
            for which in range(2):
                lo = which * HS
                scale = HS ** (-0.5) if which == 0 else 1.0
                u1, u2 = rows[lo : lo + HALF], rows[lo + HALF : lo + ROT]
                pieces += [(u1 * cos - u2 * sin) * scale, (u2 * cos + u1 * sin) * scale, rows[lo + ROT : lo + HS] * scale]
            pieces.append(rows[2 * HS :])
            q_s[micro, base : base + 3 * HS, lane] = jnp.concatenate(pieces, axis=0).astype(BF16)

    @at(attend0)
    def _():
        keep[0].start()

    @at(attend1)
    def _():
        keep[1].start()

    attending = ((now >= attend0) & (now < far1)) | (now >= attend1)

    @pl.when(attending)
    def _():
        micro = jnp.where(now < far1, 0, 1)
        head = jnp.where(now < far1, now - attend0, now - attend1)
        base = pl.multiple_of(head * 3 * HS, HS)
        query_of = lambda lo, hi: q_s[micro, pl.ds(base, HS), lo:hi]
        keys_of = lambda lo, hi: q_s[micro, pl.ds(pl.multiple_of(base + HS, HS), HS), lo:hi]
        v_s[0:HS, :] = q_s[micro, pl.ds(pl.multiple_of(base + 2 * HS, HS), HS), :]
        extra = lax.broadcasted_iota(jnp.int32, (16, length), 0)
        v_s[HS : HS + 16, :] = jnp.where(extra == 0, 1.0, 0.0).astype(BF16)
        allowed = causal_tile(step)
        for i in range(length // step):
            lo, hi = i * step, (i + 1) * step
            query = query_of(lo, hi)
            diag = jnp.where(allowed, mm(keys_of(lo, hi), query, TN), MASKED)
            highest = jnp.max(diag, axis=0, keepdims=True)
            if i:
                past = mm(keys_of(0, lo), query, TN)
                highest = jnp.maximum(highest, jnp.max(past, axis=0, keepdims=True))
            raised = jnp.exp(diag - highest).astype(BF16)
            result = mm(v_s[:, lo:hi], raised, NN)
            if i:
                raised = jnp.exp(past - highest).astype(BF16)
                result = result + mm(v_s[:, :lo], raised, NN)
            total = result[HS : HS + 1]
            o_s[:, lo:hi] = (result[:HS] / total).astype(BF16)
            logsum[0, 0, :, lo:hi] = highest + jnp.log(total)
        att_own[0] = o_s[:, lanes(here, own_tokens)]
        att_far[0] = o_s[:, lanes(there, own_tokens)]

    @at(end)
    def _():
        gather.finish()
        g_col.wait()
        g_core.wait()
        x_col.wait_send()
        x_row.wait_send()
        g_row.wait_send()
        keep[0].wait()
        keep[1].wait()


def lanes(index, tokens):
    return pl.ds(pl.multiple_of(index * tokens, tokens), tokens)


def forward(residual, xc, xb0, xd0, weight, bias, vectors, cosine, sine, mine, theirs, cotangent, count, block=512, step=512):
    micros, tokens, wide = residual.shape
    width, length = 2 * wide, 2 * tokens
    block, step = min(block, tokens), min(step, length)
    blocks = tokens // block
    rows = weight.shape[0]
    heads = rows // (3 * HS)
    depth = count // 2
    a0, f1, a1 = 3 * blocks, 3 * blocks + heads, 4 * blocks + heads
    steps = a1 + heads
    clip = lambda v, lo, hi: jnp.minimum(jnp.maximum(v, lo), hi)
    own = pl.BlockSpec((1, block, wide), lambda i: (jnp.where(i < blocks, 0, 1), jnp.where(i < 2 * blocks, i % blocks, blocks - 1), 0))
    far = pl.BlockSpec((block, wide), lambda i: (clip(i - 2 * blocks, 0, blocks - 1), 0))

    def place(i):
        late = i >= f1
        micro = jnp.where(i < blocks, 0, jnp.where(i < 2 * blocks, 1, jnp.where(late, 1, 0)))
        half = jnp.where(i < 2 * blocks, 1, 0)
        number = jnp.where(i < 2 * blocks, i % blocks, jnp.where(late, clip(i - f1, 0, blocks - 1), clip(i - 2 * blocks, 0, blocks - 1)))
        return micro, half, number, 0

    def head_of(i):
        late = i >= a1
        return jnp.where(late, 1, 0), jnp.where(late, i - a1, clip(i - a0, 0, heads - 1))

    normal = pl.BlockSpec((1, 1, block, width), place)
    att = pl.BlockSpec((1, HS, tokens), lambda i: (*head_of(i), 0))
    half = jax.ShapeDtypeStruct((tokens, wide), BF16)
    piece = mine.shape[0]
    return pl.pallas_call(
        partial(forward_kernel, block=block, step=step),
        grid=(steps,),
        in_specs=[
            own, own, far, far, whole(weight.shape), whole(bias.shape), whole(vectors.shape),
            whole(cosine.shape), whole(sine.shape), ANYWHERE, ANYWHERE, ANYWHERE, ANYWHERE,
        ],
        out_specs=[
            normal, normal, ANYWHERE, att, att, pl.BlockSpec((1, 1, 1, length), lambda i: (*head_of(i), 0, 0)),
            *[ANYWHERE] * 6,
        ],
        out_shape=[
            jax.ShapeDtypeStruct((micros, 2, tokens, width), BF16),
            jax.ShapeDtypeStruct((micros, 2, tokens, width), BF16),
            jax.ShapeDtypeStruct((micros, rows, length), BF16),
            jax.ShapeDtypeStruct((micros, heads * HS, tokens), BF16),
            jax.ShapeDtypeStruct((micros, heads * HS, tokens), BF16),
            jax.ShapeDtypeStruct((micros, heads, 1, length), F32),
            jax.ShapeDtypeStruct((count, piece, width), BF16),
            half, half, half, jax.ShapeDtypeStruct(cotangent.shape, BF16), half,
        ],
        scratch_shapes=[
            pltpu.VMEM((block, width), BF16),
            pltpu.VMEM((block, width), BF16),
            pltpu.VMEM((micros, rows, length), BF16),
            pltpu.VMEM((HS + 16, length), BF16),
            pltpu.VMEM((HS, length), BF16),
            pltpu.VMEM((tokens, wide), BF16),
            pltpu.VMEM((tokens, wide), BF16),
            pltpu.SemaphoreType.DMA, Gather.sems(2 * depth), Gather.sems(2 * depth),
            Gather.sems(2), Gather.sems(2), Gather.sems(3), Gather.sems(3), Gather.sems(2), Gather.sems(2),
        ],
        compiler_params=params(collective_id=1, has_side_effects=True),
        cost_estimate=cost(micros * length * width * rows * 2 + micros * heads * length * length * 256 * 2, 40 << 20),
        name="forward",
    )(residual, xc, xb0, xd0, weight, bias, vectors, cosine, sine, mine, theirs, residual, cotangent)
def causal_tile(size):
    keys = lax.broadcasted_iota(jnp.int32, (size, size), 0)
    places = lax.broadcasted_iota(jnp.int32, (size, size), 1)
    return keys <= places


def lanes(index, tokens):
    return pl.ds(pl.multiple_of(index * tokens, tokens), tokens)


POLY = (0.254829592, -0.284496736, 1.421413741, -1.453152027, 1.061405429)


def gelu_pair(value):
    magnitude = jnp.abs(value)
    t = 1.0 / (1.0 + magnitude * (0.3275911 * 0.5**0.5))
    bell = jnp.exp(value * value * -0.5)
    series = POLY[4]
    for term in (POLY[3], POLY[2], POLY[1], POLY[0]):
        series = series * t + term
    tail = 0.5 * series * t * bell
    cumulative = jnp.where(value >= 0.0, 1.0 - tail, tail)
    return value * cumulative, cumulative + value * bell * (1.0 / (2.0 * np.pi) ** 0.5)


def column_of(row):
    return jnp.transpose(jnp.broadcast_to(row, (128, row.shape[1])))[:, 0:1]


def middle_kernel(
    second, normed, ca, cc, cb0, cd0, att_own, att_far, pieces, wo, bias, vectors, out_bias, grads, x_fin,
    out, heads_own, heads_far, part, tiles, dvec, dbias, cb1, cd1,
    w1, w2, dw1, dw2, dwo, n_s, f_s, c_s, a_s, act_s, eg_s,
    near_f, near_o, other_f, other_o, cross_f, cross_o, y_s, moved,
    w_sem, l_sem, y_send, y_recv, c_send, c_recv, cf_send, cf_recv, co_send, co_recv, m_send, m_recv,
    *, block, chunk, out_part,
):
    spot = Spot()
    now = pl.program_id(0)
    wide = ca.shape[2]
    count, rows, width = pieces.shape
    hid = w1.shape[0] // count
    heads = wo.shape[0] // HS
    steps = ca_steps = grads.shape[1] // block
    end = 4 * steps
    micro, half, at = now // (2 * steps), (now // steps) % 2, now % steps
    g_row = remote(spot, "row", grads.at[1], cb1, y_send, y_recv)
    g_col = remote(spot, "col", cb1, cd1, c_send, c_recv)
    load_near = pltpu.make_async_copy(cb1, n_s, l_sem.at[0])
    load_far = pltpu.make_async_copy(cd1, f_s, l_sem.at[1])

    def over_core(which, m, i):
        k = m * steps + i
        if which == 0:
            return remote(spot, "col", other_f.at[m, i], cross_f.at[m, i], cf_send.at[k], cf_recv.at[k])
        return remote(spot, "col", other_o.at[m, i], cross_o.at[m, i], co_send.at[k], co_recv.at[k])

    def over_row(m, i):
        k = m * steps + i
        return remote(spot, "row", y_s.at[m, i], moved.at[m, i], m_send.at[k], m_recv.at[k])

    @pl.when(now == 0)
    def _():
        spot.greet("row", "col")
        g_row.start()
        lo = heads * out_part
        copies = []
        for p in range(count):
            here = slice(p * hid, (p + 1) * hid)
            copies.append(pltpu.make_async_copy(pieces.at[p, lo : lo + hid], w1.at[here], w_sem.at[2 * p]))
            copies.append(pltpu.make_async_copy(pieces.at[p, lo + hid :], w2.at[here], w_sem.at[2 * p + 1]))
        for copy in copies:
            copy.start()
        dw1[...] = jnp.zeros_like(dw1)
        dw2[...] = jnp.zeros_like(dw2)
        dwo[...] = jnp.zeros_like(dwo)
        dbias[...] = jnp.zeros_like(dbias)
        for copy in copies:
            copy.wait()

    @pl.when(now == 2 * steps - 2)
    def _():
        g_row.wait_recv()
        g_col.start()

    @pl.when(now == 2 * steps - 1)
    def _():
        g_col.wait_recv()
        load_near.start()
        load_far.start()

    @pl.when(now == 2 * steps)
    def _():
        load_near.wait()
        load_far.wait()

    before = now - 1

    @pl.when((now > 0) & ((before // steps) % 2 == 0) & (now < end))
    def _():
        m, i = before // (2 * steps), before % steps
        over_core(0, m, i).wait_recv()
        y_s[m, i] = (near_f[...] + cross_f[m, i].astype(F32)).astype(BF16)
        over_row(m, i).start()

    def finish(m, i):
        over_row(m, i).wait_recv()
        over_core(1, m, i).wait_recv()
        out[0] = (
            x_fin[0].astype(F32) + near_o[m, i].astype(F32) + cross_o[m, i].astype(F32)
            + moved[m, i].astype(F32) + out_bias[...]
        ).astype(BF16)

    @pl.when((now >= 2 * steps) & (now < 3 * steps))
    def _():
        finish(0, now - 2 * steps)

    @pl.when(now > 3 * steps)
    def _():
        finish(1, now - 3 * steps - 1)

    @pl.when((half == 0) & (now < steps))
    def _():
        c_s[:, :wide] = cb0[...]
        c_s[:, wide:] = cd0[...]

    @pl.when((half == 0) & (now >= 2 * steps) & (now < end))
    def _():
        here = pl.ds(pl.multiple_of(at * block, block), block)
        c_s[:, :wide] = n_s[here, :]
        c_s[:, wide:] = f_s[here, :]

    @pl.when((half == 1) & (now < end))
    def _():
        c_s[:, :wide] = ca[0]
        c_s[:, wide:] = cc[0]
        a_s[...] = att_own[0]

    @pl.when((half == 0) & (now < end))
    def _():
        a_s[...] = att_far[0]

    @pl.when(now < end)
    def _():
        hidden = w1.shape[0]
        for lo in range(0, hidden, chunk):
            hi = lo + chunk
            expanded = mm(second[0, 0], w1[lo:hi, :], NT) + bias[:, lo:hi]
            active, slope = gelu_pair(expanded)
            act_s[:, lo:hi] = active.astype(BF16)
            rounded = (mm(c_s[...], w2[lo:hi, :], NT) * slope).astype(BF16)
            eg_s[:, lo:hi] = rounded
            dbias[:, lo:hi] += jnp.sum(rounded.astype(F32), axis=0, keepdims=True)
        for lo in range(0, hidden, chunk):
            hi = lo + chunk
            dw2[lo:hi, :] += mm(act_s[:, lo:hi], c_s[...], TN)
            dw1[lo:hi, :] += mm(eg_s[:, lo:hi], normed[0, 0], TN)
        dwo[...] += mm(a_s[...], c_s[...], NN)
        near = mm(act_s[...], w2[:, :wide], NN) + mm(a_s[...], wo[:, :wide], TN)
        other = (mm(act_s[...], w2[:, wide:], NN) + mm(a_s[...], wo[:, wide:], TN)).astype(BF16)
        part[0, 0] = (mm(eg_s[...], w1[...], NN) * vectors[2:3, :]).astype(BF16)
        heads_grad = mm(wo[...], c_s[...], NT).astype(BF16)

        @pl.when(half == 0)
        def _():
            heads_far[0] = heads_grad
            near_f[...] = near
            other_f[micro, at] = other
            over_core(0, micro, at).start()

        @pl.when(half == 1)
        def _():
            heads_own[0] = heads_grad
            near_o[micro, at] = near.astype(BF16)
            other_o[micro, at] = other
            over_core(1, micro, at).start()

    @pl.when(now == end)
    def _():
        lo = heads * out_part
        summed = column_of(dbias[...])
        gain_grad = jnp.zeros((1, width), F32)
        bias_grad = jnp.zeros((1, width), F32)
        for p in range(count):
            here = slice(p * hid, (p + 1) * hid)
            small = [dwo[h * HS + p * out_part : h * HS + (p + 1) * out_part, :] for h in range(heads)]
            tiles[p, :lo] = jnp.concatenate(small, axis=0).astype(BF16)
            tiles[p, lo : lo + hid] = (dw1[here, :] * vectors[2:3, :] + summed[here] * vectors[3:4, :]).astype(BF16)
            tiles[p, lo + hid :] = dw2[here, :].astype(BF16)
            weight = w1[here, :].astype(F32)
            gain_grad += jnp.sum(weight * dw1[here, :], axis=0, keepdims=True)
            bias_grad += jnp.sum(weight * summed[here], axis=0, keepdims=True)
        dvec[0:1, :] = gain_grad
        dvec[1:2, :] = bias_grad
        g_row.wait_send()
        g_col.wait_send()
        for m in range(2):
            for i in range(steps):
                over_core(0, m, i).wait_send()
                over_core(1, m, i).wait_send()
                over_row(m, i).wait_send()


def middle(second, normed, residual, cotangent, cc, cb0, cd0, att_own, att_far, pieces, wo, bias, vectors, out_bias, block=256, chunk=256):
    micros, tokens, wide = cotangent.shape
    count, rows, width = pieces.shape
    block = min(block, tokens)
    steps = tokens // block
    hidden, head_rows = bias.shape[1], wo.shape[0]
    hid = hidden // count
    out_part = (rows - 2 * hid) * HS // head_rows
    end, top = steps - 1, 4 * steps - 1

    def place(s):
        s = jnp.minimum(s, top)
        return s // (2 * steps), (s // steps) % 2, s % steps

    def own_at(s):
        m, h, i = place(s)
        return m, h * i

    def far_at(s):
        m, h, i = place(s)
        return m, i * (1 - h) + end * h

    def finished(s):
        late = s > 3 * steps
        number = jnp.where(late, s - 3 * steps - 1, jnp.clip(s - 2 * steps, 0, end))
        return jnp.where(late, 1, 0), number, 0

    both = lambda n: pl.BlockSpec((1, 1, block, n), lambda s: (*place(s), 0))
    own = pl.BlockSpec((1, block, wide), lambda s: (*own_at(s), 0))
    far0 = pl.BlockSpec((block, wide), lambda s: (jnp.minimum(s, end), 0))
    cols_own = pl.BlockSpec((1, head_rows, block), lambda s: (own_at(s)[0], 0, own_at(s)[1]))
    cols_far = pl.BlockSpec((1, head_rows, block), lambda s: (far_at(s)[0], 0, far_at(s)[1]))
    fin = pl.BlockSpec((1, block, wide), finished)
    halves = jax.ShapeDtypeStruct((tokens, wide), BF16)
    stack = lambda dtype: pltpu.VMEM((micros, steps, block, wide), dtype)
    return pl.pallas_call(
        partial(middle_kernel, block=block, chunk=min(chunk, hidden), out_part=out_part),
        grid=(4 * steps + 1,),
        in_specs=[
            both(width), both(width), own, own, far0, far0, cols_own, cols_far, ANYWHERE, whole(wo.shape),
            whole(bias.shape), whole(vectors.shape), whole(out_bias.shape), ANYWHERE, fin,
        ],
        out_specs=[
            fin, cols_own, cols_far, both(width), whole(pieces.shape), whole((8, width)), whole(bias.shape),
            ANYWHERE, ANYWHERE,
        ],
        out_shape=[
            jax.ShapeDtypeStruct((micros, tokens, wide), BF16),
            jax.ShapeDtypeStruct((micros, head_rows, tokens), BF16),
            jax.ShapeDtypeStruct((micros, head_rows, tokens), BF16),
            jax.ShapeDtypeStruct((micros, 2, tokens, width), BF16),
            jax.ShapeDtypeStruct(pieces.shape, BF16),
            jax.ShapeDtypeStruct((8, width), F32),
            jax.ShapeDtypeStruct(bias.shape, F32),
            halves, halves,
        ],
        scratch_shapes=[
            pltpu.VMEM((hidden, width), BF16),
            pltpu.VMEM((hidden, width), BF16),
            pltpu.VMEM((hidden, width), F32),
            pltpu.VMEM((hidden, width), F32),
            pltpu.VMEM((head_rows, width), F32),
            pltpu.VMEM((tokens, wide), BF16),
            pltpu.VMEM((tokens, wide), BF16),
            pltpu.VMEM((block, width), BF16),
            pltpu.VMEM((head_rows, block), BF16),
            pltpu.VMEM((block, hidden), BF16),
            pltpu.VMEM((block, hidden), BF16),
            pltpu.VMEM((block, wide), F32), stack(BF16), stack(BF16), stack(BF16), stack(BF16), stack(BF16),
            stack(BF16), stack(BF16),
            Gather.sems(2 * count), Gather.sems(2),
            pltpu.SemaphoreType.DMA, pltpu.SemaphoreType.DMA, pltpu.SemaphoreType.DMA, pltpu.SemaphoreType.DMA,
            *[Gather.sems(micros * steps) for _ in range(6)],
        ],
        compiler_params=params(collective_id=2, has_side_effects=True),
        cost_estimate=cost(2 * micros * tokens * 2 * width * (6 * hidden + 3 * head_rows), 80 << 20),
        name="middle",
    )(
        second, normed, cotangent, cc, cb0, cd0, att_own, att_far, pieces, wo, bias, vectors, out_bias, cotangent,
        residual,
    )


class Scatter:
    def __init__(self, spot, tiles, own, rx, tx, rz, total, out, x_send, x_recv, z_send, z_recv, c_send, c_recv, local):
        self.spot, self.own, self.rx, self.tx, self.rz, self.total = spot, own, rx, tx, rz, total
        depth, wide = spot.depth, out.shape[2]
        self.order = [*range(1, depth), 0]
        self.cross, self.along = {}, {}
        for s in self.order:
            away = spot.along(s) + 1 - 2 * spot.x
            self.cross[s] = remote(spot, "x", tiles.at[away], rx.at[s], x_send.at[s], x_recv.at[s])
            if s:
                self.along[s] = pltpu.make_async_remote_copy(
                    src_ref=tx.at[s - 1], dst_ref=rz.at[s - 1], send_sem=z_send.at[s], recv_sem=z_recv.at[s],
                    device_id={"dp": spot.along(s)}, device_id_type=MESH,
                )
        self.core = remote(spot, "col", total.at[:, pl.ds(wide, wide)], out.at[spot.col], c_send, c_recv)
        self.keep = pltpu.make_async_copy(total.at[:, pl.ds(0, wide)], out.at[spot.col], local)

    def begin(self):
        for s in self.order:
            self.cross[s].start()

    def fold(self, s):
        self.cross[s].wait_recv()
        added = self.own(s).astype(F32) + self.rx[s].astype(F32)
        if s:
            self.tx[s - 1] = added.astype(BF16)
            self.along[s].start()
        else:
            self.total[...] = added

    def finish(self):
        added = self.total[...]
        for s in self.order[:-1]:
            self.along[s].wait_recv()
            added = added + self.rz[s - 1].astype(F32)
        self.total[...] = added
        self.core.start()
        self.keep.start()

    def close(self):
        self.core.wait()
        self.keep.wait()
        for s in self.order:
            self.cross[s].wait_send()
            if s:
                self.along[s].wait_send()


def back_kernel(
    triple, h_own, h_far, att_own, att_far, logsum, cosine, sine, normed, part, weight, vectors, tiles, early,
    x_fin, xc_fin, g_fin,
    grad_out, rest_out, dq_out, vec_out,
    g_s, delta_s, dq_s, dk_s, dv_s, t_s, total, bias_s,
    near_f, near_o, other_f, other_o, cross_f, cross_o, y_s, moved, sum_s, sum_r, ng_s, norm_s, inv_s,
    a_own, a_rx, a_tx, a_rz, a_total, b_tiles, b_rx, b_tx, b_rz, b_total, held, arrived,
    a_load, a_xs, a_xr, a_zs, a_zr, a_cs, a_cr, a_loc, b_xs, b_xr, b_zs, b_zr, b_cs, b_cr, b_loc,
    v_send, v_recv, cf_send, cf_recv, co_send, co_recv, m_send, m_recv, s_send, s_recv,
    *, block, wider, step,
):
    spot = Spot()
    now = pl.program_id(0)
    tokens, wide = h_own.shape[2], x_fin.shape[2]
    width, length = 2 * wide, 2 * tokens
    heads = weight.shape[0] // (3 * HS)
    steps = tokens // block
    count, depth = spot.count, spot.depth
    slow = length // wider
    d0 = heads
    l0 = d0 + slow
    b1 = l0 + 2 * steps
    d1 = b1 + heads
    l1 = d1 + slow
    e1 = l1 + 2 * steps
    end = e1 + steps
    here, there = spot.row, 1 - spot.row
    at_step = lambda k: pl.when(now == k)

    first_sum = Scatter(
        spot, tiles, lambda s: a_own[s], a_rx, a_tx, a_rz, a_total, rest_out,
        a_xs, a_xr, a_zs, a_zr, a_cs, a_cr, a_loc,
    )
    last_sum = Scatter(
        spot, b_tiles, lambda s: b_tiles[spot.along(s)], b_rx, b_tx, b_rz, b_total, dq_out,
        b_xs, b_xr, b_zs, b_zr, b_cs, b_cr, b_loc,
    )
    loads = [pltpu.make_async_copy(tiles.at[spot.along(s)], a_own.at[s], a_load.at[s]) for s in range(depth)]

    partners = [{"col": 1 - spot.col}, {"row": 1 - spot.row}, {"dp": spot.z * 2 + (1 - spot.x)}]
    stride = 1
    while stride < depth:
        other_z = spot.z + stride * (1 - 2 * ((spot.z // stride) % 2))
        partners.append({"dp": other_z * 2 + spot.x})
        stride *= 2
    hops = [
        pltpu.make_async_remote_copy(
            src_ref=held.at[k], dst_ref=arrived.at[k], send_sem=v_send.at[k], recv_sem=v_recv.at[k],
            device_id=partner, device_id_type=MESH,
        )
        for k, partner in enumerate(partners)
    ]

    def over_core(which, m, i):
        k = m * steps + i
        if which == 0:
            return remote(spot, "col", other_f.at[i], cross_f.at[m, i], cf_send.at[k], cf_recv.at[k])
        return remote(spot, "col", other_o.at[i], cross_o.at[m, i], co_send.at[k], co_recv.at[k])

    def over_row(m, i):
        k = m * steps + i
        return remote(spot, "row", y_s.at[m, i], moved.at[m, i], m_send.at[k], m_recv.at[k])

    def sums_over(m, i):
        k = m * steps + i
        return remote(spot, "col", sum_s.at[m, i], sum_r.at[m, i], s_send.at[k], s_recv.at[k])

    @at_step(0)
    def _():
        barrier = pltpu.get_barrier_semaphore()
        near = [{"col": 1 - spot.col}, {"row": 1 - spot.row}, {"dp": spot.z * 2 + (1 - spot.x)}]
        for device in near + [{"dp": spot.along(s)} for s in range(1, depth)]:
            pl.semaphore_signal(barrier, inc=1, device_id=device, device_id_type=MESH)
        pl.semaphore_wait(barrier, depth + 2)
        first_sum.begin()
        for load in loads:
            load.start()
        bias_s[...] = jnp.zeros_like(bias_s)

    @at_step(1)
    def _():
        for load in loads:
            load.wait()

    moments = {1: 2, 2: d0, 3: l0 + 4, 0: b1 + 1} if depth == 4 else {}
    for s in first_sum.order:
        @at_step(moments.get(s, b1 + 1))
        def _():
            first_sum.fold(s)

    @pl.when((now < d0) | ((now >= b1) & (now < d1)))
    def _():
        head = jnp.where(now < d0, now, now - b1)
        for grad, att, place in ((h_own, att_own, here), (h_far, att_far, there)):
            at = lanes(place, tokens)
            g_s[:, at] = grad[0]
            delta_s[:, at] = jnp.sum(grad[0].astype(F32) * att[0].astype(F32), axis=0, keepdims=True)
        q_s, k_s, v_s = (triple.at[0, i * HS : (i + 1) * HS] for i in range(3))
        dk_s[...] = jnp.zeros_like(dk_s)
        dv_s[...] = jnp.zeros_like(dv_s)
        allowed = causal_tile(step)
        for i in range(length // step):
            lo, hi = i * step, (i + 1) * step
            query, grad = q_s[:, lo:hi], g_s[:, lo:hi]
            base, delta = logsum[0, 0, :, lo:hi], delta_s[:, lo:hi]
            query_grad = None
            for begin, stop in ((0, lo), (lo, hi)):
                if stop == begin:
                    continue
                raised = jnp.exp(mm(k_s[:, begin:stop], query, TN) - base)
                if begin == lo:
                    raised = jnp.where(allowed, raised, 0.0)
                prob_grad = mm(v_s[:, begin:stop], grad, TN)
                score_grad = (raised * (prob_grad - delta)).astype(BF16)
                dv_s[:, begin:stop] += mm(grad, raised.astype(BF16), NT)
                dk_s[:, begin:stop] += mm(query, score_grad, NT)
                term = mm(k_s[:, begin:stop], score_grad, NN)
                query_grad = term if query_grad is None else query_grad + term
            dq_s[:, lo:hi] = query_grad * HS ** (-0.5)
        cos, sin = cosine[...], sine[...]
        pieces = []
        for ref in (dq_s, dk_s):
            g1, g2 = ref[0:HALF, :], ref[HALF:ROT, :]
            pieces += [g1 * cos + g2 * sin, g2 * cos - g1 * sin, ref[ROT:HS, :]]
        pieces.append(dv_s[...])
        rounded = jnp.concatenate(pieces, axis=0).astype(BF16)
        at = pl.ds(pl.multiple_of(head * 3 * HS, HS), 3 * HS)
        t_s[at, :] = rounded
        bias_s[at, :] += jnp.sum(rounded.astype(F32), axis=1, keepdims=True)

    @pl.when(((now >= d0) & (now < l0)) | ((now >= d1) & (now < l1)))
    def _():
        number = jnp.where(now < l0, now - d0, now - d1)
        half, at = number // (slow // 2), number % (slow // 2)
        place = jnp.where(half == 0, there, here)
        lane = pl.ds(pl.multiple_of(place * tokens + at * wider, wider), wider)
        term = mm(t_s[:, lane], normed[0, 0], NN)

        @at_step(d0)
        def _():
            total[...] = term

        @pl.when(now > d0)
        def _():
            total[...] += term

    @at_step(l1 - 1)
    def _():
        size = 3 * HS // count
        gain, shift = vectors[0:1, :], vectors[1:2, :]
        weights = weight[...].astype(F32)
        gain_grad = jnp.sum(weights * total[...], axis=0, keepdims=True)
        shift_grad = jnp.sum(weights * bias_s[...], axis=0, keepdims=True)
        total[...] = total[...] * gain + bias_s[...] * shift
        for p in range(count):
            small = [total[h * 3 * HS + p * size : h * 3 * HS + (p + 1) * size, :] for h in range(heads)]
            b_tiles[p] = jnp.concatenate(small, axis=0).astype(BF16)
        last_sum.begin()
        used = early.shape[0]
        part_rows = width // (2 * held.shape[2])
        lanes_here = held.shape[2]
        held[0] = jnp.zeros_like(held[0])
        held[0, 0:used, :] = early[...]
        at = used
        for vector in (gain_grad, shift_grad):
            for r in range(2 * part_rows):
                mirror = (r + part_rows) % (2 * part_rows)
                plain = vector[:, r * lanes_here : (r + 1) * lanes_here]
                turned = vector[:, mirror * lanes_here : (mirror + 1) * lanes_here]
                held[0, at : at + 1, :] = jnp.where(spot.col == 0, plain, turned)
                at += 1
        line = jnp.transpose(jnp.broadcast_to(bias_s[...], (bias_s.shape[0], 128)))[0:1, :]
        mine = spot.row * 2 + spot.col
        for h in range(4 * heads):
            k = h % heads
            values = line[:, k * 3 * HS : (k + 1) * 3 * HS]
            held[0, at : at + 1, 0 : 3 * HS] = jnp.where(mine == h // heads, values, 0.0)
            at += 1

    for k in range(len(hops) + 1):
        @at_step(l1 + k)
        def _():
            if k:
                hops[k - 1].wait_recv()
            if 0 < k < len(hops):
                held[k] = held[k - 1] + arrived[k - 1]
            if k < len(hops):
                hops[k].start()
            else:
                vec_out[...] = held[k - 1] + arrived[k - 1]

    @at_step(l1)
    def _():
        first_sum.finish()

    moments_b = {1: l1 + 3, 2: l1 + 5, 3: l1 + 7, 0: e1} if depth == 4 else {}
    for s in last_sum.order:
        @at_step(moments_b.get(s, e1))
        def _():
            last_sum.fold(s)

    @at_step(b1)
    def _():
        for i in range(steps):
            over_core(0, 0, i).wait_send()
            over_core(1, 0, i).wait_send()

    later = now >= b1
    lead = jnp.where(later, now - l1, now - l0)

    @pl.when((lead > 0) & (lead <= steps))
    def _():
        m, i = jnp.where(later, 1, 0), lead - 1
        over_core(0, m, i).wait_recv()
        y_s[m, i] = (near_f[...] + cross_f[m, i].astype(F32)).astype(BF16)
        over_row(m, i).start()

    trail = jnp.where(now >= e1, now - e1, now - l1)
    micro = jnp.where(now >= e1, 1, 0)

    @pl.when((trail > 0) & (trail <= steps))
    def _():
        i = trail - 1
        sums_over(micro, i).wait_recv()
        sums = (sum_s[micro, i] + sum_r[micro, i]) / width
        grad_out[0] = g_fin[0].astype(F32) + inv_s[...] * (ng_s[...] - sums[:, 0:1] - norm_s[...] * sums[:, 1:2])

    @pl.when((trail >= 0) & (trail < steps))
    def _():
        over_row(micro, trail).wait_recv()
        over_core(1, micro, trail).wait_recv()
        grad = near_o[trail] + cross_o[micro, trail].astype(F32) + moved[micro, trail].astype(F32)
        near_x, far_x = x_fin[0].astype(F32), xc_fin[0].astype(F32)
        center = jnp.sum(near_x + far_x, axis=1, keepdims=True) / width
        spread = jnp.sum(near_x * near_x + far_x * far_x, axis=1, keepdims=True) / width - center * center
        inv = lax.rsqrt(spread + EPSILON)
        normed_x = (near_x - center) * inv
        ng_s[...] = grad
        norm_s[...] = normed_x
        inv_s[...] = inv
        column = lax.broadcasted_iota(jnp.int32, (block, 128), 1)
        one = jnp.sum(grad, axis=1, keepdims=True)
        two = jnp.sum(grad * normed_x, axis=1, keepdims=True)
        sum_s[micro, trail] = jnp.where(column == 0, one, jnp.where(column == 1, two, 0.0))
        sums_over(micro, trail).start()

    @pl.when((lead >= 0) & (lead < 2 * steps))
    def _():
        m, half, i = jnp.where(later, 1, 0), lead // steps, lead % steps
        place = jnp.where(half == 0, there, here)
        lane = pl.ds(pl.multiple_of(place * tokens + i * block, block), block)
        turned = t_s[:, lane]
        near = mm(turned, weight[:, :wide], TN) * vectors[0:1, :wide] + part[0, 0, :, :wide].astype(F32)
        other = mm(turned, weight[:, wide:], TN) * vectors[0:1, wide:] + part[0, 0, :, wide:].astype(F32)

        @pl.when(half == 0)
        def _():
            near_f[...] = near
            other_f[i] = other.astype(BF16)
            over_core(0, m, i).start()

        @pl.when(half == 1)
        def _():
            near_o[i] = near
            other_o[i] = other.astype(BF16)
            over_core(1, m, i).start()

    @at_step(end)
    def _():
        last_sum.finish()
        first_sum.close()
        for k in hops:
            k.wait_send()
        for i in range(steps):
            over_core(0, 1, i).wait_send()
            over_core(1, 1, i).wait_send()
            for m in range(2):
                over_row(m, i).wait_send()
                sums_over(m, i).wait_send()
        last_sum.close()


def backward(
    triple, h_own, h_far, att_own, att_far, logsum, cosine, sine, normed, part, weight, vectors, tiles, early,
    residual, xc, cotangent, block=256, wider=512, step=256,
):
    micros, rows, length = triple.shape
    tokens, wide = length // 2, residual.shape[2]
    width = 2 * wide
    heads = rows // (3 * HS)
    block, wider, step = min(block, tokens), min(wider, tokens), min(step, length)
    steps, slow = tokens // block, length // wider
    count, piece = tiles.shape[:2]
    depth = count // 2
    small = rows // count
    d0 = heads
    l0 = d0 + slow
    b1 = l0 + 2 * steps
    d1 = b1 + heads
    l1 = d1 + slow
    e1 = l1 + 2 * steps
    head_of = lambda s: (jnp.where(s >= b1, 1, 0), jnp.where(s >= b1, jnp.minimum(s - b1, heads - 1), jnp.minimum(s, heads - 1)))

    def slow_at(s):
        late = s >= b1
        number = jnp.clip(jnp.where(late, s - d1, s - d0), 0, slow - 1)
        return jnp.where(late, 1, 0), number // (slow // 2), number % (slow // 2), 0

    def part_at(s):
        late = s >= b1
        number = jnp.clip(jnp.where(late, s - l1, s - l0), 0, 2 * steps - 1)
        return jnp.where(late, 1, 0), number // steps, number % steps, 0

    def in_at(s):
        late = s > l1 + steps
        return jnp.where(late, 1, 0), jnp.clip(jnp.where(late, s - e1, s - l1), 0, steps - 1), 0

    def out_at(s):
        late = s > l1 + steps
        return jnp.where(late, 1, 0), jnp.clip(jnp.where(late, s - e1 - 1, s - l1 - 1), 0, steps - 1), 0

    narrow = pl.BlockSpec((1, HS, tokens), lambda s: (*head_of(s), 0))
    fin_in = pl.BlockSpec((1, block, wide), in_at)
    fin_out = pl.BlockSpec((1, block, wide), out_at)
    hops = 3 + max(depth - 1, 0).bit_length()
    vec_rows = early.shape[0] + 2 * (width // early.shape[1]) + 4 * heads
    pair = lambda dtype: pltpu.VMEM((micros, steps, block, wide), dtype)
    single = lambda dtype: pltpu.VMEM((steps, block, wide), dtype)
    sems, one = Gather.sems, pltpu.SemaphoreType.DMA
    return pl.pallas_call(
        partial(back_kernel, block=block, wider=wider, step=step),
        grid=(e1 + steps + 1,),
        in_specs=[
            pl.BlockSpec((1, 3 * HS, length), lambda s: (*head_of(s), 0)), narrow, narrow, narrow, narrow,
            pl.BlockSpec((1, 1, 1, length), lambda s: (*head_of(s), 0, 0)), whole(cosine.shape), whole(sine.shape),
            pl.BlockSpec((1, 1, wider, width), slow_at), pl.BlockSpec((1, 1, block, width), part_at),
            whole(weight.shape), whole(vectors.shape), ANYWHERE, whole(early.shape), fin_in, fin_in, fin_out,
        ],
        out_specs=[fin_out, ANYWHERE, ANYWHERE, whole((vec_rows, early.shape[1]))],
        out_shape=[
            jax.ShapeDtypeStruct((micros, tokens, wide), F32),
            jax.ShapeDtypeStruct((2, piece, wide), F32),
            jax.ShapeDtypeStruct((2, small, wide), F32),
            jax.ShapeDtypeStruct((vec_rows, early.shape[1]), F32),
        ],
        scratch_shapes=[
            pltpu.VMEM((HS, length), BF16),
            pltpu.VMEM((1, length), F32),
            pltpu.VMEM((HS, length), F32),
            pltpu.VMEM((HS, length), F32),
            pltpu.VMEM((HS, length), F32),
            pltpu.VMEM((rows, length), BF16),
            pltpu.VMEM((rows, width), F32),
            pltpu.VMEM((rows, 1), F32),
            pltpu.VMEM((block, wide), F32), single(F32), single(BF16), single(BF16), pair(BF16), pair(BF16),
            pair(BF16), pair(BF16),
            pltpu.VMEM((micros, steps, block, 128), F32), pltpu.VMEM((micros, steps, block, 128), F32),
            pltpu.VMEM((block, wide), F32), pltpu.VMEM((block, wide), F32), pltpu.VMEM((block, 1), F32),
            pltpu.VMEM((depth, piece, width), BF16), pltpu.VMEM((depth, piece, width), BF16),
            pltpu.VMEM((depth - 1, piece, width), BF16), pltpu.VMEM((depth - 1, piece, width), BF16),
            pltpu.VMEM((piece, width), F32),
            pltpu.VMEM((count, small, width), BF16), pltpu.VMEM((depth, small, width), BF16),
            pltpu.VMEM((depth - 1, small, width), BF16), pltpu.VMEM((depth - 1, small, width), BF16),
            pltpu.VMEM((small, width), F32),
            pltpu.VMEM((hops, vec_rows, early.shape[1]), F32), pltpu.VMEM((hops, vec_rows, early.shape[1]), F32),
            sems(depth), sems(depth), sems(depth), sems(depth), sems(depth), one, one, one,
            sems(depth), sems(depth), sems(depth), sems(depth), one, one, one,
            sems(hops), sems(hops), *[sems(micros * steps) for _ in range(8)],
        ],
        compiler_params=params(collective_id=3, has_side_effects=True),
        cost_estimate=cost(micros * (heads * length * length * 256 * 5 + length * width * 4 * rows), 100 << 20),
        name="backward",
    )(
        triple, h_own, h_far, att_own, att_far, logsum, cosine, sine, normed, part, weight, vectors, tiles, early,
        residual, xc, cotangent,
    )


def pick(value, index, axis=0):
    return lax.dynamic_index_in_dim(value, index, axis, keepdims=False)


def body(
    residual, attend_norm_gain, attend_norm_bias, expand_norm_gain, expand_norm_bias,
    attend_weight, attend_bias, output_weight, output_bias, expand_weight, expand_bias,
    shrink_weight, shrink_bias, cotangent,
):
    count = lax.axis_size("dp")
    row, col = lax.axis_index("row"), lax.axis_index("col")
    micros, tokens, wide = residual.shape
    width, length = 2 * wide, 2 * tokens
    heads = attend_weight.shape[1] // 2
    head_part, out_part = attend_weight.shape[2], output_weight.shape[1]
    hid = expand_weight.shape[1] // 2

    def sides(rows):
        return pick(rows, col), pick(rows, 1 - col)

    head_mine, head_theirs = sides(attend_weight.transpose(1, 2, 0).reshape(2, heads * head_part, wide))
    rest_mine, rest_theirs = sides(
        jnp.concatenate(
            [
                output_weight.reshape(2, heads * out_part, wide),
                expand_weight.T.reshape(2, hid, wide),
                shrink_weight.reshape(2, hid, wide),
            ],
            axis=1,
        )
    )
    head_all, xb0, xc, xd0 = enter(head_mine, head_theirs, residual, count)
    wq = head_all.reshape(count, heads, head_part, width).transpose(1, 0, 2, 3).reshape(heads * 3 * HS, width)

    vectors = jnp.stack([attend_norm_gain, attend_norm_bias, expand_norm_gain, expand_norm_bias])
    vectors = jnp.concatenate([jnp.roll(vectors, -col * wide, axis=1), jnp.zeros((4, width), F32)])
    head_begin = row * 2 * heads + col * heads
    bias_q = lax.dynamic_slice_in_dim(attend_bias, head_begin, heads, 0).reshape(-1, 1)
    bias_1 = pick(expand_bias.reshape(count, 4, hid), row * 2 + col, 1).reshape(1, -1)
    out_bias = lax.dynamic_slice_in_dim(output_bias + shrink_bias, col * wide, wide, 0).reshape(1, -1)
    powers = 10000.0 ** (-np.arange(HALF) * (2.0 / ROT))
    angles = powers[:, None] * np.arange(length)[None, :]
    cosine, sine = jnp.asarray(np.cos(angles), F32), jnp.asarray(np.sin(angles), F32)

    normed, second, triple, att_own, att_far, logsum, pieces, xb1, xd1, cb0, cc, cd0 = forward(
        residual, xc, xb0, xd0, wq, bias_q, vectors, cosine, sine, rest_mine, rest_theirs, cotangent, count
    )
    lo = heads * out_part
    wo = pieces[:, :lo].reshape(count, heads, out_part, width).transpose(1, 0, 2, 3).reshape(heads * HS, width)
    outputs, h_own, h_far, part, tiles, dvec, db1, _, _ = middle(
        second, normed, residual, cotangent, cc, cb0, cd0, att_own, att_far, pieces, wo, bias_1, vectors, out_bias
    )

    dout = jnp.sum(cotangent.astype(F32), axis=(0, 1))
    dout = lax.dynamic_update_slice_in_dim(jnp.zeros((width,), F32), dout, col * wide, 0)
    dvec = jnp.roll(dvec[:2], col * wide, axis=1)
    db1 = lax.dynamic_update_slice_in_dim(
        jnp.zeros((count, 4, hid), F32), db1.reshape(count, 1, hid), row * 2 + col, 1
    )
    lane = 256
    early = jnp.concatenate([db1.reshape(-1, lane), dout.reshape(-1, lane), dvec.reshape(-1, lane)])
    early = jnp.pad(early, ((0, -early.shape[0] % 8), (0, 0)))

    grads, rest_sum, dq_sum, vec = backward(
        triple, h_own, h_far, att_own, att_far, logsum, cosine, sine, normed, part, wq, vectors, tiles, early,
        residual, xc, cotangent,
    )
    attend_weight_grad = dq_sum.reshape(2 * heads, head_part, wide).transpose(2, 0, 1)
    output_weight_grad = rest_sum[:, :lo].reshape(2 * heads, out_part, wide)
    expand_weight_grad = rest_sum[:, lo : lo + hid].reshape(2 * hid, wide).T
    shrink_weight_grad = rest_sum[:, lo + hid :].reshape(2 * hid, wide)

    n1, nw, ne = db1.size // lane, width // lane, early.shape[0]
    cut = lambda at, rows: vec[at : at + rows].reshape(-1)
    dout = cut(n1, nw)
    return (
        outputs, grads, cut(ne, nw), cut(ne + nw, nw), cut(n1 + nw, nw), cut(n1 + 2 * nw, nw),
        attend_weight_grad, vec[ne + 2 * nw :, : 3 * HS], output_weight_grad, dout, expand_weight_grad, cut(0, n1),
        shrink_weight_grad, dout,
    )


def solution(mesh):
    tokens = P(None, ("dp", "row"), "col")
    weights = (P("col", "row", "dp"), P("row", "dp", "col"), P("col", ("dp", "row")), P(("dp", "row"), "col"))
    one = P()
    in_specs = (tokens, one, one, one, one, weights[0], one, weights[1], one, weights[2], one, weights[3], one, tokens)
    out_specs = (tokens, tokens, one, one, one, one, weights[0], one, weights[1], one, weights[2], one, weights[3], one)
    return jax.shard_map(body, mesh=mesh, in_specs=in_specs, out_specs=out_specs, check_vma=False)
```

time: 523 us -> 380 us (0.73); the launches traced: 513 us -> 380 us
  waiting for transfers between devices: 120 us -> 0 us
  Pallas kernels: 312 us -> 349 us
  other arithmetic: 35.5 us -> 1.91 us
  starting transfers between devices: 18 us -> 0 us
    ppermute x22 -> x0, waiting for transfers between devices: 120 us -> none  [the longest x14 59 us: swap(): return lax.ppermute(value, axis, [(0, 1), (1, 0)])]
    pallas_call x5 -> x1, Pallas kernels: 116 us -> 137 us  [backward(): pl.pallas_call(partial(back_kernel, block=block, wider=wider, step=step),...]
    pallas_call x1, Pallas kernels: 84.7 us -> 104 us  [middle(): pl.pallas_call(partial(middle_kernel, block=block, chunk=min(chunk, hidde...]
    ppermute x22 -> x0, starting transfers between devices: 18 us -> none  [the longest x6 9.25 us: shifted(): lax.ppermute(value, 'dp', [(i, (i + 2 * steps) % count) for i in range(co...]
    convert_element_type x4 -> x0, other arithmetic: 12.5 us -> none  [the longest x1 4.71 us: body(): outputs = (residual.astype(F32) + near[:, 1].astype(F32) + crossed[:, 1]....]
    another operation x2 -> x0, other arithmetic: 7.76 us -> none  [body(): jnp.stack([grad_0, grad_1])]
    add x10 -> x0, other arithmetic: 7.33 us -> none  [the longest x1 3.41 us: body(): kept = pick(tiles, place_x, 1).astype(F32) + tiles_back.astype(F32)]
  transfers between devices with their start and end apart: 22 -> 0, of which waited for: 8 -> 0; matrix products, arithmetic and copies ran while one was open for 8% -> 0% of each run, Pallas kernels for 13% -> 0%
where the time goes in v3:
time: 380 us
  Pallas kernels  349 us (92%)
  local copies, waits for them, and re-layouts  27.7 us (7%)
    pallas_call x1, Pallas kernels, backward(): pl.pallas_call(partial(back_kernel, block=block, wider=wider, step=step),...  137 us
    pallas_call x1, Pallas kernels, middle(): pl.pallas_call(partial(middle_kernel, block=block, chunk=min(chunk, hidde...  104 us
    pallas_call x1, Pallas kernels, forward(): pl.pallas_call(partial(forward_kernel, block=block, step=step), grid=(ste...  77.4 us
    pallas_call x1, Pallas kernels, enter(): pl.pallas_call(partial(enter_kernel, chunks=chunks), in_specs=[ANYWHERE]...  31.6 us
    unnamed x38, local copies, waits for them, and re-layouts  9.37 us

profile of v3, /device:TPU:0, one launch (start us, length us, event | category | flops | bytes accessed | tf_op | source)
XLA Modules:
  0.0 379.9 jit_solution(17979253555940832759)
XLA Ops:
  0.6 0.0 copy-start
  0.7 0.9 fusion.3
  1.6 0.6 concatenate.18.vectors
  2.2 1.6 dynamic-slice_bitcast_fusion.2
  3.8 31.6 %enter.1 = (bf16[8,96,1024]{2,1,0:T(8,128)(2,1)}, bf16[1024,512]{1,0:T(8,128)(2,1)}, bf16[2,1024,512]{2,1,0:T(8,128)(2,1)}, bf16[1024,512]{1,0:T(8,128)(2,1)}) custom-call(bf16[96,512]{1,0:T(8,128)(2,1)} %get-tuple-element.69.mine, bf16[96,512]{1,0:T(8,128)(2,1)} %get-tuple-element.68.theirs, bf16[2,1024,512]{2,1,0:T(8,128)(2,1)} %x_fin.3), custom_call_target="tpu_custom_call" | custom-call | tf_op jit(solution)/shard_map/enter/pallas_call | solution.py:158
  35.5 0.0 copy-start.6
  35.5 0.0 copy-start.7
  35.5 0.0 copy-start.8
  35.5 2.8 copy.35
  38.3 0.0 copy-done.6
  38.3 0.1 copy.41
  38.4 0.0 copy-done.7
  38.4 0.0 copy-done.8
  38.5 0.9 dynamic-slice_bitcast_fusion
  39.3 0.7 constant_dynamic-slice_fusion
  40.0 1.0 reshape.133.bias
  41.1 77.4 %forward.1 = (bf16[2,2,1024,1024]{3,2,1,0:T(8,128)(2,1)}, bf16[2,2,1024,1024]{3,2,1,0:T(8,128)(2,1)}, bf16[2,768,2048]{2,1,0:T(8,128)(2,1)}, bf16[2,256,1024]{2,...) custom-call(bf16[2,1024,512]{2,1,0:T(8,128)(2,1)} %x_fin.3, ...), custom_call_target="tpu_custom_call" | custom-call | flops 23622320128 | bytes 41943040 | tf_op jit(solution)/shard_map/forward/pallas_call | solution.py:375
  118.5 0.0 copy-start.11
  118.5 0.0 copy-start.12
  118.5 1.1 slice_bitcast_fusion
  119.6 0.8 copy.38
  120.5 0.0 copy-done.11
  120.5 0.7 dynamic_slice.39
  121.1 0.0 copy-done
  121.1 0.6 dynamic-slice_bitcast_fusion.4.bias
  121.7 103.7 %middle.1 = (bf16[2,1024,512]{2,1,0:T(8,128)(2,1)}, bf16[2,256,1024]{2,1,0:T(8,128)(2,1)}, bf16[2,256,1024]{2,1,0:T(8,128)(2,1)}, bf16[2,2,1024,1024]{3,2,1,0:T(...) custom-call(bf16[2,2,1024,1024]{3,2,1,0:T(8,128)(2,1)} %get-tuple-el, ...), custom_call_target="tpu_custom_call" | custom-call | flops 57982058496 | bytes 83886080 | tf_op jit(solution)/shard_map/middle/pallas_call | solution.py:649
  225.5 0.8 slice.37
  226.3 0.7 dynamic_update_slice.6
  227.0 0.3 convert_reduce_fusion
  227.4 0.5 dynamic_update_slice.7
  227.9 0.6 select_maximum_fusion.early
  228.5 136.7 %backward.1 = (f32[2,1024,512]{2,1,0:T(8,128)}, f32[2,288,512]{2,1,0:T(8,128)}, f32[2,96,512]{2,1,0:T(8,128)}, f32[56,256]{1,0:T(8,128)}) custom-call(bf16[2,768,2048]{2,1,0:T(8,128)(2,1)} %get-tuple-element.52.triple, bf16[2,256,1024]{2,1,0:T(8,128)(2,1)} %get-tuple-element.53.h_own, bf16[2,256,1024]{2,1,0:T(8,128)(2,1)} %get-tuple-element.54.h_far, ...), custom_call_target="tpu_custom_call" | custom-call | flops 55834574848 | bytes 104857600 | tf_op jit(solution)/shard_map/backward/pallas_call | solution.py:1074
  365.2 2.2 fusion.8
  367.4 1.0 copy.40
  368.4 1.6 slice.43
  370.0 0.6 copy.47
  370.6 0.0 copy-start.10
  370.6 0.6 copy.42
  371.2 0.6 copy.43
  371.8 0.6 copy.44
  372.4 0.6 copy.45
  373.0 0.6 slice.42
  373.6 0.6 copy.54
  374.2 1.3 copy.55
  375.5 1.6 copy-done.2
  377.2 2.0 copy.56
  379.2 0.7 copy.57
  379.9 0.0 copy-done.1
  (23 shorter events, 0.1 us)
Async XLA Ops:
  0.6 120.5 %copy-start = (f32[4096]{0:T(1024)S(1)}, f32[4096]{0:T(1024)}, u32[]{:S(2)}) copy-start(f32[4096]{0:T(1024)} %param.26) | copy-start | bytes 49156
  35.5 2.8 copy-start.6
  35.5 2.9 copy-start.7
  35.5 2.9 copy-start.8
  118.5 2.0 copy-start.11
  118.5 2.0 copy-start.12
  121.7 105.3 %copy-start.3 = (bf16[2,1024,512]{2,1,0:T(8,128)(2,1)S(1)}, bf16[2,1024,512]{2,1,0:T(8,128)(2,1)}, u32[]{:S(2)}) copy-start(bf16[2,1024,512]{2,1,0:T(8,128)(2,1)} %g_fin.1) | copy-start | bytes 6291460
  365.2 4.8 %copy-start.9 = (f32[56,256]{1,0:T(8,128)S(1)}, f32[56,256]{1,0:T(8,128)}, u32[]{:S(2)}) copy-start(f32[56,256]{1,0:T(8,128)} %get-tuple-element.61) | copy-start | bytes 172036
  365.2 9.1 %copy-start.4 = (bf16[2,1024,512]{2,1,0:T(8,128)(2,1)S(1)}, bf16[2,1024,512]{2,1,0:T(8,128)(2,1)}, u32[]{:S(2)}) copy-start(bf16[2,1024,512]{2,1,0:T(8,128)(2,1)} %get-tuple-element.117) | copy-start | bytes 6291460
  370.6 4.9 %copy-start.10 = (f32[1,2,4,128]{3,1,2,0:T(2,128)}, f32[1,2,4,128]{3,1,2,0:T(2,128)S(1)}, u32[]{:S(2)}) copy-start(f32[1,2,4,128]{3,1,2,0:T(2,128)S(1)} %copy.46) | copy-start | bytes 12292
  374.2 2.9 copy-start.2
  377.2 2.0 copy-start.5
  377.2 2.8 copy-start.1

commit v4 on v3

--- a/solution.py
+++ b/solution.py
@@ -111,71 +111,24 @@
             self.ring[k].start()
         self.cross[k].start()
 
-    def finish(self):
+    def arrive(self):
         for copy in self.cross:
             copy.wait_recv()
+
+    def close(self):
         for copy in (self.core, *self.ring, *self.cross):
             copy.wait_send()
 
 
-def enter_kernel(mine, theirs, tokens, all_ref, xb, xc, xd, local, send, recv, y_send, y_recv, c_send, c_recv, *, chunks):
-    spot = Spot()
-    spot.greet("row", "col", "x", "right", "left")
-    gather = Gather(spot, mine, theirs, all_ref, local, send, recv)
-    size = xb.shape[0] // chunks
-    part = lambda k: pl.ds(k * size, size)
-    over_row = [
-        remote(spot, "row", tokens.at[0, part(k)], xb.at[part(k)], y_send.at[k], y_recv.at[k]) for k in range(chunks)
-    ]
-    over_col = [
-        remote(spot, "col", xb.at[part(k)], xd.at[part(k)], c_send.at[k], c_recv.at[k]) for k in range(chunks)
-    ]
-    core = remote(spot, "col", tokens, xc, c_send.at[chunks], c_recv.at[chunks])
-    gather.begin()
-    for copy in over_row:
-        copy.start()
-    gather.first()
-    core.start()
-    depth = spot.depth
-    for k in range(max(depth - 1, chunks)):
-        if k + 1 < depth:
-            gather.forward(k + 1)
-        if k < chunks:
-            over_row[k].wait_recv()
-            over_col[k].start()
-    gather.finish()
-    core.wait()
-    for k in range(chunks):
-        over_col[k].wait()
-        over_row[k].wait_send()
-
-
-def enter(mine, theirs, tokens, count, chunks=4):
-    rows, wide = mine.shape
-    micros, length, _ = tokens.shape
-    depth = count // 2
-    half = jax.ShapeDtypeStruct((length, wide), BF16)
-    return pl.pallas_call(
-        partial(enter_kernel, chunks=chunks),
-        in_specs=[ANYWHERE] * 3,
-        out_specs=[ANYWHERE] * 4,
-        out_shape=[
-            jax.ShapeDtypeStruct((count, rows, 2 * wide), BF16), half,
-            jax.ShapeDtypeStruct(tokens.shape, BF16), half,
-        ],
-        scratch_shapes=[
-            pltpu.SemaphoreType.DMA, Gather.sems(2 * depth), Gather.sems(2 * depth),
-            Gather.sems(chunks), Gather.sems(chunks), Gather.sems(chunks + 1), Gather.sems(chunks + 1),
-        ],
-        compiler_params=pltpu.CompilerParams(collective_id=0, has_side_effects=True),
-        name="enter",
-    )(mine, theirs, tokens)
+def lanes(index, tokens):
+    return pl.ds(pl.multiple_of(index * tokens, tokens), tokens)
 
 
 def forward_kernel(
-    xa, xc, xb0, xd0, weight, bias, vectors, cosine, sine, mine, theirs, tokens, grads,
-    plain, second, triple, att_own, att_far, logsum, all_ref, xb1, xd1, cb0, cc, cd0,
-    x_s, first, q_s, v_s, o_s, n_s, f_s, local, send, recv, y_send, y_recv, c_send, c_recv, t_sem, l_sem, *, block, step,
+    xa, bias, vectors, cosine, sine, head_mine, head_theirs, mine, theirs, tokens, grads,
+    plain, second, triple, weight_out, att_own, att_far, logsum, all_ref, xc, cb0, cc, cd0,
+    x_s, first, q_s, v_s, o_s, xc_s, near_s, far_s, pieces, weight,
+    a_local, a_send, a_recv, local, send, recv, y_send, y_recv, c_send, c_recv, t_sem, *, block, step, chunks, rows_at_once,
 ):
     spot = Spot()
     now = pl.program_id(0)
@@ -185,107 +138,153 @@
     length = 2 * own_tokens
     blocks = own_tokens // block
     heads = weight.shape[0] // (3 * HS)
-    depth = spot.depth
-    attend0, far1, attend1 = 3 * blocks, 3 * blocks + heads, 4 * blocks + heads
+    depth, count = spot.depth, spot.count
+    cast0 = 2 * blocks
+    far0 = 2 * cast0
+    attend0 = far0 + blocks
+    far1 = attend0 + heads
+    attend1 = far1 + blocks
     end = attend1 + heads - 1
     here, there = spot.row, 1 - spot.row
-
+    at = lambda k: pl.when(now == k)
+
+    head_gather = Gather(spot, head_mine, head_theirs, pieces, a_local, a_send, a_recv)
     gather = Gather(spot, mine, theirs, all_ref, local, send, recv)
-    x_row = remote(spot, "row", tokens.at[1], xb1, y_send.at[0], y_recv.at[0])
-    x_col = remote(spot, "col", xb1, xd1, c_send.at[0], c_recv.at[0])
-    g_row = remote(spot, "row", grads.at[0], cb0, y_send.at[1], y_recv.at[1])
-    g_col = remote(spot, "col", cb0, cd0, c_send.at[1], c_recv.at[1])
-    g_core = remote(spot, "col", grads, cc, c_send.at[2], c_recv.at[2])
-    load_near = pltpu.make_async_copy(xb1, n_s, l_sem.at[0])
-    load_far = pltpu.make_async_copy(xd1, f_s, l_sem.at[1])
+    size = own_tokens // chunks
+    part = lambda k: pl.ds(k * size, size)
+    x_row = [
+        [remote(spot, "row", tokens.at[m, part(k)], near_s.at[m, part(k)], y_send.at[m * chunks + k], y_recv.at[m * chunks + k]) for k in range(chunks)]
+        for m in range(2)
+    ]
+    x_col = [
+        [remote(spot, "col", near_s.at[m, part(k)], far_s.at[m, part(k)], c_send.at[m * chunks + k], c_recv.at[m * chunks + k]) for k in range(chunks)]
+        for m in range(2)
+    ]
+    x_core = [remote(spot, "col", tokens.at[m], xc_s.at[m], c_send.at[2 * chunks + m], c_recv.at[2 * chunks + m]) for m in range(2)]
+    g_row = remote(spot, "row", grads.at[0], cb0, y_send.at[2 * chunks], y_recv.at[2 * chunks])
+    g_col = remote(spot, "col", cb0, cd0, c_send.at[2 * chunks + 2], c_recv.at[2 * chunks + 2])
+    g_core = remote(spot, "col", grads, cc, c_send.at[2 * chunks + 3], c_recv.at[2 * chunks + 3])
     keep = [pltpu.make_async_copy(q_s.at[m], triple.at[m], t_sem.at[m]) for m in range(2)]
-
-    at = lambda k: pl.when(now == k)
+    keep_weight = pltpu.make_async_copy(weight, weight_out, t_sem.at[2])
+    keep_core = pltpu.make_async_copy(xc_s, xc, t_sem.at[3])
 
     @at(0)
     def _():
         spot.greet("row", "col", "x", "right", "left")
+        head_gather.begin()
+        for copy in x_row[0]:
+            copy.start()
+        x_core[0].start()
         gather.begin()
-        x_row.start()
-
-    @at(1)
-    def _():
+        head_gather.first()
+        x_core[1].start()
+        x_core[0].wait_recv()
+
+    @at(blocks)
+    def _():
+        x_core[1].wait_recv()
+        keep_core.start()
+
+    @at(2)
+    def _():
+        head_gather.forward(1)
+
+    @at(cast0)
+    def _():
+        for k in range(2, depth):
+            head_gather.forward(k)
         gather.first()
+        for copy in x_row[1]:
+            copy.start()
+        head_gather.arrive()
+        size = weight.shape[0] // (heads * count)
+        for h in range(heads):
+            small = [pieces[p, h * size : (h + 1) * size, :].astype(F32) for p in range(count)]
+            weight[h * 3 * HS : (h + 1) * 3 * HS, :] = jnp.concatenate(small, axis=0).astype(BF16)
+        keep_weight.start()
+
+    @at(cast0 + 1)
+    def _():
+        for k in range(chunks):
+            x_row[0][k].wait_recv()
+            x_col[0][k].start()
+
+    @at(far0)
+    def _():
+        for k in range(chunks):
+            x_col[0][k].wait_recv()
         g_core.start()
 
-    moments = {1: attend0 + 1, 2: far1, 3: attend1 + 2} if depth == 4 else {}
+    moments = {1: attend0, 2: attend0 + 3, 3: attend1} if depth == 4 else {}
     for k in range(1, depth):
-        moment = moments.get(k, attend1 + 2)
-
-        @at(moment)
+        @at(moments.get(k, attend1))
         def _():
             gather.forward(k)
 
-    @at(attend0 + 2)
-    def _():
-        x_row.wait_recv()
-        x_col.start()
+    @at(far1 - 1)
+    def _():
+        for k in range(chunks):
+            x_row[1][k].wait_recv()
+            x_col[1][k].start()
         g_row.start()
 
-    @at(attend0 + 3)
-    def _():
-        x_col.wait_recv()
-        load_near.start()
-        load_far.start()
-
     @at(far1)
     def _():
-        load_near.wait()
-        load_far.wait()
-
-    @at(end - 1)
-    def _():
-        g_row.wait_recv()
-        g_col.start()
-
-    @pl.when(now < 2 * blocks)
-    def _():
+        for k in range(chunks):
+            x_col[1][k].wait_recv()
+
+    norming = (now < cast0) | ((now >= far0) & (now < attend0)) | ((now >= far1) & (now < attend1))
+
+    @pl.when(now < cast0)
+    def _():
+        lo = pl.multiple_of((now % blocks) * block, block)
         x_s[:, :wide] = xa[0]
-        x_s[:, wide:] = xc[0]
-
-    @pl.when((now >= 2 * blocks) & (now < attend0))
-    def _():
-        x_s[:, :wide] = xb0[...]
-        x_s[:, wide:] = xd0[...]
-
-    for k in range(blocks):
-        @at(far1 + k)
+        x_s[:, wide:] = xc_s[now // blocks, pl.ds(lo, block), :]
+
+    for begin, m in ((far0, 0), (far1, 1)):
+        @pl.when((now >= begin) & (now < begin + blocks))
         def _():
-            x_s[:, :wide] = n_s[k * block : (k + 1) * block]
-            x_s[:, wide:] = f_s[k * block : (k + 1) * block]
-
-    project = (now < attend0) | ((now >= far1) & (now < attend1))
-
-    @pl.when(project)
-    def _():
-        micro = jnp.where(now < blocks, 0, jnp.where(now < 2 * blocks, 1, jnp.where(now < attend0, 0, 1)))
-        half = jnp.where(now < 2 * blocks, here, there)
-        number = jnp.where(now < attend0, now % blocks, (now - far1) % blocks)
-        lane = pl.ds(pl.multiple_of(half * own_tokens + number * block, block), block)
-        values = x_s[...].astype(F32)
-        center = jnp.sum(values, axis=1, keepdims=True) / width
-        spread = jnp.sum(values * values, axis=1, keepdims=True) / width - center * center
-        normed = (values - center) * lax.rsqrt(spread + EPSILON)
-        plain[0, 0] = normed.astype(BF16)
-        first[...] = (normed * vectors[0:1, :] + vectors[1:2, :]).astype(BF16)
-        second[0, 0] = (normed * vectors[2:3, :] + vectors[3:4, :]).astype(BF16)
+            lo = pl.multiple_of((now - begin) * block, block)
+            x_s[:, :wide] = near_s[m, pl.ds(lo, block), :]
+            x_s[:, wide:] = far_s[m, pl.ds(lo, block), :]
+
+    slot = jnp.where(now < far0, now % cast0, (now - far0) % blocks)
+    slot = jnp.where(now >= far1, now - far1, slot)
+
+    @pl.when(norming)
+    def _():
+        for lo in range(0, block, rows_at_once):
+            rows = slice(lo, lo + rows_at_once)
+            values = x_s[rows, :].astype(F32)
+            center = jnp.sum(values, axis=1, keepdims=True) / width
+            spread = jnp.sum(values * values, axis=1, keepdims=True) / width - center * center
+            normed = (values - center) * lax.rsqrt(spread + EPSILON)
+            plain[0, 0, rows, :] = normed.astype(BF16)
+            first[slot, rows, :] = (normed * vectors[0:1, :] + vectors[1:2, :]).astype(BF16)
+            second[0, 0, rows, :] = (normed * vectors[2:3, :] + vectors[3:4, :]).astype(BF16)
+
+    casting = ((now >= cast0) & (now < attend0)) | ((now >= far1) & (now < attend1))
+
+    @pl.when(casting)
+    def _():
+        number = now - cast0
+        micro = jnp.where(now < far0, number // blocks, jnp.where(now < attend0, 0, 1))
+        half = jnp.where(now < far0, here, there)
+        block_at = jnp.where(now >= far1, now - far1, number % blocks)
+        lane = pl.ds(pl.multiple_of(half * own_tokens + block_at * block, block), block)
         cos, sin = cosine[:, lane], sine[:, lane]
+        every = mm(weight[...], first[slot], NT) + bias[...]
         for head in range(heads):
             base = head * 3 * HS
-            rows = mm(weight[base : base + 3 * HS, :], first[...], NT) + bias[base : base + 3 * HS, :]
-            pieces = []
+            rows = every[base : base + 3 * HS]
+            parts = []
             for which in range(2):
                 lo = which * HS
                 scale = HS ** (-0.5) if which == 0 else 1.0
                 u1, u2 = rows[lo : lo + HALF], rows[lo + HALF : lo + ROT]
-                pieces += [(u1 * cos - u2 * sin) * scale, (u2 * cos + u1 * sin) * scale, rows[lo + ROT : lo + HS] * scale]
-            pieces.append(rows[2 * HS :])
-            q_s[micro, base : base + 3 * HS, lane] = jnp.concatenate(pieces, axis=0).astype(BF16)
+                parts += [(u1 * cos - u2 * sin) * scale, (u2 * cos + u1 * sin) * scale, rows[lo + ROT : lo + HS] * scale]
+            parts.append(rows[2 * HS :])
+            q_s[micro, base : base + 3 * HS, lane] = jnp.concatenate(parts, axis=0).astype(BF16)
 
     @at(attend0)
     def _():
@@ -329,85 +328,98 @@
 
     @at(end)
     def _():
-        gather.finish()
+        g_row.wait_recv()
+        g_col.start()
+        gather.arrive()
+        gather.close()
+        head_gather.close()
         g_col.wait()
         g_core.wait()
-        x_col.wait_send()
-        x_row.wait_send()
+        for m in range(2):
+            x_core[m].wait_send()
+            for k in range(chunks):
+                x_row[m][k].wait_send()
+                x_col[m][k].wait_send()
         g_row.wait_send()
         keep[0].wait()
         keep[1].wait()
-
-
-def lanes(index, tokens):
-    return pl.ds(pl.multiple_of(index * tokens, tokens), tokens)
-
-
-def forward(residual, xc, xb0, xd0, weight, bias, vectors, cosine, sine, mine, theirs, cotangent, count, block=512, step=512):
+        keep_weight.wait()
+        keep_core.wait()
+
+
+def forward(residual, bias, vectors, cosine, sine, head_mine, head_theirs, mine, theirs, cotangent, count, block=512, step=512):
     micros, tokens, wide = residual.shape
     width, length = 2 * wide, 2 * tokens
     block, step = min(block, tokens), min(step, length)
     blocks = tokens // block
-    rows = weight.shape[0]
+    rows = bias.shape[0]
     heads = rows // (3 * HS)
     depth = count // 2
-    a0, f1, a1 = 3 * blocks, 3 * blocks + heads, 4 * blocks + heads
+    chunks = 4
+    cast0 = 2 * blocks
+    far0 = 2 * cast0
+    a0 = far0 + blocks
+    f1 = a0 + heads
+    a1 = f1 + blocks
     steps = a1 + heads
-    clip = lambda v, lo, hi: jnp.minimum(jnp.maximum(v, lo), hi)
-    own = pl.BlockSpec((1, block, wide), lambda i: (jnp.where(i < blocks, 0, 1), jnp.where(i < 2 * blocks, i % blocks, blocks - 1), 0))
-    far = pl.BlockSpec((block, wide), lambda i: (clip(i - 2 * blocks, 0, blocks - 1), 0))
+    own = pl.BlockSpec((1, block, wide), lambda i: (jnp.minimum(i, cast0 - 1) // blocks, jnp.minimum(i, cast0 - 1) % blocks, 0))
 
     def place(i):
+        early = jnp.minimum(i, cast0 - 1)
         late = i >= f1
-        micro = jnp.where(i < blocks, 0, jnp.where(i < 2 * blocks, 1, jnp.where(late, 1, 0)))
-        half = jnp.where(i < 2 * blocks, 1, 0)
-        number = jnp.where(i < 2 * blocks, i % blocks, jnp.where(late, clip(i - f1, 0, blocks - 1), clip(i - 2 * blocks, 0, blocks - 1)))
-        return micro, half, number, 0
+        far = i >= far0
+        micro = jnp.where(late, 1, jnp.where(far, 0, early // blocks))
+        number = jnp.where(late, jnp.minimum(i - f1, blocks - 1), jnp.where(far, jnp.minimum(i - far0, blocks - 1), early % blocks))
+        return micro, jnp.where(far, 0, 1), number, 0
 
     def head_of(i):
         late = i >= a1
-        return jnp.where(late, 1, 0), jnp.where(late, i - a1, clip(i - a0, 0, heads - 1))
+        return jnp.where(late, 1, 0), jnp.where(late, i - a1, jnp.clip(i - a0, 0, heads - 1))
 
     normal = pl.BlockSpec((1, 1, block, width), place)
     att = pl.BlockSpec((1, HS, tokens), lambda i: (*head_of(i), 0))
     half = jax.ShapeDtypeStruct((tokens, wide), BF16)
     piece = mine.shape[0]
+    sems, one = Gather.sems, pltpu.SemaphoreType.DMA
     return pl.pallas_call(
-        partial(forward_kernel, block=block, step=step),
+        partial(forward_kernel, block=block, step=step, chunks=chunks, rows_at_once=min(64, block)),
         grid=(steps,),
         in_specs=[
-            own, own, far, far, whole(weight.shape), whole(bias.shape), whole(vectors.shape),
-            whole(cosine.shape), whole(sine.shape), ANYWHERE, ANYWHERE, ANYWHERE, ANYWHERE,
+            own, whole(bias.shape), whole(vectors.shape), whole(cosine.shape), whole(sine.shape), *[ANYWHERE] * 6,
         ],
         out_specs=[
-            normal, normal, ANYWHERE, att, att, pl.BlockSpec((1, 1, 1, length), lambda i: (*head_of(i), 0, 0)),
-            *[ANYWHERE] * 6,
+            normal, normal, ANYWHERE, ANYWHERE, att, att,
+            pl.BlockSpec((1, 1, 1, length), lambda i: (*head_of(i), 0, 0)), *[ANYWHERE] * 5,
         ],
         out_shape=[
             jax.ShapeDtypeStruct((micros, 2, tokens, width), BF16),
             jax.ShapeDtypeStruct((micros, 2, tokens, width), BF16),
             jax.ShapeDtypeStruct((micros, rows, length), BF16),
+            jax.ShapeDtypeStruct((rows, width), BF16),
             jax.ShapeDtypeStruct((micros, heads * HS, tokens), BF16),
             jax.ShapeDtypeStruct((micros, heads * HS, tokens), BF16),
             jax.ShapeDtypeStruct((micros, heads, 1, length), F32),
             jax.ShapeDtypeStruct((count, piece, width), BF16),
-            half, half, half, jax.ShapeDtypeStruct(cotangent.shape, BF16), half,
+            jax.ShapeDtypeStruct(residual.shape, BF16), half, jax.ShapeDtypeStruct(cotangent.shape, BF16), half,
         ],
         scratch_shapes=[
             pltpu.VMEM((block, width), BF16),
-            pltpu.VMEM((block, width), BF16),
+            pltpu.VMEM((cast0, block, width), BF16),
             pltpu.VMEM((micros, rows, length), BF16),
             pltpu.VMEM((HS + 16, length), BF16),
             pltpu.VMEM((HS, length), BF16),
-            pltpu.VMEM((tokens, wide), BF16),
-            pltpu.VMEM((tokens, wide), BF16),
-            pltpu.SemaphoreType.DMA, Gather.sems(2 * depth), Gather.sems(2 * depth),
-            Gather.sems(2), Gather.sems(2), Gather.sems(3), Gather.sems(3), Gather.sems(2), Gather.sems(2),
+            pltpu.VMEM((micros, tokens, wide), BF16),
+            pltpu.VMEM((micros, tokens, wide), BF16),
+            pltpu.VMEM((micros, tokens, wide), BF16),
+            pltpu.VMEM((count, rows // count, width), BF16),
+            pltpu.VMEM((rows, width), BF16),
+            one, sems(2 * depth), sems(2 * depth), one, sems(2 * depth), sems(2 * depth),
+            sems(2 * chunks + 1), sems(2 * chunks + 1), sems(2 * chunks + 4), sems(2 * chunks + 4), sems(4),
         ],
         compiler_params=params(collective_id=1, has_side_effects=True),
         cost_estimate=cost(micros * length * width * rows * 2 + micros * heads * length * length * 256 * 2, 40 << 20),
         name="forward",
-    )(residual, xc, xb0, xd0, weight, bias, vectors, cosine, sine, mine, theirs, residual, cotangent)
+    )(residual, bias, vectors, cosine, sine, head_mine, head_theirs, mine, theirs, residual, cotangent)
 def causal_tile(size):
     keys = lax.broadcasted_iota(jnp.int32, (size, size), 0)
     places = lax.broadcasted_iota(jnp.int32, (size, size), 1)
@@ -695,21 +707,18 @@
 
 
 class Scatter:
-    def __init__(self, spot, tiles, own, rx, tx, rz, total, out, x_send, x_recv, z_send, z_recv, c_send, c_recv, local):
-        self.spot, self.own, self.rx, self.tx, self.rz, self.total = spot, own, rx, tx, rz, total
-        depth, wide = spot.depth, out.shape[2]
-        self.order = [*range(1, depth), 0]
+    def __init__(self, spot, tiles, own, rx, rz, x_sems, z_sems):
+        self.spot, self.own, self.rx, self.rz = spot, own, rx, rz
+        self.order = [*range(1, spot.depth), 0]
         self.cross, self.along = {}, {}
         for s in self.order:
             away = spot.along(s) + 1 - 2 * spot.x
-            self.cross[s] = remote(spot, "x", tiles.at[away], rx.at[s], x_send.at[s], x_recv.at[s])
+            self.cross[s] = remote(spot, "x", tiles(away), rx(s), x_sems[0](s), x_sems[1](s))
             if s:
                 self.along[s] = pltpu.make_async_remote_copy(
-                    src_ref=tx.at[s - 1], dst_ref=rz.at[s - 1], send_sem=z_send.at[s], recv_sem=z_recv.at[s],
+                    src_ref=rx(s), dst_ref=rz(s - 1), send_sem=z_sems[0](s), recv_sem=z_sems[1](s),
                     device_id={"dp": spot.along(s)}, device_id_type=MESH,
                 )
-        self.core = remote(spot, "col", total.at[:, pl.ds(wide, wide)], out.at[spot.col], c_send, c_recv)
-        self.keep = pltpu.make_async_copy(total.at[:, pl.ds(0, wide)], out.at[spot.col], local)
 
     def begin(self):
         for s in self.order:
@@ -717,25 +726,19 @@
 
     def fold(self, s):
         self.cross[s].wait_recv()
-        added = self.own(s).astype(F32) + self.rx[s].astype(F32)
+        rx = self.rx(s)
         if s:
-            self.tx[s - 1] = added.astype(BF16)
+            rx[...] = (self.own(s)[...].astype(F32) + rx[...].astype(F32)).astype(BF16)
             self.along[s].start()
-        else:
-            self.total[...] = added
-
-    def finish(self):
-        added = self.total[...]
+
+    def total(self):
+        added = self.own(0)[...].astype(F32) + self.rx(0)[...].astype(F32)
         for s in self.order[:-1]:
             self.along[s].wait_recv()
-            added = added + self.rz[s - 1].astype(F32)
-        self.total[...] = added
-        self.core.start()
-        self.keep.start()
+            added = added + self.rz(s - 1)[...].astype(F32)
+        return added
 
     def close(self):
-        self.core.wait()
-        self.keep.wait()
         for s in self.order:
             self.cross[s].wait_send()
             if s:
@@ -743,13 +746,13 @@
 
 
 def back_kernel(
-    triple, h_own, h_far, att_own, att_far, logsum, cosine, sine, normed, part, weight, vectors, tiles, early,
+    triple, h_own, h_far, att_own, att_far, logsum, cosine, sine, part, weight, vectors, early, normed, tiles,
     x_fin, xc_fin, g_fin,
     grad_out, rest_out, dq_out, vec_out,
-    g_s, delta_s, dq_s, dk_s, dv_s, t_s, total, bias_s,
-    near_f, near_o, other_f, other_o, cross_f, cross_o, y_s, moved, sum_s, sum_r, ng_s, norm_s, inv_s,
-    a_own, a_rx, a_tx, a_rz, a_total, b_tiles, b_rx, b_tx, b_rz, b_total, held, arrived,
-    a_load, a_xs, a_xr, a_zs, a_zr, a_cs, a_cr, a_loc, b_xs, b_xr, b_zs, b_zr, b_cs, b_cr, b_loc,
+    g_s, delta_s, dq_s, dk_s, dv_s, t_s, norm_in, total, bias_s, gain_s, shift_s,
+    near_f, near_o, other_f, other_o, cross_f, cross_o, moved, sum_s, sum_r, ng_s, norm_s, inv_s,
+    a_own, a_rx, a_rz, a_total, b_tiles, b_rx, b_rz, b_total, held, arrived,
+    n_load, a_load, a_xs, a_xr, a_zs, a_zr, b_xs, b_xr, b_zs, b_zr, k_send, k_recv, k_loc,
     v_send, v_recv, cf_send, cf_recv, co_send, co_recv, m_send, m_recv, s_send, s_recv,
     *, block, wider, step,
 ):
@@ -759,27 +762,40 @@
     width, length = 2 * wide, 2 * tokens
     heads = weight.shape[0] // (3 * HS)
     steps = tokens // block
+    group = wider // block
+    slow = tokens // wider
     count, depth = spot.count, spot.depth
-    slow = length // wider
-    d0 = heads
-    l0 = d0 + slow
-    b1 = l0 + 2 * steps
-    d1 = b1 + heads
-    l1 = d1 + slow
-    e1 = l1 + 2 * steps
-    end = e1 + steps
+    size = 3 * HS // count
+    l0 = heads
+    b1 = l0 + 2 * slow
+    l1 = b1 + heads
+    e0 = l1 + 2 * slow
+    end = e0 + 2 * steps
     here, there = spot.row, 1 - spot.row
     at_step = lambda k: pl.when(now == k)
 
+    sem = lambda ref, base=0: (lambda s: ref.at[base + s])
     first_sum = Scatter(
-        spot, tiles, lambda s: a_own[s], a_rx, a_tx, a_rz, a_total, rest_out,
-        a_xs, a_xr, a_zs, a_zr, a_cs, a_cr, a_loc,
+        spot, lambda p: tiles.at[p], lambda s: a_own.at[s], lambda s: a_rx.at[s], lambda s: a_rz.at[s],
+        (sem(a_xs), sem(a_xr)), (sem(a_zs), sem(a_zr)),
     )
-    last_sum = Scatter(
-        spot, b_tiles, lambda s: b_tiles[spot.along(s)], b_rx, b_tx, b_rz, b_total, dq_out,
-        b_xs, b_xr, b_zs, b_zr, b_cs, b_cr, b_loc,
-    )
+
+    def head_sum(h):
+        return Scatter(
+            spot, lambda p: b_tiles.at[p, h], lambda s: b_tiles.at[spot.along(s), h], lambda s: b_rx.at[h, s],
+            lambda s: b_rz.at[h, s], (sem(b_xs, h * depth), sem(b_xr, h * depth)), (sem(b_zs, h * depth), sem(b_zr, h * depth)),
+        )
+
     loads = [pltpu.make_async_copy(tiles.at[spot.along(s)], a_own.at[s], a_load.at[s]) for s in range(depth)]
+    load_norm = [pltpu.make_async_copy(normed.at[m], norm_in, n_load.at[m]) for m in range(2)]
+
+    def to_core(k, source, out):
+        return (
+            remote(spot, "col", source.at[:, pl.ds(wide, wide)], out.at[spot.col], k_send.at[k], k_recv.at[k]),
+            pltpu.make_async_copy(source.at[:, pl.ds(0, wide)], out.at[spot.col], k_loc.at[k]),
+        )
+
+    a_core, b_core = to_core(0, a_total, rest_out), to_core(1, b_total, dq_out)
 
     partners = [{"col": 1 - spot.col}, {"row": 1 - spot.row}, {"dp": spot.z * 2 + (1 - spot.x)}]
     stride = 1
@@ -803,7 +819,7 @@
 
     def over_row(m, i):
         k = m * steps + i
-        return remote(spot, "row", y_s.at[m, i], moved.at[m, i], m_send.at[k], m_recv.at[k])
+        return remote(spot, "row", cross_f.at[m, i], moved.at[m, i], m_send.at[k], m_recv.at[k])
 
     def sums_over(m, i):
         k = m * steps + i
@@ -815,26 +831,35 @@
         near = [{"col": 1 - spot.col}, {"row": 1 - spot.row}, {"dp": spot.z * 2 + (1 - spot.x)}]
         for device in near + [{"dp": spot.along(s)} for s in range(1, depth)]:
             pl.semaphore_signal(barrier, inc=1, device_id=device, device_id_type=MESH)
-        pl.semaphore_wait(barrier, depth + 2)
-        first_sum.begin()
+        load_norm[0].start()
         for load in loads:
             load.start()
         bias_s[...] = jnp.zeros_like(bias_s)
+        gain_s[...] = jnp.zeros_like(gain_s)
+        shift_s[...] = jnp.zeros_like(shift_s)
+        pl.semaphore_wait(barrier, depth + 2)
+        first_sum.begin()
+        load_norm[0].wait()
 
     @at_step(1)
     def _():
         for load in loads:
             load.wait()
 
-    moments = {1: 2, 2: d0, 3: l0 + 4, 0: b1 + 1} if depth == 4 else {}
-    for s in first_sum.order:
-        @at_step(moments.get(s, b1 + 1))
-        def _():
-            first_sum.fold(s)
-
-    @pl.when((now < d0) | ((now >= b1) & (now < d1)))
-    def _():
-        head = jnp.where(now < d0, now, now - b1)
+    @at_step(l0)
+    def _():
+        load_norm[1].start()
+
+    @at_step(b1)
+    def _():
+        load_norm[1].wait()
+        for i in range(steps):
+            over_core(0, 0, i).wait_send()
+            over_core(1, 0, i).wait_send()
+
+    @pl.when((now < l0) | ((now >= b1) & (now < l1)))
+    def _():
+        head = jnp.where(now < l0, now, now - b1)
         for grad, att, place in ((h_own, att_own, here), (h_far, att_far, there)):
             at = lanes(place, tokens)
             g_s[:, at] = grad[0]
@@ -855,8 +880,9 @@
                 if begin == lo:
                     raised = jnp.where(allowed, raised, 0.0)
                 prob_grad = mm(v_s[:, begin:stop], grad, TN)
-                score_grad = (raised * (prob_grad - delta)).astype(BF16)
-                dv_s[:, begin:stop] += mm(grad, raised.astype(BF16), NT)
+                raised = raised.astype(BF16)
+                score_grad = raised * (prob_grad - delta).astype(BF16)
+                dv_s[:, begin:stop] += mm(grad, raised, NT)
                 dk_s[:, begin:stop] += mm(query, score_grad, NT)
                 term = mm(k_s[:, begin:stop], score_grad, NN)
                 query_grad = term if query_grad is None else query_grad + term
@@ -871,42 +897,46 @@
         at = pl.ds(pl.multiple_of(head * 3 * HS, HS), 3 * HS)
         t_s[at, :] = rounded
         bias_s[at, :] += jnp.sum(rounded.astype(F32), axis=1, keepdims=True)
-
-    @pl.when(((now >= d0) & (now < l0)) | ((now >= d1) & (now < l1)))
-    def _():
-        number = jnp.where(now < l0, now - d0, now - d1)
-        half, at = number // (slow // 2), number % (slow // 2)
-        place = jnp.where(half == 0, there, here)
-        lane = pl.ds(pl.multiple_of(place * tokens + at * wider, wider), wider)
-        term = mm(t_s[:, lane], normed[0, 0], NN)
-
-        @at_step(d0)
+        term = mm(t_s[at, lanes(there, tokens)], norm_in[0], NN) + mm(t_s[at, lanes(here, tokens)], norm_in[1], NN)
+
+        @pl.when(now < l0)
         def _():
-            total[...] = term
-
-        @pl.when(now > d0)
+            total[head] = term
+
+        @pl.when(now >= b1)
         def _():
-            total[...] += term
-
-    @at_step(l1 - 1)
-    def _():
-        size = 3 * HS // count
-        gain, shift = vectors[0:1, :], vectors[1:2, :]
-        weights = weight[...].astype(F32)
-        gain_grad = jnp.sum(weights * total[...], axis=0, keepdims=True)
-        shift_grad = jnp.sum(weights * bias_s[...], axis=0, keepdims=True)
-        total[...] = total[...] * gain + bias_s[...] * shift
-        for p in range(count):
-            small = [total[h * 3 * HS + p * size : h * 3 * HS + (p + 1) * size, :] for h in range(heads)]
-            b_tiles[p] = jnp.concatenate(small, axis=0).astype(BF16)
-        last_sum.begin()
+            gain, shift = vectors[0:1, :], vectors[1:2, :]
+            every = total[head] + term
+            weights = weight[at, :].astype(F32)
+            summed = bias_s[at, :]
+            gain_s[...] += jnp.sum(weights * every, axis=0, keepdims=True)
+            shift_s[...] += jnp.sum(weights * summed, axis=0, keepdims=True)
+            every = every * gain + summed * shift
+            for p in range(count):
+                b_tiles[p, head] = every[p * size : (p + 1) * size].astype(BF16)
+            head_sum(head).begin()
+
+    moments = {1: 2, 2: l0, 3: b1, 0: b1 + 2} if depth == 4 else {}
+    for s in first_sum.order:
+        @at_step(moments.get(s, b1 + 2))
+        def _():
+            first_sum.fold(s)
+
+    @pl.when((now > b1) & (now < l1))
+    def _():
+        before = head_sum(now - 1 - b1)
+        for s in before.order:
+            before.fold(s)
+
+    @at_step(l1 + 1)
+    def _():
         used = early.shape[0]
-        part_rows = width // (2 * held.shape[2])
         lanes_here = held.shape[2]
+        part_rows = width // (2 * lanes_here)
         held[0] = jnp.zeros_like(held[0])
         held[0, 0:used, :] = early[...]
         at = used
-        for vector in (gain_grad, shift_grad):
+        for vector in (gain_s, shift_s):
             for r in range(2 * part_rows):
                 mirror = (r + part_rows) % (2 * part_rows)
                 plain = vector[:, r * lanes_here : (r + 1) * lanes_here]
@@ -921,8 +951,54 @@
             held[0, at : at + 1, 0 : 3 * HS] = jnp.where(mine == h // heads, values, 0.0)
             at += 1
 
+    later = now >= b1
+    lead = jnp.where(later, now - l1, now - l0)
+
+    @pl.when((lead >= 0) & (lead < 2 * slow))
+    def _():
+        m, half, at = jnp.where(later, 1, 0), lead // slow, lead % slow
+        place = jnp.where(half == 0, there, here)
+        blocks = [(j, at * group + j, slice(j * block, (j + 1) * block)) for j in range(group)]
+        turned = lambda i: t_s[:, pl.ds(pl.multiple_of(place * tokens + i * block, block), block)]
+        for j, i, rows in blocks:
+            other = (mm(turned(i), weight[:, wide:], TN) * vectors[0:1, wide:] + part[0, 0, rows, wide:].astype(F32)).astype(BF16)
+
+            @pl.when(half == 0)
+            def _():
+                other_f[i] = other
+                over_core(0, m, i).start()
+
+            @pl.when(half == 1)
+            def _():
+                other_o[i] = other
+                over_core(1, m, i).start()
+
+        for j, i, rows in blocks:
+            near = mm(turned(i), weight[:, :wide], TN) * vectors[0:1, :wide] + part[0, 0, rows, :wide].astype(F32)
+
+            @pl.when(half == 0)
+            def _():
+                near_f[j] = near
+
+            @pl.when(half == 1)
+            def _():
+                near_o[m, i] = near.astype(BF16)
+
+        @pl.when(half == 0)
+        def _():
+            for j, i, rows in blocks:
+                over_core(0, m, i).wait_recv()
+                cross_f[m, i] = (near_f[j] + cross_f[m, i].astype(F32)).astype(BF16)
+                over_row(m, i).start()
+
+    @at_step(l1 + 2)
+    def _():
+        before = head_sum(heads - 1)
+        for s in before.order:
+            before.fold(s)
+
     for k in range(len(hops) + 1):
-        @at_step(l1 + k)
+        @at_step(l1 + 1 + k)
         def _():
             if k:
                 hops[k - 1].wait_recv()
@@ -933,86 +1009,55 @@
             else:
                 vec_out[...] = held[k - 1] + arrived[k - 1]
 
-    @at_step(l1)
-    def _():
-        first_sum.finish()
-
-    moments_b = {1: l1 + 3, 2: l1 + 5, 3: l1 + 7, 0: e1} if depth == 4 else {}
-    for s in last_sum.order:
-        @at_step(moments_b.get(s, e1))
-        def _():
-            last_sum.fold(s)
-
-    @at_step(b1)
-    def _():
-        for i in range(steps):
-            over_core(0, 0, i).wait_send()
-            over_core(1, 0, i).wait_send()
-
-    later = now >= b1
-    lead = jnp.where(later, now - l1, now - l0)
-
-    @pl.when((lead > 0) & (lead <= steps))
-    def _():
-        m, i = jnp.where(later, 1, 0), lead - 1
-        over_core(0, m, i).wait_recv()
-        y_s[m, i] = (near_f[...] + cross_f[m, i].astype(F32)).astype(BF16)
-        over_row(m, i).start()
-
-    trail = jnp.where(now >= e1, now - e1, now - l1)
-    micro = jnp.where(now >= e1, 1, 0)
-
-    @pl.when((trail > 0) & (trail <= steps))
-    def _():
-        i = trail - 1
-        sums_over(micro, i).wait_recv()
-        sums = (sum_s[micro, i] + sum_r[micro, i]) / width
-        grad_out[0] = g_fin[0].astype(F32) + inv_s[...] * (ng_s[...] - sums[:, 0:1] - norm_s[...] * sums[:, 1:2])
-
-    @pl.when((trail >= 0) & (trail < steps))
-    def _():
-        over_row(micro, trail).wait_recv()
-        over_core(1, micro, trail).wait_recv()
-        grad = near_o[trail] + cross_o[micro, trail].astype(F32) + moved[micro, trail].astype(F32)
+    @at_step(e0)
+    def _():
+        a_total[...] = first_sum.total()
+        for copy in a_core:
+            copy.start()
+
+    trail = now - e0
+
+    @at_step(e0 + steps - 1)
+    def _():
+        for h in range(heads):
+            b_total[h * size : (h + 1) * size, :] = head_sum(h).total()
+        for copy in b_core:
+            copy.start()
+
+    @pl.when((trail >= 0) & (trail < 2 * steps))
+    def _():
+        m, i, slot = trail // steps, trail % steps, trail % 2
+        over_row(m, i).wait_recv()
+        over_core(1, m, i).wait_recv()
+        grad = near_o[m, i].astype(F32) + cross_o[m, i].astype(F32) + moved[m, i].astype(F32)
         near_x, far_x = x_fin[0].astype(F32), xc_fin[0].astype(F32)
         center = jnp.sum(near_x + far_x, axis=1, keepdims=True) / width
         spread = jnp.sum(near_x * near_x + far_x * far_x, axis=1, keepdims=True) / width - center * center
         inv = lax.rsqrt(spread + EPSILON)
         normed_x = (near_x - center) * inv
-        ng_s[...] = grad
-        norm_s[...] = normed_x
-        inv_s[...] = inv
+        ng_s[slot] = grad
+        norm_s[slot] = normed_x
+        inv_s[slot] = inv
         column = lax.broadcasted_iota(jnp.int32, (block, 128), 1)
         one = jnp.sum(grad, axis=1, keepdims=True)
         two = jnp.sum(grad * normed_x, axis=1, keepdims=True)
-        sum_s[micro, trail] = jnp.where(column == 0, one, jnp.where(column == 1, two, 0.0))
-        sums_over(micro, trail).start()
-
-    @pl.when((lead >= 0) & (lead < 2 * steps))
-    def _():
-        m, half, i = jnp.where(later, 1, 0), lead // steps, lead % steps
-        place = jnp.where(half == 0, there, here)
-        lane = pl.ds(pl.multiple_of(place * tokens + i * block, block), block)
-        turned = t_s[:, lane]
-        near = mm(turned, weight[:, :wide], TN) * vectors[0:1, :wide] + part[0, 0, :, :wide].astype(F32)
-        other = mm(turned, weight[:, wide:], TN) * vectors[0:1, wide:] + part[0, 0, :, wide:].astype(F32)
-
-        @pl.when(half == 0)
-        def _():
-            near_f[...] = near
-            other_f[i] = other.astype(BF16)
-            over_core(0, m, i).start()
-
-        @pl.when(half == 1)
-        def _():
-            near_o[i] = near
-            other_o[i] = other.astype(BF16)
-            over_core(1, m, i).start()
+        sum_s[m, i] = jnp.where(column == 0, one, jnp.where(column == 1, two, 0.0))
+        sums_over(m, i).start()
+
+    @pl.when(trail > 0)
+    def _():
+        m, i, slot = (trail - 1) // steps, (trail - 1) % steps, (trail - 1) % 2
+        sums_over(m, i).wait_recv()
+        sums = (sum_s[m, i] + sum_r[m, i]) / width
+        grad_out[0] = g_fin[0].astype(F32) + inv_s[slot] * (ng_s[slot] - sums[:, 0:1] - norm_s[slot] * sums[:, 1:2])
 
     @at_step(end)
     def _():
-        last_sum.finish()
+        for copy in (*a_core, *b_core):
+            copy.wait()
         first_sum.close()
+        for h in range(heads):
+            head_sum(h).close()
         for k in hops:
             k.wait_send()
         for i in range(steps):
@@ -1021,7 +1066,6 @@
             for m in range(2):
                 over_row(m, i).wait_send()
                 sums_over(m, i).wait_send()
-        last_sum.close()
 
 
 def backward(
@@ -1033,35 +1077,31 @@
     width = 2 * wide
     heads = rows // (3 * HS)
     block, wider, step = min(block, tokens), min(wider, tokens), min(step, length)
-    steps, slow = tokens // block, length // wider
+    steps, slow = tokens // block, tokens // wider
     count, piece = tiles.shape[:2]
     depth = count // 2
     small = rows // count
-    d0 = heads
-    l0 = d0 + slow
-    b1 = l0 + 2 * steps
-    d1 = b1 + heads
-    l1 = d1 + slow
-    e1 = l1 + 2 * steps
-    head_of = lambda s: (jnp.where(s >= b1, 1, 0), jnp.where(s >= b1, jnp.minimum(s - b1, heads - 1), jnp.minimum(s, heads - 1)))
-
-    def slow_at(s):
+    l0 = heads
+    b1 = l0 + 2 * slow
+    l1 = b1 + heads
+    e0 = l1 + 2 * slow
+
+    def head_of(s):
         late = s >= b1
-        number = jnp.clip(jnp.where(late, s - d1, s - d0), 0, slow - 1)
-        return jnp.where(late, 1, 0), number // (slow // 2), number % (slow // 2), 0
+        return jnp.where(late, 1, 0), jnp.minimum(jnp.where(late, s - b1, s), heads - 1)
 
     def part_at(s):
         late = s >= b1
-        number = jnp.clip(jnp.where(late, s - l1, s - l0), 0, 2 * steps - 1)
-        return jnp.where(late, 1, 0), number // steps, number % steps, 0
+        number = jnp.clip(jnp.where(late, s - l1, s - l0), 0, 2 * slow - 1)
+        return jnp.where(late, 1, 0), number // slow, number % slow, 0
 
     def in_at(s):
-        late = s > l1 + steps
-        return jnp.where(late, 1, 0), jnp.clip(jnp.where(late, s - e1, s - l1), 0, steps - 1), 0
+        number = jnp.clip(s - e0, 0, 2 * steps - 1)
+        return number // steps, number % steps, 0
 
     def out_at(s):
-        late = s > l1 + steps
-        return jnp.where(late, 1, 0), jnp.clip(jnp.where(late, s - e1 - 1, s - l1 - 1), 0, steps - 1), 0
+        number = jnp.clip(s - e0 - 1, 0, 2 * steps - 1)
+        return number // steps, number % steps, 0
 
     narrow = pl.BlockSpec((1, HS, tokens), lambda s: (*head_of(s), 0))
     fin_in = pl.BlockSpec((1, block, wide), in_at)
@@ -1070,15 +1110,15 @@
     vec_rows = early.shape[0] + 2 * (width // early.shape[1]) + 4 * heads
     pair = lambda dtype: pltpu.VMEM((micros, steps, block, wide), dtype)
     single = lambda dtype: pltpu.VMEM((steps, block, wide), dtype)
-    sems, one = Gather.sems, pltpu.SemaphoreType.DMA
+    sems = Gather.sems
     return pl.pallas_call(
         partial(back_kernel, block=block, wider=wider, step=step),
-        grid=(e1 + steps + 1,),
+        grid=(e0 + 2 * steps + 1,),
         in_specs=[
             pl.BlockSpec((1, 3 * HS, length), lambda s: (*head_of(s), 0)), narrow, narrow, narrow, narrow,
             pl.BlockSpec((1, 1, 1, length), lambda s: (*head_of(s), 0, 0)), whole(cosine.shape), whole(sine.shape),
-            pl.BlockSpec((1, 1, wider, width), slow_at), pl.BlockSpec((1, 1, block, width), part_at),
-            whole(weight.shape), whole(vectors.shape), ANYWHERE, whole(early.shape), fin_in, fin_in, fin_out,
+            pl.BlockSpec((1, 1, wider, width), part_at),
+            whole(weight.shape), whole(vectors.shape), whole(early.shape), ANYWHERE, ANYWHERE, fin_in, fin_in, fin_out,
         ],
         out_specs=[fin_out, ANYWHERE, ANYWHERE, whole((vec_rows, early.shape[1]))],
         out_shape=[
@@ -1094,28 +1134,30 @@
             pltpu.VMEM((HS, length), F32),
             pltpu.VMEM((HS, length), F32),
             pltpu.VMEM((rows, length), BF16),
-            pltpu.VMEM((rows, width), F32),
+            pltpu.VMEM((2, tokens, width), BF16),
+            pltpu.VMEM((heads, 3 * HS, width), F32),
             pltpu.VMEM((rows, 1), F32),
-            pltpu.VMEM((block, wide), F32), single(F32), single(BF16), single(BF16), pair(BF16), pair(BF16),
-            pair(BF16), pair(BF16),
+            pltpu.VMEM((1, width), F32), pltpu.VMEM((1, width), F32),
+            pltpu.VMEM((wider // block, block, wide), F32), pair(BF16), single(BF16), single(BF16), pair(BF16), pair(BF16),
+            pair(BF16),
             pltpu.VMEM((micros, steps, block, 128), F32), pltpu.VMEM((micros, steps, block, 128), F32),
-            pltpu.VMEM((block, wide), F32), pltpu.VMEM((block, wide), F32), pltpu.VMEM((block, 1), F32),
+            pltpu.VMEM((2, block, wide), F32), pltpu.VMEM((2, block, wide), F32), pltpu.VMEM((2, block, 1), F32),
             pltpu.VMEM((depth, piece, width), BF16), pltpu.VMEM((depth, piece, width), BF16),
-            pltpu.VMEM((depth - 1, piece, width), BF16), pltpu.VMEM((depth - 1, piece, width), BF16),
-            pltpu.VMEM((piece, width), F32),
-            pltpu.VMEM((count, small, width), BF16), pltpu.VMEM((depth, small, width), BF16),
-            pltpu.VMEM((depth - 1, small, width), BF16), pltpu.VMEM((depth - 1, small, width), BF16),
+            pltpu.VMEM((depth - 1, piece, width), BF16), pltpu.VMEM((piece, width), F32),
+            pltpu.VMEM((count, heads, small // heads, width), BF16),
+            pltpu.VMEM((heads, depth, small // heads, width), BF16),
+            pltpu.VMEM((heads, depth - 1, small // heads, width), BF16),
             pltpu.VMEM((small, width), F32),
             pltpu.VMEM((hops, vec_rows, early.shape[1]), F32), pltpu.VMEM((hops, vec_rows, early.shape[1]), F32),
-            sems(depth), sems(depth), sems(depth), sems(depth), sems(depth), one, one, one,
-            sems(depth), sems(depth), sems(depth), sems(depth), one, one, one,
+            sems(2), sems(depth), sems(depth), sems(depth), sems(depth), sems(depth),
+            *[sems(depth * heads) for _ in range(4)], sems(2), sems(2), sems(2),
             sems(hops), sems(hops), *[sems(micros * steps) for _ in range(8)],
         ],
         compiler_params=params(collective_id=3, has_side_effects=True),
         cost_estimate=cost(micros * (heads * length * length * 256 * 5 + length * width * 4 * rows), 100 << 20),
         name="backward",
     )(
-        triple, h_own, h_far, att_own, att_far, logsum, cosine, sine, normed, part, weight, vectors, tiles, early,
+        triple, h_own, h_far, att_own, att_far, logsum, cosine, sine, part, weight, vectors, early, normed, tiles,
         residual, xc, cotangent,
     )
 
@@ -1151,8 +1193,6 @@
             axis=1,
         )
     )
-    head_all, xb0, xc, xd0 = enter(head_mine, head_theirs, residual, count)
-    wq = head_all.reshape(count, heads, head_part, width).transpose(1, 0, 2, 3).reshape(heads * 3 * HS, width)
 
     vectors = jnp.stack([attend_norm_gain, attend_norm_bias, expand_norm_gain, expand_norm_bias])
     vectors = jnp.concatenate([jnp.roll(vectors, -col * wide, axis=1), jnp.zeros((4, width), F32)])
@@ -1164,8 +1204,8 @@
     angles = powers[:, None] * np.arange(length)[None, :]
     cosine, sine = jnp.asarray(np.cos(angles), F32), jnp.asarray(np.sin(angles), F32)
 
-    normed, second, triple, att_own, att_far, logsum, pieces, xb1, xd1, cb0, cc, cd0 = forward(
-        residual, xc, xb0, xd0, wq, bias_q, vectors, cosine, sine, rest_mine, rest_theirs, cotangent, count
+    normed, second, triple, wq, att_own, att_far, logsum, pieces, xc, cb0, cc, cd0 = forward(
+        residual, bias_q, vectors, cosine, sine, head_mine, head_theirs, rest_mine, rest_theirs, cotangent, count
     )
     lo = heads * out_part
     wo = pieces[:, :lo].reshape(count, heads, out_part, width).transpose(1, 0, 2, 3).reshape(heads * HS, width)

time: 380 us -> 358 us (0.942)
  Pallas kernels: 349 us -> 329 us
    pallas_call x2 -> x1, Pallas kernels: 109 us -> 92.3 us  [forward(): pl.pallas_call(partial(forward_kernel, block=block, step=step, chunks=chu...]
    pallas_call x1, Pallas kernels: 137 us -> 132 us  [backward(): pl.pallas_call(partial(back_kernel, block=block, wider=wider, step=step),...]
    unnamed x38 -> x34, local copies, waits for them, and re-layouts: 9.37 us -> 9.36 us
where the time goes in v4:
time: 358 us; the launch traced here: 357 us
  Pallas kernels  329 us (92%)
  local copies, waits for them, and re-layouts  24.9 us (7%)
    pallas_call x1, Pallas kernels, backward(): pl.pallas_call(partial(back_kernel, block=block, wider=wider, step=step),...  132 us
    pallas_call x1, Pallas kernels, middle(): pl.pallas_call(partial(middle_kernel, block=block, chunk=min(chunk, hidde...  105 us
    pallas_call x1, Pallas kernels, forward(): pl.pallas_call(partial(forward_kernel, block=block, step=step, chunks=chu...  92.3 us
    unnamed x34, local copies, waits for them, and re-layouts  9.36 us

profile of v4, /device:TPU:0, one launch (start us, length us, event | category | flops | bytes accessed | tf_op | source)
XLA Modules:
  0.0 357.3 jit_solution(14759374137093984088)
XLA Ops:
  0.6 0.0 copy-start
  0.7 0.0 copy-start.6
  0.7 0.9 fusion.3
  1.6 0.6 concatenate.18.vectors
  2.3 1.1 copy.39
  3.3 1.0 pad_maximum_fusion
  4.3 0.9 dynamic-slice_bitcast_fusion
  5.2 0.0 copy-done.6
  5.2 0.7 dynamic-slice_bitcast_fusion.2
  5.9 0.7 constant_dynamic-slice_fusion
  6.6 1.0 reshape.125.bias
  7.6 92.3 %forward.1 = (bf16[2,2,1024,1024]{3,2,1,0:T(8,128)(2,1)}, bf16[2,2,1024,1024]{3,2,1,0:T(8,128)(2,1)}, bf16[2,768,2048]{2,1,0:T(8,128)(2,1)}, bf16[768,1024]{1,0:...) custom-call(bf16[2,1024,512]{2,1,0:T(8,128)(2,1)} %x_fin.3, ...), custom_call_target="tpu_custom_call" | custom-call | flops 23622320128 | bytes 41943040 | tf_op jit(solution)/shard_map/forward/pallas_call | solution.py:384
  99.9 0.0 copy-start.9
  100.0 0.0 copy-start.10
  100.0 1.1 slice_bitcast_fusion
  101.1 0.8 copy.36
  101.9 0.0 copy-done.9
  101.9 0.0 copy-done.10
  101.9 0.7 dynamic_slice.39
  102.6 0.0 copy-done
  102.6 0.6 dynamic-slice_bitcast_fusion.4.bias
  103.2 104.7 %middle.1 = (bf16[2,1024,512]{2,1,0:T(8,128)(2,1)}, bf16[2,256,1024]{2,1,0:T(8,128)(2,1)}, bf16[2,256,1024]{2,1,0:T(8,128)(2,1)}, bf16[2,2,1024,1024]{3,2,1,0:T(...) custom-call(bf16[2,2,1024,1024]{3,2,1,0:T(8,128)(2,1)} %get-tuple-el, ...), custom_call_target="tpu_custom_call" | custom-call | flops 57982058496 | bytes 83886080 | tf_op jit(solution)/shard_map/middle/pallas_call | solution.py:661
  207.9 0.8 slice.37
  208.7 0.7 dynamic_update_slice.6
  209.5 0.0 copy-done.3
  209.5 0.3 convert_reduce_fusion
  209.8 0.5 dynamic_update_slice.7
  210.3 0.6 select_maximum_fusion.early
  210.9 131.5 %backward.1 = (f32[2,1024,512]{2,1,0:T(8,128)}, f32[2,288,512]{2,1,0:T(8,128)}, f32[2,96,512]{2,1,0:T(8,128)}, f32[56,256]{1,0:T(8,128)}) custom-call(bf16[2,768,2048]{2,1,0:T(8,128)(2,1)} %get-tuple-element.46.triple, bf16[2,256,1024]{2,1,0:T(8,128)(2,1)} %get-tuple-element.47.h_own, bf16[2,256,1024]{2,1,0:T(8,128)(2,1)} %get-tuple-element.48.h_far, ...), custom_call_target="tpu_custom_call" | custom-call | flops 55834574848 | bytes 104857600 | tf_op jit(solution)/shard_map/backward/pallas_call | solution.py:1114
  342.5 0.0 copy-start.7
  342.5 0.0 copy-start.4
  342.5 2.2 fusion.8
  344.8 1.0 copy.38
  345.8 1.6 slice.43
  347.3 0.6 copy.45
  348.0 0.0 copy-start.8
  348.0 0.6 copy.40
  348.6 0.6 copy.41
  349.2 0.6 copy.42
  349.8 0.6 copy.43
  350.3 0.6 slice.42
  351.0 0.6 copy.52
  351.6 1.3 copy.53
  352.9 0.0 copy-done.8
  352.9 1.6 copy-done.2
  354.5 2.0 copy.54
  356.5 0.0 copy-done.5
  356.5 0.7 copy.55
  (17 shorter events, 0.1 us)
Async XLA Ops:
  0.6 101.9 %copy-start = (f32[4096]{0:T(1024)S(1)}, f32[4096]{0:T(1024)}, u32[]{:S(2)}) copy-start(f32[4096]{0:T(1024)} %param.26) | copy-start | bytes 49156
  0.7 4.5 %copy-start.6 = (bf16[512,8,24]{0,2,1:T(8,128)(2,1)S(1)}, bf16[512,8,24]{0,2,1:T(8,128)(2,1)}, u32[]{:S(2)}) copy-start(bf16[512,8,24]{0,2,1:T(8,128)(2,1)} %param.21) | copy-start | bytes 589828
  99.9 2.0 copy-start.9
  100.0 2.0 copy-start.10
  103.2 106.3 %copy-start.3 = (bf16[2,1024,512]{2,1,0:T(8,128)(2,1)S(1)}, bf16[2,1024,512]{2,1,0:T(8,128)(2,1)}, u32[]{:S(2)}) copy-start(bf16[2,1024,512]{2,1,0:T(8,128)(2,1)} %g_fin.1) | copy-start | bytes 6291460
  342.5 4.8 %copy-start.7 = (f32[56,256]{1,0:T(8,128)S(1)}, f32[56,256]{1,0:T(8,128)}, u32[]{:S(2)}) copy-start(f32[56,256]{1,0:T(8,128)} %get-tuple-element.57) | copy-start | bytes 172036
  342.5 9.1 %copy-start.4 = (bf16[2,1024,512]{2,1,0:T(8,128)(2,1)S(1)}, bf16[2,1024,512]{2,1,0:T(8,128)(2,1)}, u32[]{:S(2)}) copy-start(bf16[2,1024,512]{2,1,0:T(8,128)(2,1)} %get-tuple-element.113) | copy-start | bytes 6291460
  348.0 4.9 %copy-start.8 = (f32[1,2,4,128]{3,1,2,0:T(2,128)}, f32[1,2,4,128]{3,1,2,0:T(2,128)S(1)}, u32[]{:S(2)}) copy-start(f32[1,2,4,128]{3,1,2,0:T(2,128)S(1)} %copy.44) | copy-start | bytes 12292
  351.6 2.9 copy-start.2
  354.5 2.0 copy-start.5
  354.5 2.8 copy-start.1

commit v5 on v4

--- a/solution.py
+++ b/solution.py
@@ -17,7 +17,7 @@
 NN = (((1,), (0,)), ((), ()))
 NT = (((1,), (1,)), ((), ()))
 TN = (((0,), (0,)), ((), ()))
-VMEM_LIMIT = 56 << 20
+VMEM_LIMIT = 60 << 20
 F32 = jnp.float32
 BF16 = jnp.bfloat16
 
@@ -94,6 +94,21 @@
     @staticmethod
     def sems(count):
         return pltpu.SemaphoreType.DMA((count,))
+
+    @staticmethod
+    def parts(spot, mine, theirs, all_ref, local, send, recv):
+        rows = mine.shape[0]
+        cuts = 2 if rows % 32 == 0 else 1
+        size, slots = rows // cuts, send.shape[0] // 2
+        found = []
+        for c in range(cuts):
+            part, sems = pl.ds(c * size, size), pl.ds(c * slots, slots)
+            found.append(
+                Gather(
+                    spot, mine.at[part], theirs.at[part], all_ref.at[:, part], local.at[c], send.at[sems], recv.at[sems]
+                )
+            )
+        return found
 
     def begin(self):
         self.local.start()
@@ -148,8 +163,8 @@
     here, there = spot.row, 1 - spot.row
     at = lambda k: pl.when(now == k)
 
-    head_gather = Gather(spot, head_mine, head_theirs, pieces, a_local, a_send, a_recv)
-    gather = Gather(spot, mine, theirs, all_ref, local, send, recv)
+    head_parts = Gather.parts(spot, head_mine, head_theirs, pieces, a_local, a_send, a_recv)
+    rest_parts = Gather.parts(spot, mine, theirs, all_ref, local, send, recv)
     size = own_tokens // chunks
     part = lambda k: pl.ds(k * size, size)
     x_row = [
@@ -171,32 +186,40 @@
     @at(0)
     def _():
         spot.greet("row", "col", "x", "right", "left")
-        head_gather.begin()
+        for gather in head_parts:
+            gather.begin()
         for copy in x_row[0]:
             copy.start()
         x_core[0].start()
-        gather.begin()
-        head_gather.first()
+        for gather in rest_parts:
+            gather.begin()
+        for gather in head_parts:
+            gather.first()
         x_core[1].start()
         x_core[0].wait_recv()
 
+    @at(1)
+    def _():
+        head_parts[0].forward(1)
+
     @at(blocks)
     def _():
+        for gather in head_parts[1:]:
+            gather.forward(1)
         x_core[1].wait_recv()
         keep_core.start()
 
-    @at(2)
-    def _():
-        head_gather.forward(1)
-
     @at(cast0)
     def _():
         for k in range(2, depth):
-            head_gather.forward(k)
-        gather.first()
+            for gather in head_parts:
+                gather.forward(k)
+        for gather in rest_parts:
+            gather.first()
+        for gather in head_parts:
+            gather.arrive()
         for copy in x_row[1]:
             copy.start()
-        head_gather.arrive()
         size = weight.shape[0] // (heads * count)
         for h in range(heads):
             small = [pieces[p, h * size : (h + 1) * size, :].astype(F32) for p in range(count)]
@@ -215,13 +238,14 @@
             x_col[0][k].wait_recv()
         g_core.start()
 
-    moments = {1: attend0, 2: attend0 + 3, 3: attend1} if depth == 4 else {}
+    moments = {(1, 0): cast0 + 3, (1, 1): far0, (2, 0): attend0 + 1, (2, 1): attend0 + 2, (3, 0): far1, (3, 1): attend1}
     for k in range(1, depth):
-        @at(moments.get(k, attend1))
-        def _():
-            gather.forward(k)
-
-    @at(far1 - 1)
+        for c, gather in enumerate(rest_parts):
+            @at(moments.get((k, c), attend1) if depth == 4 else attend1)
+            def _():
+                gather.forward(k)
+
+    @at(far1 - 2)
     def _():
         for k in range(chunks):
             x_row[1][k].wait_recv()
@@ -330,9 +354,10 @@
     def _():
         g_row.wait_recv()
         g_col.start()
-        gather.arrive()
-        gather.close()
-        head_gather.close()
+        for gather in rest_parts:
+            gather.arrive()
+        for gather in (*rest_parts, *head_parts):
+            gather.close()
         g_col.wait()
         g_core.wait()
         for m in range(2):
@@ -380,7 +405,7 @@
     att = pl.BlockSpec((1, HS, tokens), lambda i: (*head_of(i), 0))
     half = jax.ShapeDtypeStruct((tokens, wide), BF16)
     piece = mine.shape[0]
-    sems, one = Gather.sems, pltpu.SemaphoreType.DMA
+    sems = Gather.sems
     return pl.pallas_call(
         partial(forward_kernel, block=block, step=step, chunks=chunks, rows_at_once=min(64, block)),
         grid=(steps,),
@@ -413,7 +438,7 @@
             pltpu.VMEM((micros, tokens, wide), BF16),
             pltpu.VMEM((count, rows // count, width), BF16),
             pltpu.VMEM((rows, width), BF16),
-            one, sems(2 * depth), sems(2 * depth), one, sems(2 * depth), sems(2 * depth),
+            sems(2), sems(4 * depth), sems(4 * depth), sems(2), sems(4 * depth), sems(4 * depth),
             sems(2 * chunks + 1), sems(2 * chunks + 1), sems(2 * chunks + 4), sems(2 * chunks + 4), sems(4),
         ],
         compiler_params=params(collective_id=1, has_side_effects=True),
@@ -500,17 +525,6 @@
         for copy in copies:
             copy.wait()
 
-    @pl.when(now == 2 * steps - 2)
-    def _():
-        g_row.wait_recv()
-        g_col.start()
-
-    @pl.when(now == 2 * steps - 1)
-    def _():
-        g_col.wait_recv()
-        load_near.start()
-        load_far.start()
-
     @pl.when(now == 2 * steps)
     def _():
         load_near.wait()
@@ -596,6 +610,17 @@
             near_o[micro, at] = near.astype(BF16)
             other_o[micro, at] = other
             over_core(1, micro, at).start()
+
+    @pl.when(now == 2 * steps - 2)
+    def _():
+        g_row.wait_recv()
+        g_col.start()
+
+    @pl.when(now == 2 * steps - 1)
+    def _():
+        g_col.wait_recv()
+        load_near.start()
+        load_far.start()
 
     @pl.when(now == end)
     def _():
@@ -623,7 +648,7 @@
                 over_row(m, i).wait_send()
 
 
-def middle(second, normed, residual, cotangent, cc, cb0, cd0, att_own, att_far, pieces, wo, bias, vectors, out_bias, block=256, chunk=256):
+def middle(second, normed, residual, cotangent, cc, cb0, cd0, att_own, att_far, pieces, wo, bias, vectors, out_bias, block=512, chunk=1024):
     micros, tokens, wide = cotangent.shape
     count, rows, width = pieces.shape
     block = min(block, tokens)
@@ -873,7 +898,8 @@
             query, grad = q_s[:, lo:hi], g_s[:, lo:hi]
             base, delta = logsum[0, 0, :, lo:hi], delta_s[:, lo:hi]
             query_grad = None
-            for begin, stop in ((0, lo), (lo, hi)):
+            cuts = [*range(0, lo, 512), lo, hi]
+            for begin, stop in zip(cuts[:-1], cuts[1:]):
                 if stop == begin:
                     continue
                 raised = jnp.exp(mm(k_s[:, begin:stop], query, TN) - base)
@@ -1015,6 +1041,16 @@
         for copy in a_core:
             copy.start()
 
+    @at_step(e0 + steps)
+    def _():
+        first_sum.close()
+        for h in range(heads):
+            head_sum(h).close()
+        for i in range(steps):
+            over_core(0, 1, i).wait_send()
+            over_core(1, 1, i).wait_send()
+            over_row(0, i).wait_send()
+
     trail = now - e0
 
     @at_step(e0 + steps - 1)
@@ -1055,22 +1091,17 @@
     def _():
         for copy in (*a_core, *b_core):
             copy.wait()
-        first_sum.close()
-        for h in range(heads):
-            head_sum(h).close()
         for k in hops:
             k.wait_send()
         for i in range(steps):
-            over_core(0, 1, i).wait_send()
-            over_core(1, 1, i).wait_send()
+            over_row(1, i).wait_send()
             for m in range(2):
-                over_row(m, i).wait_send()
                 sums_over(m, i).wait_send()
 
 
 def backward(
     triple, h_own, h_far, att_own, att_far, logsum, cosine, sine, normed, part, weight, vectors, tiles, early,
-    residual, xc, cotangent, block=256, wider=512, step=256,
+    residual, xc, cotangent, block=512, wider=512, step=512,
 ):
     micros, rows, length = triple.shape
     tokens, wide = length // 2, residual.shape[2]

time: 358 us -> 342 us (0.955)
  Pallas kernels: 329 us -> 313 us
    pallas_call x1, Pallas kernels: 132 us -> 125 us  [backward(): pl.pallas_call(partial(back_kernel, block=block, wider=wider, step=step),...]
    pallas_call x1, Pallas kernels: 105 us -> 98.5 us  [middle(): pl.pallas_call(partial(middle_kernel, block=block, chunk=min(chunk, hidde...]
where the time goes in v5:
time: 342 us
  Pallas kernels  313 us (92%)
  local copies, waits for them, and re-layouts  24.9 us (7%)
    pallas_call x1, Pallas kernels, backward(): pl.pallas_call(partial(back_kernel, block=block, wider=wider, step=step),...  125 us
    pallas_call x1, Pallas kernels, middle(): pl.pallas_call(partial(middle_kernel, block=block, chunk=min(chunk, hidde...  98.5 us
    pallas_call x1, Pallas kernels, forward(): pl.pallas_call(partial(forward_kernel, block=block, step=step, chunks=chu...  89.6 us
    unnamed x34, local copies, waits for them, and re-layouts  9.36 us

profile of v5, /device:TPU:0, one launch (start us, length us, event | category | flops | bytes accessed | tf_op | source)
XLA Modules:
  0.0 341.7 jit_solution(3858529421449856478)
XLA Ops:
  0.6 0.0 copy-start
  0.7 0.0 copy-start.6
  0.7 0.9 fusion.3
  1.6 0.6 concatenate.18.vectors
  2.3 1.1 copy.39
  3.3 1.0 pad_maximum_fusion
  4.3 0.9 dynamic-slice_bitcast_fusion
  5.2 0.0 copy-done.6
  5.2 0.7 dynamic-slice_bitcast_fusion.2
  5.9 0.7 constant_dynamic-slice_fusion
  6.6 1.0 reshape.125.bias
  7.6 89.6 %forward.1 = (bf16[2,2,1024,1024]{3,2,1,0:T(8,128)(2,1)}, bf16[2,2,1024,1024]{3,2,1,0:T(8,128)(2,1)}, bf16[2,768,2048]{2,1,0:T(8,128)(2,1)}, bf16[768,1024]{1,0:...) custom-call(bf16[2,1024,512]{2,1,0:T(8,128)(2,1)} %x_fin.3, ...), custom_call_target="tpu_custom_call" | custom-call | flops 23622320128 | bytes 41943040 | tf_op jit(solution)/shard_map/forward/pallas_call | solution.py:409
  97.3 0.0 copy-start.9
  97.3 0.0 copy-start.10
  97.3 1.1 slice_bitcast_fusion
  98.4 0.8 copy.36
  99.2 0.0 copy-done.9
  99.2 0.0 copy-done.10
  99.3 0.7 dynamic_slice.39
  99.9 0.0 copy-done
  99.9 0.6 dynamic-slice_bitcast_fusion.4.bias
  100.5 98.5 %middle.1 = (bf16[2,1024,512]{2,1,0:T(8,128)(2,1)}, bf16[2,256,1024]{2,1,0:T(8,128)(2,1)}, bf16[2,256,1024]{2,1,0:T(8,128)(2,1)}, bf16[2,2,1024,1024]{3,2,1,0:T(...) custom-call(bf16[2,2,1024,1024]{3,2,1,0:T(8,128)(2,1)} %get-tuple-el, ...), custom_call_target="tpu_custom_call" | custom-call | flops 57982058496 | bytes 83886080 | tf_op jit(solution)/shard_map/middle/pallas_call | solution.py:686
  199.0 0.8 slice.37
  199.8 0.7 dynamic_update_slice.6
  200.6 0.0 copy-done.3
  200.6 0.3 convert_reduce_fusion
  200.9 0.5 dynamic_update_slice.7
  201.4 0.6 select_maximum_fusion.early
  202.0 124.8 %backward.1 = (f32[2,1024,512]{2,1,0:T(8,128)}, f32[2,288,512]{2,1,0:T(8,128)}, f32[2,96,512]{2,1,0:T(8,128)}, f32[56,256]{1,0:T(8,128)}) custom-call(bf16[2,768,2048]{2,1,0:T(8,128)(2,1)} %get-tuple-element.46.triple, bf16[2,256,1024]{2,1,0:T(8,128)(2,1)} %get-tuple-element.47.h_own, bf16[2,256,1024]{2,1,0:T(8,128)(2,1)} %get-tuple-element.48.h_far, ...), custom_call_target="tpu_custom_call" | custom-call | flops 55834574848 | bytes 104857600 | tf_op jit(solution)/shard_map/backward/pallas_call | solution.py:1145
  326.9 0.0 copy-start.7
  326.9 0.0 copy-start.4
  326.9 2.2 fusion.8
  329.1 1.0 copy.38
  330.1 1.6 slice.43
  331.7 0.6 copy.45
  332.3 0.0 copy-start.8
  332.4 0.6 copy.40
  332.9 0.6 copy.41
  333.5 0.6 copy.42
  334.1 0.6 copy.43
  334.7 0.6 slice.42
  335.3 0.6 copy.52
  335.9 1.3 copy.53
  337.3 0.0 copy-done.8
  337.3 1.6 copy-done.2
  338.9 2.0 copy.54
  340.9 0.0 copy-done.5
  340.9 0.7 copy.55
  (17 shorter events, 0.1 us)
Async XLA Ops:
  0.6 99.3 %copy-start = (f32[4096]{0:T(1024)S(1)}, f32[4096]{0:T(1024)}, u32[]{:S(2)}) copy-start(f32[4096]{0:T(1024)} %param.26) | copy-start | bytes 49156
  0.7 4.5 %copy-start.6 = (bf16[512,8,24]{0,2,1:T(8,128)(2,1)S(1)}, bf16[512,8,24]{0,2,1:T(8,128)(2,1)}, u32[]{:S(2)}) copy-start(bf16[512,8,24]{0,2,1:T(8,128)(2,1)} %param.21) | copy-start | bytes 589828
  97.3 2.0 copy-start.9
  97.3 2.0 copy-start.10
  100.5 100.1 %copy-start.3 = (bf16[2,1024,512]{2,1,0:T(8,128)(2,1)S(1)}, bf16[2,1024,512]{2,1,0:T(8,128)(2,1)}, u32[]{:S(2)}) copy-start(bf16[2,1024,512]{2,1,0:T(8,128)(2,1)} %g_fin.1) | copy-start | bytes 6291460
  326.9 4.8 %copy-start.7 = (f32[56,256]{1,0:T(8,128)S(1)}, f32[56,256]{1,0:T(8,128)}, u32[]{:S(2)}) copy-start(f32[56,256]{1,0:T(8,128)} %get-tuple-element.57) | copy-start | bytes 172036
  326.9 9.1 %copy-start.4 = (bf16[2,1024,512]{2,1,0:T(8,128)(2,1)S(1)}, bf16[2,1024,512]{2,1,0:T(8,128)(2,1)}, u32[]{:S(2)}) copy-start(bf16[2,1024,512]{2,1,0:T(8,128)(2,1)} %get-tuple-element.113) | copy-start | bytes 6291460
  332.3 4.9 %copy-start.8 = (f32[1,2,4,128]{3,1,2,0:T(2,128)}, f32[1,2,4,128]{3,1,2,0:T(2,128)S(1)}, u32[]{:S(2)}) copy-start(f32[1,2,4,128]{3,1,2,0:T(2,128)S(1)} %copy.44) | copy-start | bytes 12292
  335.9 2.9 copy-start.2
  338.9 2.0 copy-start.5
  338.9 2.8 copy-start.1

commit v6 on v5

--- a/solution.py
+++ b/solution.py
@@ -380,7 +380,7 @@
     rows = bias.shape[0]
     heads = rows // (3 * HS)
     depth = count // 2
-    chunks = 4
+    chunks = 2
     cast0 = 2 * blocks
     far0 = 2 * cast0
     a0 = far0 + blocks
@@ -942,7 +942,7 @@
                 b_tiles[p, head] = every[p * size : (p + 1) * size].astype(BF16)
             head_sum(head).begin()
 
-    moments = {1: 2, 2: l0, 3: b1, 0: b1 + 2} if depth == 4 else {}
+    moments = {1: 3, 2: l0 + 3, 3: b1 + 2, 0: l1} if depth == 4 else {}
     for s in first_sum.order:
         @at_step(moments.get(s, b1 + 2))
         def _():

time: 342 us -> 342 us (level)
  no operation moved by 1% of the time
where the time goes in v6:
time: 342 us; the launch traced here: 341 us
  Pallas kernels  312 us (91%)
  local copies, waits for them, and re-layouts  24.9 us (7%)
    pallas_call x1, Pallas kernels, backward(): pl.pallas_call(partial(back_kernel, block=block, wider=wider, step=step),...  125 us
    pallas_call x1, Pallas kernels, middle(): pl.pallas_call(partial(middle_kernel, block=block, chunk=min(chunk, hidde...  98.5 us
    pallas_call x1, Pallas kernels, forward(): pl.pallas_call(partial(forward_kernel, block=block, step=step, chunks=chu...  89.1 us
    unnamed x34, local copies, waits for them, and re-layouts  9.36 us

profile of v6, /device:TPU:0, one launch (start us, length us, event | category | flops | bytes accessed | tf_op | source)
XLA Modules:
  0.0 341.1 jit_solution(6098158617746749780)
XLA Ops:
  0.6 0.0 copy-start
  0.7 0.0 copy-start.6
  0.7 0.9 fusion.3
  1.6 0.6 concatenate.18.vectors
  2.3 1.1 copy.39
  3.3 1.0 pad_maximum_fusion
  4.3 0.9 dynamic-slice_bitcast_fusion
  5.2 0.0 copy-done.6
  5.2 0.7 dynamic-slice_bitcast_fusion.2
  5.9 0.7 constant_dynamic-slice_fusion
  6.6 1.0 reshape.125.bias
  7.6 89.1 %forward.1 = (bf16[2,2,1024,1024]{3,2,1,0:T(8,128)(2,1)}, bf16[2,2,1024,1024]{3,2,1,0:T(8,128)(2,1)}, bf16[2,768,2048]{2,1,0:T(8,128)(2,1)}, bf16[768,1024]{1,0:...) custom-call(bf16[2,1024,512]{2,1,0:T(8,128)(2,1)} %x_fin.3, ...), custom_call_target="tpu_custom_call" | custom-call | flops 23622320128 | bytes 41943040 | tf_op jit(solution)/shard_map/forward/pallas_call | solution.py:409
  96.8 0.0 copy-start.9
  96.8 0.0 copy-start.10
  96.8 1.1 slice_bitcast_fusion
  97.9 0.8 copy.36
  98.7 0.0 copy-done.9
  98.7 0.0 copy-done.10
  98.7 0.7 dynamic_slice.39
  99.4 0.0 copy-done
  99.4 0.6 dynamic-slice_bitcast_fusion.4.bias
  100.0 98.5 %middle.1 = (bf16[2,1024,512]{2,1,0:T(8,128)(2,1)}, bf16[2,256,1024]{2,1,0:T(8,128)(2,1)}, bf16[2,256,1024]{2,1,0:T(8,128)(2,1)}, bf16[2,2,1024,1024]{3,2,1,0:T(...) custom-call(bf16[2,2,1024,1024]{3,2,1,0:T(8,128)(2,1)} %get-tuple-el, ...), custom_call_target="tpu_custom_call" | custom-call | flops 57982058496 | bytes 83886080 | tf_op jit(solution)/shard_map/middle/pallas_call | solution.py:686
  198.5 0.8 slice.37
  199.3 0.7 dynamic_update_slice.6
  200.1 0.0 copy-done.3
  200.1 0.3 convert_reduce_fusion
  200.4 0.5 dynamic_update_slice.7
  200.9 0.6 select_maximum_fusion.early
  201.5 124.8 %backward.1 = (f32[2,1024,512]{2,1,0:T(8,128)}, f32[2,288,512]{2,1,0:T(8,128)}, f32[2,96,512]{2,1,0:T(8,128)}, f32[56,256]{1,0:T(8,128)}) custom-call(bf16[2,768,2048]{2,1,0:T(8,128)(2,1)} %get-tuple-element.46.triple, bf16[2,256,1024]{2,1,0:T(8,128)(2,1)} %get-tuple-element.47.h_own, bf16[2,256,1024]{2,1,0:T(8,128)(2,1)} %get-tuple-element.48.h_far, ...), custom_call_target="tpu_custom_call" | custom-call | flops 55834574848 | bytes 104857600 | tf_op jit(solution)/shard_map/backward/pallas_call | solution.py:1145
  326.3 0.0 copy-start.7
  326.3 0.0 copy-start.4
  326.4 2.2 fusion.8
  328.6 1.0 copy.38
  329.6 1.6 slice.43
  331.2 0.6 copy.45
  331.8 0.0 copy-start.8
  331.8 0.6 copy.40
  332.4 0.6 copy.41
  333.0 0.6 copy.42
  333.6 0.6 copy.43
  334.2 0.6 slice.42
  334.8 0.6 copy.52
  335.4 0.0 copy-done.4
  335.4 1.3 copy.53
  336.7 1.6 copy-done.2
  338.3 2.0 copy.54
  340.4 0.7 copy.55
  341.1 0.0 copy-done.1
  (17 shorter events, 0.1 us)
Async XLA Ops:
  0.6 98.7 %copy-start = (f32[4096]{0:T(1024)S(1)}, f32[4096]{0:T(1024)}, u32[]{:S(2)}) copy-start(f32[4096]{0:T(1024)} %param.26) | copy-start | bytes 49156
  0.7 4.5 %copy-start.6 = (bf16[512,8,24]{0,2,1:T(8,128)(2,1)S(1)}, bf16[512,8,24]{0,2,1:T(8,128)(2,1)}, u32[]{:S(2)}) copy-start(bf16[512,8,24]{0,2,1:T(8,128)(2,1)} %param.21) | copy-start | bytes 589828
  96.8 2.0 copy-start.9
  96.8 2.0 copy-start.10
  100.0 100.1 %copy-start.3 = (bf16[2,1024,512]{2,1,0:T(8,128)(2,1)S(1)}, bf16[2,1024,512]{2,1,0:T(8,128)(2,1)}, u32[]{:S(2)}) copy-start(bf16[2,1024,512]{2,1,0:T(8,128)(2,1)} %g_fin.1) | copy-start | bytes 6291460
  326.3 4.8 %copy-start.7 = (f32[56,256]{1,0:T(8,128)S(1)}, f32[56,256]{1,0:T(8,128)}, u32[]{:S(2)}) copy-start(f32[56,256]{1,0:T(8,128)} %get-tuple-element.57) | copy-start | bytes 172036
  326.3 9.1 %copy-start.4 = (bf16[2,1024,512]{2,1,0:T(8,128)(2,1)S(1)}, bf16[2,1024,512]{2,1,0:T(8,128)(2,1)}, u32[]{:S(2)}) copy-start(bf16[2,1024,512]{2,1,0:T(8,128)(2,1)} %get-tuple-element.113) | copy-start | bytes 6291460
  331.8 4.9 %copy-start.8 = (f32[1,2,4,128]{3,1,2,0:T(2,128)}, f32[1,2,4,128]{3,1,2,0:T(2,128)S(1)}, u32[]{:S(2)}) copy-start(f32[1,2,4,128]{3,1,2,0:T(2,128)S(1)} %copy.44) | copy-start | bytes 12292
  335.4 2.9 copy-start.2
  338.3 2.0 copy-start.5
  338.3 2.8 copy-start.1
